TPU v7x, 32 devices: a whole 2x2x4 slice. The times are simulated.
32 devices in a mesh: dp: 4 (over y, x), seq: 8 (over z, core).
Axes of the slice: x: 2, y: 2, z: 4, core: 2. Of those that a mesh axis runs over, the one named last changes fastest.
Arguments:
- tokens: bfloat16 [12, 1024, 512], P('dp', 'seq'), may hold values from -6 to 6
- grad_out: bfloat16 [12, 1024, 512], P('dp', 'seq'), may hold values from -6 to 6
- crop: int32 [12], P('dp'), may hold values from 512 to 1024
- offsets: int32 [12, 4], P('dp'), may hold values from 0 to 1023, as said below
- w_query: bfloat16 [512, 512], replicated, may hold values from -0.25 to 0.25
- w_key: bfloat16 [512, 512], replicated, may hold values from -0.25 to 0.25
- w_value: bfloat16 [512, 512], replicated, may hold values from -0.25 to 0.25
- w_out: bfloat16 [512, 512], replicated, may hold values from -6 to 6
- w_up: bfloat16 [512, 2048], replicated, may hold values from -0.25 to 0.25
- w_down: bfloat16 [2048, 512], replicated, may hold values from -0.125 to 0.125
- b_query: float32 [512], replicated, may hold values from -3 to 3
- b_value: float32 [512], replicated, may hold values from -3 to 3
- b_out: float32 [512], replicated, may hold values from -3 to 3
- b_up: float32 [2048], replicated, may hold values from -3 to 3
- b_down: float32 [512], replicated, may hold values from -3 to 3
- gain_one: float32 [512], replicated, may hold values from 0.5 to 1.5
- shift_one: float32 [512], replicated, may hold values from -3 to 3
- gain_two: float32 [512], replicated, may hold values from 0.5 to 1.5
- shift_two: float32 [512], replicated, may hold values from -3 to 3
Outputs:
- activations: bfloat16 [12, 1024, 512], P('dp', 'seq')
- input_grad: bfloat16 [12, 1024, 512], P('dp', 'seq')
- grad_w_query: float32 [512, 512], replicated
- grad_w_key: float32 [512, 512], replicated
- grad_w_value: float32 [512, 512], replicated
- grad_w_out: float32 [512, 512], replicated
- grad_w_up: float32 [512, 2048], replicated
- grad_w_down: float32 [2048, 512], replicated
- grad_b_query: float32 [512], replicated
- grad_b_value: float32 [512], replicated
- grad_b_out: float32 [512], replicated
- grad_b_up: float32 [2048], replicated
- grad_b_down: float32 [512], replicated
- grad_gain_one: float32 [512], replicated
- grad_shift_one: float32 [512], replicated
- grad_gain_two: float32 [512], replicated
- grad_shift_two: float32 [512], replicated
Inputs may be any that keep to these rules, and one draw needn't show every extreme that they name: offsets[r, 0] is 0, a row's offsets do not fall, and each stays below crop[r].
All inputs are finite; a program needn't handle non-finite values.
Results may differ from a plain program's by a relative error of at most 0.013.
Values may be sent and summed in bfloat16 or wider, within the bound.
No kernel may reach another device: no remote copies, remote signals or barrier semaphores. Data moves between devices by JAX's collectives and lax.ppermute only.
A program may use at most 192 MiB of HBM per device.

v0:
```python
import functools

import jax
import jax.numpy as jnp
from jax import lax
from jax.experimental import pallas as pl
from jax.experimental.pallas import tpu as pltpu
from jax.sharding import PartitionSpec as P

HEADS = 8
EPSILON = 1e-06
MASKED = -1e30
MIB = 1024 * 1024
LIMITS = (16, 20, 20, 26, 20)
PIECES = 16
GROUP = 4
BACK_US = 0.05
BF16 = jnp.bfloat16
F32 = jnp.float32
GELU_C = 0.7978845608028654
GELU_A = 0.044715


def nn(a, b):
    return jnp.dot(a, b, preferred_element_type=F32)


def nt(a, b):
    return lax.dot_general(a, b, (((1,), (1,)), ((), ())), preferred_element_type=F32)


def tn(a, b):
    return lax.dot_general(a, b, (((0,), (0,)), ((), ())), preferred_element_type=F32)


def normalize(values):
    center = values - jnp.mean(values, axis=-1, keepdims=True)
    scale = lax.rsqrt(jnp.mean(center * center, axis=-1, keepdims=True) + EPSILON)
    return center * scale, scale


def norm_back(cotangent, unit, scale, gain):
    g = cotangent * gain
    return scale * (
        g
        - jnp.mean(g, axis=-1, keepdims=True)
        - unit * jnp.mean(g * unit, axis=-1, keepdims=True)
    )


def segments(pos, offsets, crop, row):
    count = offsets.shape[1]
    seg = jnp.zeros(pos.shape, jnp.int32)
    for j in range(count):
        seg += (pos >= offsets[row, j]).astype(jnp.int32)
    return seg + count * (pos >= crop[row]).astype(jnp.int32)


def ring_station(place, count):
    return jnp.where(place < count // 2, 2 * place, 2 * (count - 1 - place) + 1)


def ring_place(station, count):
    return jnp.where(station % 2 == 0, station // 2, count - 1 - station // 2)


def positions(sp, chunk, tok, shape, dim):
    start = (sp[4] ^ chunk) * (2 * tok)
    i = lax.broadcasted_iota(jnp.int32, shape, dim)
    return i + jnp.where(i < tok, start + sp[0] * tok, start + sp[1] * tok - tok)


def half_of(which, width):
    return pl.ds(pl.multiple_of(which * width, 128), width)


def padded(lines):
    return jnp.concatenate(lines + [jnp.zeros((16 - len(lines), lines[0].shape[1]), F32)], axis=0)


def load_kernel(halved, sp, *refs):
    count = len(halved)
    sources, targets, sems = refs[:count], refs[count : 2 * count], refs[2 * count :]
    copies = []
    for half, source, target, sem in zip(halved, sources, targets, sems):
        if half:
            source = source.at[:, half_of(sp[0], source.shape[1] // 2)]
        copies.append(pltpu.make_async_copy(source, target, sem))
    for copy in copies:
        copy.start()
    for copy in copies:
        copy.wait()


def chunk_kernel(chunk, last, tok, rows, *refs):
    refs = list(refs)
    first = chunk == 0
    sp, offsets, crop, xm, xo, vectors, weights = refs[:7]
    refs = refs[7:]
    if not first:
        qm_in, m_in, l_in, acc_in = refs[:4]
        refs = refs[4:]
    k_out, v_out, kt_out, nt_out = refs[:4]
    refs = refs[4:]
    if first:
        qm_out = refs.pop(0)
    if last:
        lse_out, ot_out, att_m, att_o = refs[:4]
    else:
        m_out, l_out, acc_out = refs
    half = weights.shape[2]
    heads = HEADS // 2
    size = half // heads
    chip = 2 * tok
    for at, x in ((0, xm), (tok, xo)):
        values = x[...].reshape(rows * tok, -1).astype(F32)
        unit, _ = normalize(values)
        normed = unit * vectors[0:1, :] + vectors[1:2, :]
        low = normed.astype(BF16)
        k = nn(low, weights[1])
        v = (nn(low, weights[2]) + vectors[3:4, half_of(sp[0], half)]).astype(BF16)
        if first:
            q = ((nn(low, weights[0]) + vectors[2:3, half_of(sp[0], half)]).astype(BF16).astype(F32) * size**-0.5).astype(BF16)
            lane = lax.broadcasted_iota(jnp.int32, (tok, 2 * size), 1)
        for r in range(rows):
            part = slice(r * tok, (r + 1) * tok)
            k_out[r, at : at + tok, :] = k[part].astype(BF16)
            v_out[r, at : at + tok, :] = v[part]
            kt_out[r, :, at : at + tok] = k[part].T.astype(BF16)
            nt_out[r, :, at : at + tok] = normed[part].T.astype(BF16)
            if first:
                for h in range(heads):
                    pair = q[part, (h // 2) * 2 * size : (h // 2 + 1) * 2 * size]
                    keep = (lane >= size) if h % 2 else (lane < size)
                    qm_out[r * heads + h, at : at + tok, :] = jnp.where(keep, pair, jnp.zeros_like(pair))
    qm = qm_out if first else qm_in
    for r in range(rows):
        key_seg = segments(positions(sp, chunk, tok, (chip, chip), 0), offsets, crop, r)
        query_seg = segments(positions(sp, 0, tok, (1, chip), 1), offsets, crop, r)
        bias = jnp.where(key_seg == query_seg, 0.0, MASKED)
        outs = []
        spot = [r * heads + h for h in range(heads)]
        pairs = [slice((h // 2) * 2 * size, (h // 2 + 1) * 2 * size) for h in range(heads)]
        s = [nt(k_out[r, :, pairs[h]], qm[spot[h]]) + bias for h in range(heads)]
        tops = [jnp.max(a, axis=0, keepdims=True) for a in s]
        if not first:
            olds = [m_in[at] for at in spot]
            tops = [jnp.maximum(a, b) for a, b in zip(olds, tops)]
        p = [jnp.exp(a - b) for a, b in zip(s, tops)]
        totals = [jnp.sum(a, axis=0, keepdims=True) for a in p]
        addeds = [tn(v_out[r, :, pairs[h]], p[h].astype(BF16)) for h in range(heads)]
        for h, at in enumerate(spot):
            added = addeds[h][(h % 2) * size : (h % 2 + 1) * size]
            total = totals[h]
            if not first:
                keep = jnp.exp(olds[h] - tops[h])
                total += l_in[at] * keep
                added += acc_in[at] * keep
            if last:
                lse_out[at] = tops[h] + jnp.log(total)
                out = added / total
                ot_out[at] = out
                outs.append(out)
            else:
                m_out[at] = tops[h]
                l_out[at] = total
                acc_out[at] = added
        if last:
            att = jnp.concatenate(outs, axis=0).T.astype(BF16)
            att_m[r] = att[:tok]
            att_o[r] = att[tok:]


def feed_forward_half(sp, which, normed, g, up, down, bup, hid, pre, at, vec, total, back):
    half = up.shape[1] // 2
    row = min(512, half)
    block = min(512, row)
    count = half // block
    cols = [pl.ds(pl.multiple_of(sp[which] * half + j * block, 128), block) for j in range(count)]
    for first in range(0, count, 2):
        js = range(first, min(first + 2, count))
        us = [nn(normed, up[:, cols[j]]) + bup[:, cols[j]] for j in js]
        gs = [nt(g, down[cols[j], :]) for j in js]
        outs, pres = [], []
        for j, u, back_in in zip(js, us, gs):
            square = u * u
            plus = 1.0 + jnp.tanh(u * (GELU_C + GELU_C * GELU_A * square))
            low = 0.5 * u
            hidden = (low * plus).astype(BF16)
            slope = plus * (0.5 + low * (2.0 - plus) * (GELU_C + 3 * GELU_C * GELU_A * square))
            grad = (back_in * slope).astype(BF16)
            hid[:, j * block : (j + 1) * block] = hidden
            pre[:, at + j * block : at + (j + 1) * block] = grad
            outs.append(hidden)
            pres.append(grad)
            line = jnp.sum(grad.astype(F32), axis=0, keepdims=True)
            lane = j * block % row
            vec[pl.ds(sp[which] * (half // row) + j * block // row, 1), lane : lane + block] = line
        for j, hidden, grad in zip(js, outs, pres):
            more, less = nn(hidden, down[cols[j], :]), nt(grad, up[:, cols[j]])
            total = more if total is None else total + more
            back = less if back is None else back + less
    return total, back


def ffn_first_kernel(
    sp, att_m, att_o, wo, tokens, cot, up, down, b_out, bup, gain, shift, mid_out, normed_out, send, total_out, back_out, vec
):
    rows, tok, width = tokens.shape
    flat = rows * tok
    quarter = width // 2
    mine = pl.ds(pl.multiple_of(sp[0] * quarter, 128), quarter)
    other = pl.ds(pl.multiple_of(sp[1] * quarter, 128), quarter)
    mid = (
        tokens[...].reshape(flat, width).astype(F32)
        + nn(att_m[...].reshape(flat, -1), wo[mine, :])
        + nn(att_o[...].reshape(flat, -1), wo[other, :])
        + b_out[...]
    )
    mid_out[...] = mid
    unit, _ = normalize(mid)
    normed = (unit * gain[...] + shift[...]).astype(BF16)
    normed_out[...] = normed
    half = up.shape[1] // 2
    send[:, 2 * half :] = normed
    vec[...] = jnp.zeros_like(vec)
    g = cot[...].reshape(flat, width)
    total_out[...], back_out[...] = feed_forward_half(
        sp, 1, normed, g, up, down, bup, send, send, half, vec, None, None
    )


def ffn_second_kernel(
    sp, mid_in, normed_in, cot, up, down, bup, b_down, gain, total_in, back_in, vec_in, out, hid, pre, mid_grad, branch, vec
):
    rows, tok, width = cot.shape
    flat = rows * tok
    g = cot[...].reshape(flat, width)
    vec[...] = vec_in[...]
    total, back = feed_forward_half(
        sp, 0, normed_in[...], g, up, down, bup, hid, pre, 0, vec, total_in[...], back_in[...]
    )
    mid = mid_in[...]
    out[...] = (mid + total + b_down[...]).astype(BF16).reshape(rows, tok, width)
    unit, scale = normalize(mid)
    gf = g.astype(F32)
    grad = gf + norm_back(back, unit, scale, gain[...])
    mid_grad[...] = grad
    low = grad.astype(BF16)
    branch[...] = low.reshape(rows, tok, width)
    vec[4:5, :] = jnp.sum(gf, axis=0, keepdims=True)
    vec[5:6, :] = jnp.sum(back * unit, axis=0, keepdims=True)
    vec[6:7, :] = jnp.sum(back, axis=0, keepdims=True)
    vec[7:8, :] = jnp.sum(low.astype(F32), axis=0, keepdims=True)


def ffn_grad_kernel(sp, hid_m, pre_m, n_m, got, g_m, g_o, d_keep, d_send, u_keep, u_send, gd, gu):
    half = hid_m.shape[1]
    gd[...] = tn(hid_m[...], g_m[...]) + tn(got[:, :half], g_o[...])
    gu[...] = tn(n_m[...], pre_m[...]) + tn(got[:, 2 * half :], got[:, half : 2 * half])
    rd = gd.shape[0] // PIECES
    ru = gu.shape[0] // PIECES
    width = gd.shape[1]
    for slot in range(PIECES):
        d, u = (d_keep, u_keep) if slot < PIECES // 2 else (d_send, u_send)
        at = slot % (PIECES // 2)
        d[at] = gd[pl.ds(pl.multiple_of((sp[2] ^ slot) * rd, rd), rd), :].astype(BF16)
        rows = pl.ds(pl.multiple_of((sp[3] ^ slot) * ru, ru), ru)
        for i in range(half // width):
            u[at, i * ru : (i + 1) * ru, :] = gu[rows, i * width : (i + 1) * width].astype(BF16)


def attend_back_kernel(stations, tok, row, whole, last, *refs):
    refs = list(refs)

    def take(count):
        got = refs[:count]
        del refs[:count]
        return got

    sp, offsets, crop, br_m, br_o, wo, qm, lse, ot, weights = take(10)
    k, v, kt, norm_t = (take(stations) for _ in range(4))
    sums_in = take(5) if row else None
    if last:
        vectors, vec_in = take(2)
    dn_m, dn_o = take(2)
    if last:
        ones, twos = take(2), take(2)
    gq, gk, gv, go, sums = take(5)
    at = row if whole else 0
    heads = HEADS // 2
    _, width, half = weights.shape
    size = half // heads
    chip = 2 * tok
    block = min(4, stations)
    blocks = stations // block

    branch = jnp.concatenate([br_m[at], br_o[at]], axis=0)
    do = nt(branch, wo[half_of(sp[0], half), :])
    dot = do.T
    do = do.astype(BF16)
    lane = lax.broadcasted_iota(jnp.int32, (chip, 2 * size), 1)
    head_at = at * heads
    out_t = jnp.concatenate([ot[head_at + h] for h in range(heads)], axis=0).astype(BF16)
    go_row = nn(out_t, branch)
    query_seg = segments(positions(sp, 0, tok, (1, chip), 1), offsets, crop, row)
    biases = []
    for chunk in range(stations):
        key_seg = segments(positions(sp, chunk, tok, (chip, chip), 0), offsets, crop, row)
        biases.append(jnp.where(key_seg == query_seg, 0.0, MASKED))
    dqt = []
    dks = [[] for _ in range(blocks)]
    dvs = [[] for _ in range(blocks)]
    for pair in range(heads // 2):
        lanes = slice(pair * 2 * size, (pair + 1) * 2 * size)
        dk = [None] * blocks
        dv = [None] * blocks
        for h in (2 * pair, 2 * pair + 1):
            wide = do[:, lanes]
            dm = jnp.where((lane >= size) if h % 2 else (lane < size), wide, jnp.zeros_like(wide))
            delta = jnp.sum(ot[head_at + h] * dot[h * size : (h + 1) * size], axis=0, keepdims=True)
            dq = None
            for b in range(blocks):
                chunks = range(b * block, (b + 1) * block)
                keys = jnp.concatenate([k[c][at, :, lanes] for c in chunks], axis=0)
                values = jnp.concatenate([v[c][at, :, lanes] for c in chunks], axis=0)
                keys_t = jnp.concatenate([kt[c][at, h * size : (h + 1) * size, :] for c in chunks], axis=1)
                bias = jnp.concatenate([biases[c] for c in chunks], axis=0)
                p = jnp.exp(nt(keys, qm[head_at + h]) + bias - lse[head_at + h])
                ds = (p * (nt(values, dm) - delta)).astype(BF16)
                dv_h, dk_h = nn(p.astype(BF16), dm), nn(ds, qm[head_at + h])
                dv[b] = dv_h if dv[b] is None else dv[b] + dv_h
                dk[b] = dk_h if dk[b] is None else dk[b] + dk_h
                more = nn(keys_t, ds)
                dq = more if dq is None else dq + more
            dqt.append(dq)
        for b in range(blocks):
            dks[b].append(dk[b].astype(BF16))
            dvs[b].append(dv[b].astype(BF16))
    dq = (jnp.concatenate(dqt, axis=0) * size**-0.5).T.astype(BF16)
    gq_row = nn(norm_t[0][at], dq)
    gk_row = gv_row = sum_k = sum_v = 0.0
    for b in range(blocks):
        dk = jnp.concatenate(dks[b], axis=1)
        dv = jnp.concatenate(dvs[b], axis=1)
        normed = jnp.concatenate([norm_t[c][at] for c in range(b * block, (b + 1) * block)], axis=1)
        gk_row += nn(normed, dk)
        gv_row += nn(normed, dv)
        sum_k += jnp.sum(dk.astype(F32), axis=0, keepdims=True)
        sum_v += jnp.sum(dv.astype(F32), axis=0, keepdims=True)
        dn = nt(dk, weights[1]) + nt(dv, weights[2])
        for i in range(block):
            part = dn[i * chip : (i + 1) * chip]
            if b + i == 0:
                part += nt(dq, weights[0])
            dn_m[b * block + i] = part[:tok].astype(BF16)
            dn_o[b * block + i] = part[tok:].astype(BF16)
    sum_q = jnp.sum(dq.astype(F32), axis=0, keepdims=True)
    made_here = (gq_row, gk_row, gv_row, go_row, jnp.concatenate([sum_q, sum_v, sum_k, jnp.zeros((5, half), F32)]))
    for i, (ref, value) in enumerate(zip((gq, gk, gv, go, sums), made_here)):
        ref[...] = value if sums_in is None else value + sums_in[i][...]
    if not last:
        return

    vec = refs[0]
    lane = lax.broadcasted_iota(jnp.int32, (2, width), 1)
    both = sums[0:2, :]
    both = jnp.concatenate([both, both], axis=1)
    vec[0:2, :] = jnp.where((lane >= half) == (sp[0] == 1), both, 0.0)
    vec[2:3, :] = vec_in[7:8, :]
    vec[3:4, :] = vec_in[4:5, :]
    vec[4:8, :] = vec_in[0:4, :]
    vec[10:12, :] = vec_in[5:7, :]
    vec[12:16, :] = jnp.zeros((4, width), F32)
    wide = [weights[i].astype(F32) for i in range(3)]
    shifts = sum(w * sums[i : i + 1, :] for w, i in zip(wide, (0, 2, 1)))
    gains = sum(w * g[...] for w, g in zip(wide, (gq, gk, gv)))

    def across(values):
        folded = sum(values[:, i * 128 : (i + 1) * 128] for i in range(half // 128))
        return jnp.sum(folded.T, axis=0, keepdims=True)

    shift_grad = across(shifts)
    vec[9:10, :] = shift_grad
    vec[8:9, :] = (across(gains) - vectors[1:2, :] * shift_grad) / vectors[0:1, :]
    n = width // PIECES
    low = n // 2
    per = PIECES // 2
    for slot in range(PIECES):
        one, two = ones[slot // per], twos[slot // per]
        base = slot % per * n
        piece = sp[2] ^ slot
        part = pl.ds(pl.multiple_of(piece * n, n), n)
        one[base : base + n, :half] = gq[part, :].astype(BF16)
        one[base : base + n, half:] = gk[part, :].astype(BF16)
        piece = sp[3] ^ slot
        first = pl.ds(pl.multiple_of(piece * n, n), low)
        second = pl.ds(pl.multiple_of(piece * n + low, low), low)
        two[base : base + low, :half] = gv[first, :].astype(BF16)
        two[base : base + low, half:] = gv[second, :].astype(BF16)
        two[base + low : base + n, :] = go[pl.ds(pl.multiple_of(piece * low, low), low), :].astype(BF16)
    for i, two in enumerate(twos):
        lines = [vec[pl.ds(sp[3] ^ (i * per + s), 1), :] for s in range(per)]
        two[per * n :, :] = padded(lines).astype(BF16)


def last_kernel(tokens, gain, mid_grad, *refs):
    out = refs[-1]
    rows, tok, width = tokens.shape
    flat = rows * tok
    unit, scale = normalize(tokens[...].reshape(flat, width).astype(F32))
    parts = [refs[2 * r][0].astype(F32) + refs[2 * r + 1][0].astype(F32) + refs[-2][r].astype(F32) for r in range(rows)]
    grad = mid_grad[...] + norm_back(jnp.concatenate(parts, axis=0), unit, scale, gain[0:1, :])
    out[...] = grad.astype(BF16).reshape(rows, tok, width)


def unpack_ffn_kernel(far, sp, *refs):
    refs = list(refs)
    d_both, u_both = refs[0:2], refs[2:4]
    down, up, done, d_wide, u_wide, sems = refs[-6:]
    done[...] = jnp.zeros_like(done)
    _, rd, width = d_both[0].shape
    ru = up.shape[0] // PIECES
    half = down.shape[0] // 2
    count = PIECES // GROUP
    copies = []
    for which in range(2):
        for i in range(GROUP // 2):
            at = which * (GROUP // 2) + i
            group = (GROUP // 2 if far else 0) + i
            for k in range(count):
                slot = i * count + k
                place = (sp[2] ^ k) & (count - 1)
                rows = pl.ds(pl.multiple_of(place * rd, rd), rd)
                d_wide[at, rows, :] = d_both[which][slot].astype(F32)
                place = (sp[3] ^ k) & (count - 1)
                rows = pl.ds(pl.multiple_of(place * ru, ru), ru)
                for n in range(rd // ru):
                    part = u_both[which][slot, n * ru : (n + 1) * ru, :]
                    u_wide[at, rows, n * width : (n + 1) * width] = part.astype(F32)
            size = count * rd
            rows = pl.ds(pl.multiple_of(sp[which] * half + ((sp[2] // count) ^ group) * size, size), size)
            copies.append(pltpu.make_async_copy(d_wide.at[at], down.at[rows, :], sems.at[2 * at]))
            copies[-1].start()
            size = count * ru
            rows = pl.ds(pl.multiple_of(((sp[3] // count) ^ group) * size, size), size)
            copies.append(pltpu.make_async_copy(u_wide.at[at], up.at[rows, half_of(sp[which], half)], sems.at[2 * at + 1]))
            copies[-1].start()
    for copy in copies:
        copy.wait()


def unpack_attend_kernel(sp, *refs):
    gq, gk, gv, go, *lines = refs[8:]
    vec = lines.pop()
    ones, twos = (refs[0:2], refs[2:4]), (refs[4:6], refs[6:8])
    width = gq.shape[0]
    half = width // 2
    n = width // PIECES
    low = n // 2
    per = PIECES // 2
    for slot in range(PIECES):
        base = slot % per * n
        for which in range(2):
            one, two = ones[which][slot // per], twos[which][slot // per]
            cols = half_of(sp[which], half)
            piece = sp[2] ^ slot
            rows = pl.ds(pl.multiple_of(piece * n, n), n)
            gq[rows, cols] = one[base : base + n, :half].astype(F32)
            gk[rows, cols] = one[base : base + n, half:].astype(F32)
            piece = sp[3] ^ slot
            first = pl.ds(pl.multiple_of(piece * n, n), low)
            second = pl.ds(pl.multiple_of(piece * n + low, low), low)
            gv[first, cols] = two[base : base + low, :half].astype(F32)
            gv[second, cols] = two[base : base + low, half:].astype(F32)
            out_rows = pl.ds(pl.multiple_of(sp[which] * half + piece * low, low), low)
            go[out_rows, :] = two[base + low : base + n, :].astype(F32)
    for side in range(2):
        both = twos[0][side][per * n :, :].astype(F32) + twos[1][side][per * n :, :].astype(F32)
        for s in range(per):
            vec[pl.ds(sp[3] ^ (side * per + s), 1), :] = both[s : s + 1]
    for line, row in zip(lines, (0, 1, 2, 4, 3, 8, 9, 10, 11)):
        count = line.shape[1] // width
        for i in range(count):
            line[:, i * width : (i + 1) * width] = vec[row + i : row + i + 1, :]


def total(*values):
    return sum(v.astype(F32) for v in values).astype(BF16)


def sum_kernel(*refs):
    refs[-1][...] = total(*[r[...] for r in refs[:-1]])


def upper_kernel(*refs):
    count = len(refs) // 3
    for i, out in enumerate(refs[2 * count :]):
        keep, got = refs[2 * i : 2 * i + 2]
        half = keep.shape[0] // 2
        out[...] = total(keep[half:], got[half:])


def quarter_kernel(d_keep, d_got, d_last, u_keep, u_got, u_last, keep, send):
    rd = d_keep.shape[1]
    half = keep.shape[0]
    for i in range(2 * half):
        out = send if i >= half else keep
        out[i % half, :rd] = total(d_keep[i], d_got[i], d_last[i])
        out[i % half, rd:] = total(u_keep[i], u_got[i], u_last[i])


def halve_kernel(keep, got, out_keep, out_send):
    out_keep[...] = total(keep[0], got[0])
    out_send[...] = total(keep[1], got[1])


def pair_kernel(one, two, out):
    out[0] = one[...]
    out[1] = two[...]


def divide_kernel(one, two, d, u):
    rd = d.shape[1]
    for i in range(d.shape[0]):
        part = (one if i < 2 else two)[i % 2]
        d[i] = part[:rd]
        u[i] = part[rd:]


def join_kernel(*refs):
    count = len(refs) // 3
    for i, out in enumerate(refs[2 * count :]):
        one, two = refs[2 * i : 2 * i + 2]
        out[: one.shape[0]] = one[...]
        out[one.shape[0] :] = two[...]


def attend_upper_kernel(one_keep, one_got, two_keep, two_got, one, two):
    n = one.shape[0]
    one[...] = total(one_keep[n:], one_got[n:])
    two[:n] = total(two_keep[n : 2 * n], two_got[n : 2 * n])
    lines = total(two_keep[2 * n :], two_got[2 * n :]).astype(F32)
    two[n:] = fill(lines[4:8])


def fill(lines):
    return jnp.concatenate([lines, jnp.zeros((16 - lines.shape[0], lines.shape[1]), F32)], axis=0).astype(BF16)


def attend_quarter_kernel(one_keep, one_got, one_last, two_keep, two_got, two_last, keep, send):
    count = 2 * keep.shape[0]
    n = one_last.shape[0] // count
    lines = total(two_keep[2 * count * n :], two_got[2 * count * n :], two_last[count * n :]).astype(F32)
    for i in range(count):
        out = (keep, send)[i // 2]
        part = slice(i * n, (i + 1) * n)
        out[i % 2, :n] = total(one_keep[part], one_got[part], one_last[part])
        out[i % 2, n : 2 * n] = total(two_keep[part], two_got[part], two_last[part])
        out[i % 2, 2 * n :] = jnp.broadcast_to(lines[i : i + 1], (16, lines.shape[1])).astype(BF16)


def attend_divide_kernel(first, second, one, two):
    n = one.shape[0] // 4
    lines = []
    for i in range(4):
        part = (first if i < 2 else second)[i % 2]
        one[i * n : (i + 1) * n] = part[:n]
        two[i * n : (i + 1) * n] = part[n : 2 * n]
        lines.append(part[2 * n :].astype(F32)[:1])
    two[4 * n :] = padded(lines).astype(BF16)


def attend_join_kernel(one_a, one_b, two_a, two_b, one, two):
    n = one_a.shape[0]
    one[:n] = one_a[...]
    one[n:] = one_b[...]
    two[:n] = two_a[:n]
    two[n : 2 * n] = two_b[:n]
    lines = jnp.concatenate([two_a[n:].astype(F32)[:4], two_b[n:].astype(F32)[:4]], axis=0)
    two[2 * n :] = fill(lines)


def norm_grad_kernel(step, stations, rows, sp, *refs):
    out = refs[-1]
    place = lax.rem(ring_place(sp[4], stations) + stations - step, stations)
    chunk = sp[4] ^ ring_station(place, stations)
    for r in range(rows):
        values = [refs[2 * r][chunk], refs[2 * r + 1][chunk]]
        if step > 1:
            values.append(refs[2 * rows][r])
        out[r] = total(*values)


VMEM = pl.BlockSpec(memory_space=pltpu.VMEM)
SMEM = pl.BlockSpec(memory_space=pltpu.SMEM)
HBM = pl.BlockSpec(memory_space=pltpu.HBM)
ANY = pl.BlockSpec(memory_space=pl.ANY)


def call(kernel, ins, outs, scratch=(), us=1.0, limit=16, name=None, scalars=1, specs=None, grid=(), out_specs=None, aliases=None, extra=()):
    count = len(ins)

    def body_of(*refs):
        kernel(*refs[:count], *refs[count + len(extra) :])

    return pl.pallas_call(
        body_of,
        grid=grid,
        in_specs=[SMEM] * scalars + (specs or [VMEM] * (count - scalars)) + [ANY] * len(extra),
        out_specs=out_specs or [VMEM] * len(outs),
        input_output_aliases=aliases or {},
        out_shape=list(outs),
        scratch_shapes=list(scratch),
        compiler_params=pltpu.CompilerParams(vmem_limit_bytes=limit * MIB),
        cost_estimate=pl.CostEstimate(flops=int(us * 1.1e9), bytes_accessed=0, transcendentals=0),
        name=name,
    )(*ins, *extra)


def load(sp, arrays, halved, name, limit=16):
    shapes = [a.shape[:-1] + (a.shape[-1] // (2 if h else 1),) for a, h in zip(arrays, halved)]
    return call(
        functools.partial(load_kernel, halved), [sp] + arrays, [made(s, a.dtype) for s, a in zip(shapes, arrays)],
        scratch=[pltpu.SemaphoreType.DMA] * len(arrays), us=2.0, limit=limit, name=name, specs=[HBM] * len(arrays),
    )


def made(shape, dtype):
    return jax.ShapeDtypeStruct(shape, dtype)


def exchange(array, axis, mask):
    count = lax.axis_size(axis)
    return lax.ppermute(array, axis, [(i, i ^ mask) for i in range(count)])


def merge(kernel, ins, outs, name, extra=()):
    specs = [SMEM if a.dtype == jnp.int32 else VMEM for a in ins]
    return call(kernel, list(ins), list(outs), us=0.05, limit=8, name=name, scalars=0, specs=specs, extra=extra)


def tied(*arrays):
    return lax.optimization_barrier(arrays)


class Chain:
    def __init__(self, token):
        self.token = token

    def __call__(self, function, *args, **kwargs):
        outs = list(function(*args, extra=[self.token], **kwargs))
        self.token = outs[-1]
        return outs

    def hold(self, *arrays):
        *arrays, self.token = tied(*arrays, self.token)
        return arrays


def my_id(bits):
    out = 0
    for axis, mask in bits:
        out = out * 2 + jnp.where((lax.axis_index(axis) & mask) != 0, 1, 0)
    return out


def body(
    tokens, grad_out, crop, offsets, w_query, w_key, w_value, w_out, w_up, w_down, b_query, b_value,
    b_out, b_up, b_down, gain_one, shift_one, gain_two, shift_two,
):
    rows, tok, width = tokens.shape
    seq_count, dp_count = lax.axis_size("seq"), lax.axis_size("dp")
    stations = seq_count // 2
    hidden = w_up.shape[1]
    half = width // 2
    heads = HEADS // 2
    size = half // heads
    chip = 2 * tok
    flat = rows * tok
    small = stations <= 4
    seq = lax.axis_index("seq")
    core, station = seq % 2, seq // 2
    line = lambda v: v.reshape(1, -1)

    order = list(range(0, stations, 2)) + list(range(1, stations, 2))[::-1]
    ring = []
    for i, s in enumerate(order):
        after = order[(i + 1) % stations]
        ring += [(2 * s + c, 2 * after + c) for c in range(2)]

    dp_bits = [("dp", 1 << i) for i in range(dp_count.bit_length() - 1)]
    st_bits = [("seq", 2 << i) for i in range(stations.bit_length() - 1)]
    bit_x, bit_y = dp_bits[:2]
    rest = dp_bits[2:] + st_bits[2:]
    ids = [my_id([bit_x, bit_y] + st_bits[:2]), my_id([bit_y, bit_x] + st_bits[:2])]
    sp = jnp.stack([core, 1 - core, *ids, station]).astype(jnp.int32)

    mine = lambda a: lax.dynamic_slice_in_dim(a, core * half, half, a.ndim - 1)
    weights = jnp.stack([mine(w_query), mine(w_key), mine(w_value)])
    vectors = jnp.stack([gain_one, shift_one, b_query, b_value] + [jnp.zeros_like(gain_one)] * 4)
    state = []
    kept = [[None] * stations for _ in range(4)]
    blocks = {0: tokens}
    turns = [int(f"{i:0{stations.bit_length() - 1}b}"[::-1], 2) for i in range(stations)]
    for at, j in enumerate(turns):
        if j:
            low = j & -j
            block = blocks[j] = exchange(blocks[j ^ low], "seq", 2 * low)
            if at == 1 or at == stations - 1:
                block, state[-1] = tied(block, state[-1])
                blocks[j] = block
        else:
            block = tokens
        other = exchange(block, "seq", 1)
        first, last = at == 0, at == stations - 1
        ins = [sp, offsets, crop, block, other, vectors, weights] + ([] if first else state)
        outs = [
            made((rows, chip, half), BF16),
            made((rows, chip, half), BF16),
            made((rows, half, chip), BF16),
            made((rows, width, chip), BF16),
        ]
        if first:
            outs += [made((rows * heads, chip, 2 * size), BF16)]
        stat = made((rows * heads, 1, chip), F32)
        acc = made((rows * heads, size, chip), F32)
        if last:
            outs += [stat, acc, made((rows, tok, half), BF16), made((rows, tok, half), BF16)]
        else:
            outs += [stat, stat, acc]
        got = call(
            functools.partial(chunk_kernel, j, last, tok, rows), ins, outs,
            us=0.05, limit=LIMITS[0], name=f"attend_chunk_{j}", scalars=3,
        )
        for where, array in zip(kept, got[:4]):
            where[j] = array
        got = got[4:]
        if first:
            query, got = got[0], got[1:]
        if not last:
            state = [query] + list(got)
        if at == 0:
            sp_b, state[-1] = tied(sp, state[-1])
            tokens_v, g_v, wo, up, down, bo, bu, bd, gain_b, shift_b = load(
                sp_b,
                [tokens, grad_out, w_out, w_up, w_down, line(b_out), line(b_up), line(b_down), line(gain_two), line(shift_two)],
                [False] * 10, "load_feed_forward",
            )
            g_other = exchange(g_v, "seq", 1)
            state[-1], up = tied(state[-1], up)
        if at == 1:
            state[-1], g_other = tied(state[-1], g_other)
            g_other = g_other.reshape(flat, width)
    lse, out_t, att_m, att_o = got
    att_r = exchange(att_o, "seq", 1)

    wide = made((flat, width), F32)
    vec8 = made((8, width), F32)
    mid, normed_two, send, total, back, vec_a = call(
        ffn_first_kernel, [sp, att_m, att_r, wo, tokens_v, g_v, up, down, bo, bu, gain_b, shift_b],
        [wide, made((flat, width), BF16), made((flat, hidden + width), BF16), wide, wide, vec8],
        us=4.0, limit=LIMITS[1], name="feed_forward_a",
    )
    got = exchange(send, "seq", 1)
    outputs, hid_m, pre_m, mid_grad, branch, vec_ffn = call(
        ffn_second_kernel, [sp, mid, normed_two, g_v, up, down, bu, bd, gain_b, total, back, vec_a],
        [made((rows, tok, width), BF16), made((flat, hidden // 2), BF16), made((flat, hidden // 2), BF16), wide,
         made((rows, tok, width), BF16), vec8],
        us=4.0, limit=LIMITS[1], name="feed_forward_b",
    )
    branch_r = exchange(branch, "seq", 1)
    piece = made((PIECES // 2, hidden // 2 // PIECES, width), BF16)
    d_keep, d_send, u_keep, u_send = call(
        ffn_grad_kernel, [sp, hid_m, pre_m, normed_two, got, g_v.reshape(flat, width), g_other],
        [piece, piece, piece, piece],
        scratch=[pltpu.VMEM((hidden // 2, width), F32), pltpu.VMEM((width, hidden // 2), F32)],
        us=3.0, limit=LIMITS[2], name="feed_forward_grad",
    )
    chain = Chain(u_keep)

    q = PIECES // GROUP
    d_got, u_got = exchange(d_send, *bit_x), exchange(u_send, *bit_y)

    sums = []
    dn_m, dn_o, dn_r = [], [], []

    def together(name, *jobs):
        ins = [a for _, arrays, _ in jobs for a in arrays]
        outs = [s for _, _, shapes in jobs for s in shapes]

        def kernel(*refs):
            at, to = 0, len(ins)
            for one, arrays, shapes in jobs:
                one(*refs[at : at + len(arrays)], *refs[to : to + len(shapes)])
                at, to = at + len(arrays), to + len(shapes)

        res = iter(chain(functools.partial(merge, kernel), ins, outs, name))
        return [[next(res) for _ in shapes] for _, _, shapes in jobs]

    def norm_job(chunk, before):
        pairs = [a for both in zip(dn_m, dn_r) for a in both]
        kernel = functools.partial(norm_grad_kernel, chunk, stations, rows)
        return (kernel, [sp] + pairs + before, [made((rows, tok, width), BF16)])

    for r in range(rows):
        last = r == rows - 1
        arrays = [branch, branch_r, wo, query, lse, out_t, weights] + [a for part in kept for a in part]
        specs = [VMEM] * len(arrays)
        if not small:
            for i, a in enumerate(arrays):
                if a.ndim == 3 and a is not weights:
                    block_shape = (a.shape[0] // rows,) + a.shape[1:]
                    specs[i] = pl.BlockSpec(block_shape, functools.partial(lambda r, i: (r, 0, 0), r))
        tail = list(sums)
        if last:
            tail += [vectors, vec_ffn]
        part = made((stations, tok, width), BF16)
        grads = [made((width, half), F32)] * 3 + [made((half, width), F32), made((8, half), F32)]
        outs = [part, part] + grads
        scratch = []
        if last:
            outs = [part, part] + [made((width // 2, width), BF16)] * 2 + [made((width // 2 + 16, width), BF16)] * 2
            scratch = [pltpu.VMEM(g.shape, F32) for g in grads] + [pltpu.VMEM((16, width), F32)]
        run = functools.partial(call, functools.partial(attend_back_kernel, stations, tok, r, small, last))
        res = chain(
            run, [sp, offsets, crop] + arrays + tail, outs, scratch=scratch,
            us=BACK_US, limit=LIMITS[3] if small else 48, name=f"attend_back_{r}", scalars=3,
            specs=specs + [VMEM] * len(tail), grid=() if small else (1,),
        )
        dn_m.append(res[0])
        dn_o.append(res[1])
        sums = list(res[2:7])
        if r == rows - 2:
            quarters = made((q,) + piece.shape[1:], BF16)
            ((d_next, u_next),) = together(
                "add_quarters", (upper_kernel, [d_keep, d_got, u_keep, u_got], [quarters, quarters])
            )
            d_got2, u_got2 = exchange(d_next, *bit_y), exchange(u_next, *bit_x)
            dn_r += [exchange(a, "seq", 1) for a in chain.hold(*dn_o)]
    one_keep, one_send, two_keep, two_send = res[2:]

    rd = hidden // 2 // PIECES
    n = width // PIECES
    ff_part, at_part = made((2 * rd, width), BF16), made((2 * n + 16, width), BF16)
    two_of = lambda a: made((2,) + a.shape, BF16)
    token_block = made((rows, tok, width), BF16)
    bit_z, bit_w = st_bits[:2]

    def over_rest(part):
        for i, (where, mask) in enumerate(rest):
            got = exchange(part, where, mask)
            ((part,),) = together(f"add_rest_{i}", (sum_kernel, [part, got], [made(part.shape, BF16)]))
        return part

    def unpack(far, d, d_other, u, u_other, before):
        ins = [sp, d, d_other, u, u_other] + before
        scratch = [
            pltpu.VMEM((GROUP, q * rd, width), F32), pltpu.VMEM((GROUP, q * width // PIECES, hidden // 2), F32),
            pltpu.SemaphoreType.DMA((2 * GROUP,)),
        ]
        return chain(
            functools.partial(call, functools.partial(unpack_ffn_kernel, far)), ins,
            [made((hidden, width), F32), made((width, hidden), F32), made((8, 128), F32)], scratch=scratch, us=0.1,
            limit=LIMITS[4], name="unpack_feed_forward", specs=[VMEM] * 4 + [HBM] * len(before),
            out_specs=[HBM] * 2 + [VMEM], aliases={5: 0, 6: 1} if before else None,
        )[:2]

    def other_core(*arrays):
        return [exchange(a, "seq", 1) for a in arrays]

    two_a, two_b = two_of(ff_part), two_of(at_part)
    dn_r = chain.hold(*dn_r)
    ((a_keep, a_send),) = together(
        "phase_1", (quarter_kernel, [d_keep, d_got, d_got2, u_keep, u_got, u_got2], [two_a, two_a])
    )
    one_send, two_send, dn_last = chain.hold(one_send, two_send, dn_o[-1])
    a_got = exchange(a_send, *bit_z)
    one_got, two_got = exchange(one_send, *bit_x), exchange(two_send, *bit_y)
    dn_r += chain.hold(*other_core(dn_last))

    one_shape, two_shape = made((4 * n, width), BF16), made((4 * n + 16, width), BF16)
    (a_keep, a_send), (one_next, two_next) = together(
        "phase_2",
        (halve_kernel, [a_keep, a_got], [ff_part] * 2),
        (attend_upper_kernel, [one_keep, one_got, two_keep, two_got], [one_shape, two_shape]),
    )
    a_got = exchange(a_send, *bit_w)
    one_got2, two_got2 = exchange(one_next, *bit_y), exchange(two_next, *bit_x)

    (a_own,), (b_keep, b_send) = together(
        "phase_3",
        (sum_kernel, [a_keep, a_got], [ff_part]),
        (attend_quarter_kernel, [one_keep, one_got, one_got2, two_keep, two_got, two_got2], [two_b, two_b]),
    )
    a_own = over_rest(a_own)
    a_near = exchange(a_own, *bit_w)
    b_got = exchange(b_send, *bit_z)

    (a_pair,), (b_keep, b_send) = together(
        "phase_4",
        (pair_kernel, [a_own, a_near], [two_a]),
        (halve_kernel, [b_keep, b_got], [at_part] * 2),
    )
    a_far = exchange(a_pair, *bit_z)
    b_got = exchange(b_send, *bit_w)

    (d_mine, u_mine), (b_own,) = together(
        "phase_5",
        (divide_kernel, [a_pair, a_far], [quarters, quarters]),
        (sum_kernel, [b_keep, b_got], [at_part]),
    )
    b_own = over_rest(b_own)
    d_y, u_x = exchange(d_mine, *bit_y), exchange(u_mine, *bit_x)
    b_near = exchange(b_own, *bit_w)

    (d_near, u_near), (b_pair,), (moving,) = together(
        "phase_6",
        (join_kernel, [d_mine, d_y, u_mine, u_x], [piece, piece]),
        (pair_kernel, [b_own, b_near], [two_b]),
        norm_job(1, []),
    )
    d_far, u_far = exchange(d_near, *bit_x), exchange(u_near, *bit_y)
    b_far = exchange(b_pair, *bit_z)
    moving = lax.ppermute(moving, "seq", ring)
    for chunk in range(2, stations - 2):
        ((moving,),) = together("norm_step", norm_job(chunk, [moving]))
        moving = lax.ppermute(moving, "seq", ring)
    d_far, u_far = chain.hold(d_far, u_far)

    (one_mine, two_mine), (moving,) = together(
        "phase_7",
        (attend_divide_kernel, [b_pair, b_far], [one_shape, two_shape]),
        norm_job(stations - 2, [moving]),
    )
    one_y, two_x = exchange(one_mine, *bit_y), exchange(two_mine, *bit_x)
    moving = lax.ppermute(moving, "seq", ring)
    d_near, u_near = chain.hold(d_near, u_near)
    d_near_o, u_near_o = chain.hold(*other_core(d_near, u_near))
    grad_down, grad_up = unpack(False, d_near, d_near_o, u_near, u_near_o, [])

    (one_near, two_near), (moving,) = together(
        "phase_8",
        (
            attend_join_kernel, [one_mine, one_y, two_mine, two_x],
            [made((8 * n, width), BF16), made((8 * n + 16, width), BF16)],
        ),
        norm_job(stations - 1, [moving]),
    )
    one_far, two_far = exchange(one_near, *bit_x), exchange(two_near, *bit_y)
    moving = lax.ppermute(moving, "seq", ring)
    d_far, u_far = chain.hold(d_far, u_far)
    d_far_o, u_far_o = chain.hold(*other_core(d_far, u_far))
    grad_down, grad_up = unpack(True, d_far, d_far_o, u_far, u_far_o, [grad_down, grad_up])
    one_near_o, two_near_o = other_core(*chain.hold(one_near, two_near))
    one_far_o, two_far_o = other_core(*chain.hold(one_far, two_far))
    pairs = [a for both in zip(dn_m, dn_r) for a in both]
    input_grad = call(
        last_kernel, [tokens_v, vectors, mid_grad] + pairs + [moving], [token_block],
        us=0.1, limit=LIMITS[4], name="input_grad", scalars=0, extra=[chain.token],
    )[0]
    one_all = [one_near, one_far, one_near_o, one_far_o]
    two_all = [two_near, two_far, two_near_o, two_far_o]
    square = made((width, width), F32)
    run = functools.partial(call, unpack_attend_kernel)
    thin = made((1, width), F32)
    results = chain(
        run, [sp] + one_all + two_all, [square] * 4 + [thin] * 3 + [made((1, hidden), F32)] + [thin] * 5,
        scratch=[pltpu.VMEM((PIECES, width), F32)], us=0.1, limit=LIMITS[4], name="unpack_attend",
    )
    grad_query, grad_key, grad_value, grad_out_proj = results[:4]
    lines = [r.reshape(-1) for r in results[4:]]

    return (outputs, input_grad, grad_query, grad_key, grad_value, grad_out_proj, grad_up, grad_down, *lines)


def solution(mesh):
    split, row, copied = P("dp", "seq", None), P("dp"), P()
    return jax.shard_map(
        body,
        mesh=mesh,
        in_specs=(split, split, row, P("dp", None)) + (copied,) * 15,
        out_specs=(split, split) + (copied,) * 15,
        check_vma=False,
    )
```

profile of v0, /device:TPU:0, one launch (start us, length us, event | category | flops | bytes accessed | tf_op | source)
XLA Modules:
  0.0 168.1 jit_solution(6698303165127748278)
XLA Ops:
  1.2 3.7 %collective-permute-start = (bf16[3,128,512]{2,1,0:T(8,128)(2,1)}, bf16[3,128,512]{2,1,0:T(8,128)(2,1)S(1)}, u32[]{:S(2)}, u32[]{:S(2)}) collective-permute-start(bf16[3,128,512]{2,1,0:T(8,128)(2,1)} %refs_1_.9), channel_id=1, source_target_pairs={{0,4},{1,5},{2,6},{3,7},{4,0},{5,1},{6,2},{7,3},{8,12},{9,13},{10,... | collective-permute-start | bytes 1179656 | tf_op jit(solution)/shard_map/ppermute | solution.py:635
  10.7 3.5 %attend_chunk_0.1 = (bf16[3,256,256]{2,1,0:T(8,128)(2,1)S(1)}, bf16[3,256,256]{2,1,0:T(8,128)(2,1)S(1)}, bf16[3,256,256]{2,1,0:T(8,128)(2,1)S(1)}, bf16[3,512,25...) custom-call(s32[5]{0:T(128)S(1)} %stack.53.refs_0_.refs_6_.refs_2_.r, ...), custom_call_target="tpu_custom_call" | custom-call | flops 55000000 | tf_op jit(solution)/shard_map/attend_chunk_0/pallas_call | solution.py:607
  17.6 5.8 %collective-permute-done.refs_3_ = bf16[3,128,512]{2,1,0:T(8,128)(2,1)S(1)} collective-permute-done((bf16[3,128,512]{2,1,0:T(8,128)(2,1)}, bf16[3,128,512]{2,1,0:T(8,128)(2,1)S(1)}, u32[]{:S(2)}, u32[]{:S(2)}) %collective-permute-start) | collective-permute-done | bytes 393248 | tf_op jit(solution)/shard_map/ppermute | solution.py:635
  25.1 3.4 %attend_chunk_2.1 = (bf16[3,256,256]{2,1,0:T(8,128)(2,1)S(1)}, bf16[3,256,256]{2,1,0:T(8,128)(2,1)S(1)}, bf16[3,256,256]{2,1,0:T(8,128)(2,1)S(1)}, bf16[3,512,25...) custom-call(s32[5]{0:T(128)S(1)} %stack.53.refs_0_.refs_6_.refs_2_.refs, ...), custom_call_target="tpu_custom_call" | custom-call | flops 55000000 | tf_op jit(solution)/shard_map/attend_chunk_2/pallas_call | solution.py:607
  28.4 3.4 %attend_chunk_1.1 = (bf16[3,256,256]{2,1,0:T(8,128)(2,1)S(1)}, bf16[3,256,256]{2,1,0:T(8,128)(2,1)S(1)}, bf16[3,256,256]{2,1,0:T(8,128)(2,1)S(1)}, bf16[3,512,25...) custom-call(s32[5]{0:T(128)S(1)} %stack.53.refs_0_.refs_6_.refs_2_.refs, ...), custom_call_target="tpu_custom_call" | custom-call | flops 55000000 | tf_op jit(solution)/shard_map/attend_chunk_1/pallas_call | solution.py:607
  31.8 3.6 %collective-permute-done.2.refs_3_ = bf16[3,128,512]{2,1,0:T(8,128)(2,1)S(1)} collective-permute-done((bf16[3,128,512]{2,1,0:T(8,128)(2,1)S(1)}, bf16[3,128,512]{2,1,0:T(8,128)(2,1)S(1)}, u32[]{:S(2)}, u32[]{:S(2)}) %collective-permute-start.2) | collective-permute-done | bytes 393248 | tf_op jit(solution)/shard_map/ppermute | solution.py:635
  37.1 3.5 %attend_chunk_3.1 = (bf16[3,256,256]{2,1,0:T(8,128)(2,1)S(1)}, bf16[3,256,256]{2,1,0:T(8,128)(2,1)S(1)}, bf16[3,256,256]{2,1,0:T(8,128)(2,1)S(1)}, bf16[3,512,25...) custom-call(s32[5]{0:T(128)S(1)} %stack.53.refs_0_.refs_6_.refs_2_.r, ...), custom_call_target="tpu_custom_call" | custom-call | flops 55000000 | tf_op jit(solution)/shard_map/attend_chunk_3/pallas_call | solution.py:607
  42.1 3.4 %feed_forward_a.1 = (f32[384,512]{1,0:T(8,128)S(1)}, bf16[384,512]{1,0:T(8,128)(2,1)S(1)}, bf16[384,2560]{1,0:T(8,128)(2,1)S(1)}, f32[384,512]{1,0:T(8,128)S(1)}...) custom-call(s32[5]{0:T(128)S(1)} %stack.53.refs_0_.refs_6_.refs_2_.refs_4_, ...), custom_call_target="tpu_custom_call" | custom-call | flops 4400000000 | tf_op jit(solution)/shard_map/feed_forward_a/pallas_call | solution.py:607
  45.7 3.7 %feed_forward_b.1 = (bf16[3,128,512]{2,1,0:T(8,128)(2,1)}, bf16[384,1024]{1,0:T(8,128)(2,1)S(1)}, bf16[384,1024]{1,0:T(8,128)(2,1)S(1)}, f32[384,512]{1,0:T(8,12...) custom-call(s32[5]{0:T(128)S(1)} %stack.53.refs_0_.refs_6_.refs_2_.refs_4_, ...), custom_call_target="tpu_custom_call" | custom-call | flops 4400000000 | tf_op jit(solution)/shard_map/feed_forward_b/pallas_call | solution.py:607
  49.5 3.1 %feed_forward_grad.1 = (bf16[8,64,512]{2,1,0:T(8,128)(2,1)S(1)}, bf16[8,64,512]{2,1,0:T(8,128)(2,1)S(1)}, bf16[8,64,512]{2,1,0:T(8,128)(2,1)S(1)}, bf16[8,64,512]{2,1,0:T(8,128)(2,1)S(1)}) custom-call(s32[5]{0:T(128)S(1)} %stack.53.refs_0_.refs_6_.refs_2_.refs_4_, bf16[384,1024]{1,0:T(8,128)(2,1)S(1)} %get-tuple-element.239.refs_1_, ...), custom_call_target="tpu_custom_call" | custom-call | flops 3300000000 | tf_op jit(solution)/shard_map/feed_forward_grad/pallas_call | solution.py:607
  57.5 5.2 %attend_back_0.1 = (bf16[4,128,512]{2,1,0:T(8,128)(2,1)S(1)}, bf16[4,128,512]{2,1,0:T(8,128)(2,1)S(1)}, f32[512,256]{1,0:T(8,128)S(1)}, f32[512,256]{1,0:T(8,128...) custom-call(s32[5]{0:T(128)S(1)} %stack.53.refs_0_.refs_6_.refs_2_.refs_4_, ...), custom_call_target="tpu_custom_call" | custom-call | flops 55000000 | tf_op jit(solution)/shard_map/attend_back_0/pallas_call | solution.py:607
  62.8 5.5 %attend_back_1.1 = (bf16[4,128,512]{2,1,0:T(8,128)(2,1)S(1)}, bf16[4,128,512]{2,1,0:T(8,128)(2,1)S(1)}, f32[512,256]{1,0:T(8,128)S(1)}, f32[512,256]{1,0:T(8,128...) custom-call(s32[5]{0:T(128)S(1)} %stack.53.refs_0_.refs_6_.refs_2_.refs_4_, ...), custom_call_target="tpu_custom_call" | custom-call | flops 55000000 | tf_op jit(solution)/shard_map/attend_back_1/pallas_call | solution.py:607
  70.8 5.9 %attend_back_2.1 = (bf16[4,128,512]{2,1,0:T(8,128)(2,1)S(1)}, bf16[4,128,512]{2,1,0:T(8,128)(2,1)S(1)}, bf16[256,512]{1,0:T(8,128)(2,1)S(1)}, bf16[256,512]{1,0:...) custom-call(s32[5]{0:T(128)S(1)} %stack.53.refs_0_.refs_6_.refs_2_.refs_4_, ...), custom_call_target="tpu_custom_call" | custom-call | flops 55000000 | tf_op jit(solution)/shard_map/attend_back_2/pallas_call | solution.py:607
  81.0 6.7 %collective-permute-done.19.refs_3_ = bf16[256,512]{1,0:T(8,128)(2,1)S(1)} collective-permute-done((bf16[256,512]{1,0:T(8,128)(2,1)S(1)}, bf16[256,512]{1,0:T(8,128)(2,1)S(1)}, u32[]{:S(2)}, u32[]{:S(2)}) %collective-permute-start.19) | collective-permute-done | bytes 262176 | tf_op jit(solution)/shard_map/ppermute | solution.py:635
  89.7 2.2 %collective-permute-start.21 = (bf16[128,512]{1,0:T(8,128)(2,1)S(1)}, bf16[128,512]{1,0:T(8,128)(2,1)S(1)}, u32[]{:S(2)}, u32[]{:S(2)}) collective-permute-start(bf16[128,512]{1,0:T(8,128)(2,1)S(1)} %get-tuple-element.285), channel_id=1, source_target_pairs={{0,4},{1,5},{2,6},{3,7},{4,0},{5,1},{6,2},{7,3},{8,12},{9,13},{10,... | collective-permute-start | bytes 393224 | tf_op jit(solution)/shard_map/ppermute | solution.py:635
  93.2 4.4 %collective-permute-done.21.refs_1_ = bf16[128,512]{1,0:T(8,128)(2,1)S(1)} collective-permute-done((bf16[128,512]{1,0:T(8,128)(2,1)S(1)}, bf16[128,512]{1,0:T(8,128)(2,1)S(1)}, u32[]{:S(2)}, u32[]{:S(2)}) %collective-permute-start.21) | collective-permute-done | bytes 131104 | tf_op jit(solution)/shard_map/ppermute | solution.py:635
  98.8 2.6 %collective-permute-start.24 = (bf16[128,512]{1,0:T(8,128)(2,1)S(1)}, bf16[128,512]{1,0:T(8,128)(2,1)S(1)}, u32[]{:S(2)}, u32[]{:S(2)}) collective-permute-start(bf16[128,512]{1,0:T(8,128)(2,1)S(1)} %get-tuple-element.288.refs_0_), channel_id=1, source_target_pairs={{0,4},{1,5},{2,6},{3,7},{4,0},{5,1},{6,2},{7,3},{8,12},{9,13},{10,... | collective-permute-start | bytes 393224 | tf_op jit(solution)/shard_map/ppermute | solution.py:635
  101.5 4.4 %collective-permute-done.24.refs_1_ = bf16[128,512]{1,0:T(8,128)(2,1)S(1)} collective-permute-done((bf16[128,512]{1,0:T(8,128)(2,1)S(1)}, bf16[128,512]{1,0:T(8,128)(2,1)S(1)}, u32[]{:S(2)}, u32[]{:S(2)}) %collective-permute-start.24) | collective-permute-done | bytes 131104 | tf_op jit(solution)/shard_map/ppermute | solution.py:635
  108.0 2.0 %collective-permute-start.27 = (bf16[80,512]{1,0:T(8,128)(2,1)S(1)}, bf16[80,512]{1,0:T(8,128)(2,1)S(1)}, u32[]{:S(2)}, u32[]{:S(2)}) collective-permute-start(bf16[80,512]{1,0:T(8,128)(2,1)S(1)} %get-tuple-element.293.refs_4_), channel_id=1, source_target_pairs={{0,4},{1,5},{2,6},{3,7},{4,0},{5,1},{6,2},{7,3},{8,12},{9,13},{10,... | collective-permute-start | bytes 245768 | tf_op jit(solution)/shard_map/ppermute | solution.py:635
  110.0 4.2 %collective-permute-done.27.refs_3_ = bf16[80,512]{1,0:T(8,128)(2,1)S(1)} collective-permute-done((bf16[80,512]{1,0:T(8,128)(2,1)S(1)}, bf16[80,512]{1,0:T(8,128)(2,1)S(1)}, u32[]{:S(2)}, u32[]{:S(2)}) %collective-permute-start.27) | collective-permute-done | bytes 81952 | tf_op jit(solution)/shard_map/ppermute | solution.py:635
  116.4 2.6 %collective-permute-start.30 = (bf16[80,512]{1,0:T(8,128)(2,1)S(1)}, bf16[80,512]{1,0:T(8,128)(2,1)S(1)}, u32[]{:S(2)}, u32[]{:S(2)}) collective-permute-start(bf16[80,512]{1,0:T(8,128)(2,1)S(1)} %get-tuple-element.296.refs_4_.refs_13_), channel_id=1, source_target_pairs={{0,4},{1,5},{2,6},{3,7},{4,0},{5,1},{6,2},{7,3},{8,12},{9,13},{10,... | collective-permute-start | bytes 245768 | tf_op jit(solution)/shard_map/ppermute | solution.py:635
  119.0 2.7 %collective-permute-done.30.refs_5_ = bf16[80,512]{1,0:T(8,128)(2,1)S(1)} collective-permute-done((bf16[80,512]{1,0:T(8,128)(2,1)S(1)}, bf16[80,512]{1,0:T(8,128)(2,1)S(1)}, u32[]{:S(2)}, u32[]{:S(2)}) %collective-permute-start.30) | collective-permute-done | bytes 81952 | tf_op jit(solution)/shard_map/ppermute | solution.py:635
  125.7 2.3 %collective-permute-start.32 = (bf16[3,128,512]{2,1,0:T(8,128)(2,1)S(1)}, bf16[3,128,512]{2,1,0:T(8,128)(2,1)S(1)}, u32[]{:S(2)}, u32[]{:S(2)}) collective-permute-start(bf16[3,128,512]{2,1,0:T(8,128)(2,1)S(1)} %get-tuple-element.301.refs_10_), channel_id=1, source_target_pairs={{0,4},{1,5},{4,6},{5,7},{6,2},{7,3},{2,0},{3,1},{8,12},{9,13},{12,... | collective-permute-start | bytes 1179656 | tf_op jit(solution)/shard_map/ppermute | solution.py:925
  128.0 5.3 %collective-permute-done.33.refs_1_ = bf16[8,64,512]{2,1,0:T(8,128)(2,1)S(1)} collective-permute-done((bf16[8,64,512]{2,1,0:T(8,128)(2,1)S(1)}, bf16[8,64,512]{2,1,0:T(8,128)(2,1)S(1)}, u32[]{:S(2)}, u32[]{:S(2)}) %collective-permute-start.33) | collective-permute-done | bytes 524320 | tf_op jit(solution)/shard_map/ppermute | solution.py:635
  133.4 2.4 %collective-permute-done.31.refs_1_ = bf16[2,80,512]{2,1,0:T(8,128)(2,1)S(1)} collective-permute-done((bf16[2,80,512]{2,1,0:T(8,128)(2,1)S(1)}, bf16[2,80,512]{2,1,0:T(8,128)(2,1)S(1)}, u32[]{:S(2)}, u32[]{:S(2)}) %collective-permute-start.31) | collective-permute-done | bytes 163872 | tf_op jit(solution)/shard_map/ppermute | solution.py:635
  137.1 2.0 %collective-permute-start.37 = (bf16[3,128,512]{2,1,0:T(8,128)(2,1)S(1)}, bf16[3,128,512]{2,1,0:T(8,128)(2,1)S(1)}, u32[]{:S(2)}, u32[]{:S(2)}) collective-permute-start(bf16[3,128,512]{2,1,0:T(8,128)(2,1)S(1)} %get-tuple-element.310.refs_5_), channel_id=1, source_target_pairs={{0,4},{1,5},{4,6},{5,7},{6,2},{7,3},{2,0},{3,1},{8,12},{9,13},{12,... | collective-permute-start | bytes 1179656 | tf_op jit(solution)/shard_map/ppermute | solution.py:937
  142.0 2.7 %unpack_feed_forward.2 = (f32[2048,512]{1,0:T(8,128)}, f32[512,2048]{1,0:T(8,128)}, f32[8,128]{1,0:T(8,128)S(1)}) custom-call(s32[5]{0:T(128)S(1)} %stack.53.refs_0_.refs_6_.refs_2_.refs_4_, bf16[8,64,512]{2,1,0:T(8,128)(2,1)S(1)} %get-tuple-element.305.refs_1_, bf16[8,64,512]{2,1,0:T(8,128)(2,1)S(1)} %collective-permute-done.38.refs_2_, ...), custom_call_target="tpu_custom_call" | custom-call | flops 110000000 | tf_op jit(solution)/shard_map/unpack_feed_forward/pallas_call | solution.py:607
  145.4 3.6 %collective-permute-done.37.refs_11_ = bf16[3,128,512]{2,1,0:T(8,128)(2,1)S(1)} collective-permute-done((bf16[3,128,512]{2,1,0:T(8,128)(2,1)S(1)}, bf16[3,128,512]{2,1,0:T(8,128)(2,1)S(1)}, u32[]{:S(2)}, u32[]{:S(2)}) %collective-permute-start.37) | collective-permute-done | bytes 393248 | tf_op jit(solution)/shard_map/ppermute | solution.py:937
  152.0 3.3 %collective-permute-start.40 = (bf16[3,128,512]{2,1,0:T(8,128)(2,1)S(1)}, bf16[3,128,512]{2,1,0:T(8,128)(2,1)S(1)}, u32[]{:S(2)}, u32[]{:S(2)}) collective-permute-start(bf16[3,128,512]{2,1,0:T(8,128)(2,1)S(1)} %get-tuple-element.324.refs_7_), channel_id=1, source_target_pairs={{0,4},{1,5},{4,6},{5,7},{6,2},{7,3},{2,0},{3,1},{8,12},{9,13},{12,... | collective-permute-start | bytes 1179656 | tf_op jit(solution)/shard_map/ppermute | solution.py:951
  155.3 2.7 %unpack_feed_forward.3 = (f32[2048,512]{1,0:T(8,128)}, f32[512,2048]{1,0:T(8,128)}, f32[8,128]{1,0:T(8,128)S(1)}) custom-call(s32[5]{0:T(128)S(1)} %stack.53.refs_0_.refs_6_.refs_2_.refs_4_, bf16[8,64,512]{2,1,0:T(8,128)(2,1)S(1)} %collective-permute-done.33.refs_1_, ...), custom_call_target="tpu_custom_call", output_to_operand_aliasing={{0}: (5, {}), {1}: (6, {})} | custom-call | flops 110000000 | tf_op jit(solution)/shard_map/unpack_feed_forward/pallas_call | solution.py:607
  159.9 3.6 %collective-permute-done.40.refs_9_ = bf16[3,128,512]{2,1,0:T(8,128)(2,1)S(1)} collective-permute-done((bf16[3,128,512]{2,1,0:T(8,128)(2,1)S(1)}, bf16[3,128,512]{2,1,0:T(8,128)(2,1)S(1)}, u32[]{:S(2)}, u32[]{:S(2)}) %collective-permute-start.40) | collective-permute-done | bytes 393248 | tf_op jit(solution)/shard_map/ppermute | solution.py:951
  164.9 2.7 %unpack_attend.1 = (f32[512,512]{1,0:T(8,128)}, f32[512,512]{1,0:T(8,128)}, f32[512,512]{1,0:T(8,128)}, f32[512,512]{1,0:T(8,128)}, f32[1,512]{1,0:T(1,128)}, /*...) custom-call(s32[5]{0:T(128)S(1)} %stack.53.refs_0_.refs_6_.refs_2_.r, ...), custom_call_target="tpu_custom_call" | custom-call | flops 110000000 | tf_op jit(solution)/shard_map/unpack_attend/pallas_call | solution.py:607
  (124 shorter events, 50.6 us)
Async XLA Ops:
  0.7 10.0 %collective-permute-start.1 = (bf16[3,128,512]{2,1,0:T(8,128)(2,1)}, bf16[3,128,512]{2,1,0:T(8,128)(2,1)S(1)}, u32[]{:S(2)}, u32[]{:S(2)}) collective-permute-start(bf16[3,128,512]{2,1,0:T(8,128)(2,1)} %refs_1_.9), channel_id=1, source_target_pairs={{0,1},{1,0},{2,3},{3,2},{4,5},{5,4},{6,7},{7,6},{8,9},{9,8},{10,11... | collective-permute-start | bytes 1179656 | tf_op jit(solution)/shard_map/ppermute | solution.py:635
  1.2 22.1 %collective-permute-start = (bf16[3,128,512]{2,1,0:T(8,128)(2,1)}, bf16[3,128,512]{2,1,0:T(8,128)(2,1)S(1)}, u32[]{:S(2)}, u32[]{:S(2)}) collective-permute-start(bf16[3,128,512]{2,1,0:T(8,128)(2,1)} %refs_1_.9), channel_id=1, source_target_pairs={{0,4},{1,5},{2,6},{3,7},{4,0},{5,1},{6,2},{7,3},{8,12},{9,13},{10,... | collective-permute-start | bytes 1179656 | tf_op jit(solution)/shard_map/ppermute | solution.py:635
  4.9 19.0 %collective-permute-start.3 = (bf16[3,128,512]{2,1,0:T(8,128)(2,1)}, bf16[3,128,512]{2,1,0:T(8,128)(2,1)S(1)}, u32[]{:S(2)}, u32[]{:S(2)}) collective-permute-start(bf16[3,128,512]{2,1,0:T(8,128)(2,1)} %refs_1_.9), channel_id=1, source_target_pairs={{0,2},{1,3},{2,0},{3,1},{4,6},{5,7},{6,4},{7,5},{8,10},{9,11},{10,... | collective-permute-start | bytes 1179656 | tf_op jit(solution)/shard_map/ppermute | solution.py:635
  23.9 11.5 %collective-permute-start.2 = (bf16[3,128,512]{2,1,0:T(8,128)(2,1)S(1)}, bf16[3,128,512]{2,1,0:T(8,128)(2,1)S(1)}, u32[]{:S(2)}, u32[]{:S(2)}) collective-permute-start(bf16[3,128,512]{2,1,0:T(8,128)(2,1)S(1)} %collective-permute-done.refs_3_), channel_id=1, source_target_pairs={{0,2},{1,3},{2,0},{3,1},{4,6},{5,7},{6,4},{7,5},{8,10},{9,11},{10,... | collective-permute-start | bytes 1179656 | tf_op jit(solution)/shard_map/ppermute | solution.py:635
  52.6 15.6 %collective-permute-start.11 = (bf16[8,64,512]{2,1,0:T(8,128)(2,1)S(1)}, bf16[8,64,512]{2,1,0:T(8,128)(2,1)S(1)}, u32[]{:S(2)}, u32[]{:S(2)}) collective-permute-start(bf16[8,64,512]{2,1,0:T(8,128)(2,1)S(1)} %get-tuple-element.253), channel_id=1, source_target_pairs={{0,8},{8,0},{16,24},{24,16},{1,9},{9,1},{17,25},{25,17},{2,10},{10... | collective-permute-start | bytes 1572872 | tf_op jit(solution)/shard_map/ppermute | solution.py:635
  54.2 14.0 %collective-permute-start.12 = (bf16[8,64,512]{2,1,0:T(8,128)(2,1)S(1)}, bf16[8,64,512]{2,1,0:T(8,128)(2,1)S(1)}, u32[]{:S(2)}, u32[]{:S(2)}) collective-permute-start(bf16[8,64,512]{2,1,0:T(8,128)(2,1)S(1)} %get-tuple-element.254), channel_id=1, source_target_pairs={{0,16},{8,24},{16,0},{24,8},{1,17},{9,25},{17,1},{25,9},{2,18},{10... | collective-permute-start | bytes 1572872 | tf_op jit(solution)/shard_map/ppermute | solution.py:635
  68.4 8.4 %collective-permute-start.13 = (bf16[4,128,512]{2,1,0:T(8,128)(2,1)S(1)}, bf16[4,128,512]{2,1,0:T(8,128)(2,1)S(1)}, u32[]{:S(2)}, u32[]{:S(2)}) collective-permute-start(bf16[4,128,512]{2,1,0:T(8,128)(2,1)S(1)} %get-tuple-element.257), channel_id=1, source_target_pairs={{0,1},{1,0},{2,3},{3,2},{4,5},{5,4},{6,7},{7,6},{8,9},{9,8},{10,11... | collective-permute-start | bytes 1572872 | tf_op jit(solution)/shard_map/ppermute | solution.py:635
  68.6 8.2 %collective-permute-start.14 = (bf16[4,128,512]{2,1,0:T(8,128)(2,1)S(1)}, bf16[4,128,512]{2,1,0:T(8,128)(2,1)S(1)}, u32[]{:S(2)}, u32[]{:S(2)}) collective-permute-start(bf16[4,128,512]{2,1,0:T(8,128)(2,1)S(1)} %get-tuple-element.258), channel_id=1, source_target_pairs={{0,1},{1,0},{2,3},{3,2},{4,5},{5,4},{6,7},{7,6},{8,9},{9,8},{10,11... | collective-permute-start | bytes 1572872 | tf_op jit(solution)/shard_map/ppermute | solution.py:635
  69.0 8.3 %collective-permute-start.15 = (bf16[4,64,512]{2,1,0:T(8,128)(2,1)S(1)}, bf16[4,64,512]{2,1,0:T(8,128)(2,1)S(1)}, u32[]{:S(2)}, u32[]{:S(2)}) collective-permute-start(bf16[4,64,512]{2,1,0:T(8,128)(2,1)S(1)} %get-tuple-element.272), channel_id=1, source_target_pairs={{0,16},{8,24},{16,0},{24,8},{1,17},{9,25},{17,1},{25,9},{2,18},{10... | collective-permute-start | bytes 786440 | tf_op jit(solution)/shard_map/ppermute | solution.py:635
  70.3 8.0 %collective-permute-start.16 = (bf16[4,64,512]{2,1,0:T(8,128)(2,1)S(1)}, bf16[4,64,512]{2,1,0:T(8,128)(2,1)S(1)}, u32[]{:S(2)}, u32[]{:S(2)}) collective-permute-start(bf16[4,64,512]{2,1,0:T(8,128)(2,1)S(1)} %get-tuple-element.264.refs_33_), channel_id=1, source_target_pairs={{0,8},{8,0},{16,24},{24,16},{1,9},{9,1},{17,25},{25,17},{2,10},{10... | collective-permute-start | bytes 786440 | tf_op jit(solution)/shard_map/ppermute | solution.py:635
  78.6 9.4 %collective-permute-start.20 = (bf16[272,512]{1,0:T(8,128)(2,1)S(1)}, bf16[272,512]{1,0:T(8,128)(2,1)S(1)}, u32[]{:S(2)}, u32[]{:S(2)}) collective-permute-start(bf16[272,512]{1,0:T(8,128)(2,1)S(1)} %get-tuple-element.282.refs_6_), channel_id=1, source_target_pairs={{0,16},{8,24},{16,0},{24,8},{1,17},{9,25},{17,1},{25,9},{2,18},{10... | collective-permute-start | bytes 835592 | tf_op jit(solution)/shard_map/ppermute | solution.py:635
  79.4 8.4 %collective-permute-start.19 = (bf16[256,512]{1,0:T(8,128)(2,1)S(1)}, bf16[256,512]{1,0:T(8,128)(2,1)S(1)}, u32[]{:S(2)}, u32[]{:S(2)}) collective-permute-start(bf16[256,512]{1,0:T(8,128)(2,1)S(1)} %get-tuple-element.280), channel_id=1, source_target_pairs={{0,8},{8,0},{16,24},{24,16},{1,9},{9,1},{17,25},{25,17},{2,10},{10... | collective-permute-start | bytes 786440 | tf_op jit(solution)/shard_map/ppermute | solution.py:635
  79.9 8.1 %collective-permute-start.18 = (bf16[2,128,512]{2,1,0:T(8,128)(2,1)S(1)}, bf16[2,128,512]{2,1,0:T(8,128)(2,1)S(1)}, u32[]{:S(2)}, u32[]{:S(2)}) collective-permute-start(bf16[2,128,512]{2,1,0:T(8,128)(2,1)S(1)} %get-tuple-element.283.refs_6_), channel_id=1, source_target_pairs={{0,2},{1,3},{2,0},{3,1},{4,6},{5,7},{6,4},{7,5},{8,10},{9,11},{10,... | collective-permute-start | bytes 786440 | tf_op jit(solution)/shard_map/ppermute | solution.py:635
  88.2 9.4 %collective-permute-start.23 = (bf16[144,512]{1,0:T(8,128)(2,1)S(1)}, bf16[144,512]{1,0:T(8,128)(2,1)S(1)}, u32[]{:S(2)}, u32[]{:S(2)}) collective-permute-start(bf16[144,512]{1,0:T(8,128)(2,1)S(1)} %get-tuple-element.287.refs_8_), channel_id=1, source_target_pairs={{0,8},{8,0},{16,24},{24,16},{1,9},{9,1},{17,25},{25,17},{2,10},{10... | collective-permute-start | bytes 442376 | tf_op jit(solution)/shard_map/ppermute | solution.py:635
  89.7 7.8 %collective-permute-start.21 = (bf16[128,512]{1,0:T(8,128)(2,1)S(1)}, bf16[128,512]{1,0:T(8,128)(2,1)S(1)}, u32[]{:S(2)}, u32[]{:S(2)}) collective-permute-start(bf16[128,512]{1,0:T(8,128)(2,1)S(1)} %get-tuple-element.285), channel_id=1, source_target_pairs={{0,4},{1,5},{2,6},{3,7},{4,0},{5,1},{6,2},{7,3},{8,12},{9,13},{10,... | collective-permute-start | bytes 393224 | tf_op jit(solution)/shard_map/ppermute | solution.py:635
  97.7 8.2 %collective-permute-start.25 = (bf16[2,80,512]{2,1,0:T(8,128)(2,1)S(1)}, bf16[2,80,512]{2,1,0:T(8,128)(2,1)S(1)}, u32[]{:S(2)}, u32[]{:S(2)}) collective-permute-start(bf16[2,80,512]{2,1,0:T(8,128)(2,1)S(1)} %get-tuple-element.290.refs_4_), channel_id=1, source_target_pairs={{0,2},{1,3},{2,0},{3,1},{4,6},{5,7},{6,4},{7,5},{8,10},{9,11},{10,... | collective-permute-start | bytes 491528 | tf_op jit(solution)/shard_map/ppermute | solution.py:635
  98.8 7.1 %collective-permute-start.24 = (bf16[128,512]{1,0:T(8,128)(2,1)S(1)}, bf16[128,512]{1,0:T(8,128)(2,1)S(1)}, u32[]{:S(2)}, u32[]{:S(2)}) collective-permute-start(bf16[128,512]{1,0:T(8,128)(2,1)S(1)} %get-tuple-element.288.refs_0_), channel_id=1, source_target_pairs={{0,4},{1,5},{2,6},{3,7},{4,0},{5,1},{6,2},{7,3},{8,12},{9,13},{10,... | collective-permute-start | bytes 393224 | tf_op jit(solution)/shard_map/ppermute | solution.py:635
  106.0 8.4 %collective-permute-start.26 = (bf16[2,128,512]{2,1,0:T(8,128)(2,1)S(1)}, bf16[2,128,512]{2,1,0:T(8,128)(2,1)S(1)}, u32[]{:S(2)}, u32[]{:S(2)}) collective-permute-start(bf16[2,128,512]{2,1,0:T(8,128)(2,1)S(1)} %get-tuple-element.291.refs_0_), channel_id=1, source_target_pairs={{0,2},{1,3},{2,0},{3,1},{4,6},{5,7},{6,4},{7,5},{8,10},{9,11},{10,... | collective-permute-start | bytes 786440 | tf_op jit(solution)/shard_map/ppermute | solution.py:635
  108.0 6.2 %collective-permute-start.27 = (bf16[80,512]{1,0:T(8,128)(2,1)S(1)}, bf16[80,512]{1,0:T(8,128)(2,1)S(1)}, u32[]{:S(2)}, u32[]{:S(2)}) collective-permute-start(bf16[80,512]{1,0:T(8,128)(2,1)S(1)} %get-tuple-element.293.refs_4_), channel_id=1, source_target_pairs={{0,4},{1,5},{2,6},{3,7},{4,0},{5,1},{6,2},{7,3},{8,12},{9,13},{10,... | collective-permute-start | bytes 245768 | tf_op jit(solution)/shard_map/ppermute | solution.py:635
  114.4 7.4 %collective-permute-start.28 = (bf16[4,64,512]{2,1,0:T(8,128)(2,1)S(1)}, bf16[4,64,512]{2,1,0:T(8,128)(2,1)S(1)}, u32[]{:S(2)}, u32[]{:S(2)}) collective-permute-start(bf16[4,64,512]{2,1,0:T(8,128)(2,1)S(1)} %get-tuple-element.294.refs_0_), channel_id=1, source_target_pairs={{0,16},{8,24},{16,0},{24,8},{1,17},{9,25},{17,1},{25,9},{2,18},{10... | collective-permute-start | bytes 786440 | tf_op jit(solution)/shard_map/ppermute | solution.py:635
  115.7 7.4 %collective-permute-start.29 = (bf16[4,64,512]{2,1,0:T(8,128)(2,1)S(1)}, bf16[4,64,512]{2,1,0:T(8,128)(2,1)S(1)}, u32[]{:S(2)}, u32[]{:S(2)}) collective-permute-start(bf16[4,64,512]{2,1,0:T(8,128)(2,1)S(1)} %get-tuple-element.295.refs_2_), channel_id=1, source_target_pairs={{0,8},{8,0},{16,24},{24,16},{1,9},{9,1},{17,25},{25,17},{2,10},{10... | collective-permute-start | bytes 786440 | tf_op jit(solution)/shard_map/ppermute | solution.py:635
  123.9 9.5 %collective-permute-start.33 = (bf16[8,64,512]{2,1,0:T(8,128)(2,1)S(1)}, bf16[8,64,512]{2,1,0:T(8,128)(2,1)S(1)}, u32[]{:S(2)}, u32[]{:S(2)}) collective-permute-start(bf16[8,64,512]{2,1,0:T(8,128)(2,1)S(1)} %get-tuple-element.305.refs_1_), channel_id=1, source_target_pairs={{0,8},{8,0},{16,24},{24,16},{1,9},{9,1},{17,25},{25,17},{2,10},{10... | collective-permute-start | bytes 1572872 | tf_op jit(solution)/shard_map/ppermute | solution.py:635
  124.3 9.2 %collective-permute-start.34 = (bf16[8,64,512]{2,1,0:T(8,128)(2,1)S(1)}, bf16[8,64,512]{2,1,0:T(8,128)(2,1)S(1)}, u32[]{:S(2)}, u32[]{:S(2)}) collective-permute-start(bf16[8,64,512]{2,1,0:T(8,128)(2,1)S(1)} %get-tuple-element.306.refs_3_), channel_id=1, source_target_pairs={{0,16},{8,24},{16,0},{24,8},{1,17},{9,25},{17,1},{25,9},{2,18},{10... | collective-permute-start | bytes 1572872 | tf_op jit(solution)/shard_map/ppermute | solution.py:635
  125.7 10.1 %collective-permute-start.32 = (bf16[3,128,512]{2,1,0:T(8,128)(2,1)S(1)}, bf16[3,128,512]{2,1,0:T(8,128)(2,1)S(1)}, u32[]{:S(2)}, u32[]{:S(2)}) collective-permute-start(bf16[3,128,512]{2,1,0:T(8,128)(2,1)S(1)} %get-tuple-element.301.refs_10_), channel_id=1, source_target_pairs={{0,4},{1,5},{4,6},{5,7},{6,2},{7,3},{2,0},{3,1},{8,12},{9,13},{12,... | collective-permute-start | bytes 1179656 | tf_op jit(solution)/shard_map/ppermute | solution.py:925
  128.0 7.8 %collective-permute-start.31 = (bf16[2,80,512]{2,1,0:T(8,128)(2,1)S(1)}, bf16[2,80,512]{2,1,0:T(8,128)(2,1)S(1)}, u32[]{:S(2)}, u32[]{:S(2)}) collective-permute-start(bf16[2,80,512]{2,1,0:T(8,128)(2,1)S(1)} %get-tuple-element.297.refs_0_), channel_id=1, source_target_pairs={{0,2},{1,3},{2,0},{3,1},{4,6},{5,7},{6,4},{7,5},{8,10},{9,11},{10,... | collective-permute-start | bytes 491528 | tf_op jit(solution)/shard_map/ppermute | solution.py:635
  137.1 11.8 %collective-permute-start.37 = (bf16[3,128,512]{2,1,0:T(8,128)(2,1)S(1)}, bf16[3,128,512]{2,1,0:T(8,128)(2,1)S(1)}, u32[]{:S(2)}, u32[]{:S(2)}) collective-permute-start(bf16[3,128,512]{2,1,0:T(8,128)(2,1)S(1)} %get-tuple-element.310.refs_5_), channel_id=1, source_target_pairs={{0,4},{1,5},{4,6},{5,7},{6,2},{7,3},{2,0},{3,1},{8,12},{9,13},{12,... | collective-permute-start | bytes 1179656 | tf_op jit(solution)/shard_map/ppermute | solution.py:937
  139.1 6.3 %collective-permute-start.36 = (bf16[144,512]{1,0:T(8,128)(2,1)S(1)}, bf16[144,512]{1,0:T(8,128)(2,1)S(1)}, u32[]{:S(2)}, u32[]{:S(2)}) collective-permute-start(bf16[144,512]{1,0:T(8,128)(2,1)S(1)} %get-tuple-element.303.refs_2_), channel_id=1, source_target_pairs={{0,8},{8,0},{16,24},{24,16},{1,9},{9,1},{17,25},{25,17},{2,10},{10... | collective-permute-start | bytes 442376 | tf_op jit(solution)/shard_map/ppermute | solution.py:635
  150.3 8.6 %collective-permute-start.42 = (bf16[272,512]{1,0:T(8,128)(2,1)S(1)}, bf16[272,512]{1,0:T(8,128)(2,1)S(1)}, u32[]{:S(2)}, u32[]{:S(2)}) collective-permute-start(bf16[272,512]{1,0:T(8,128)(2,1)S(1)} %get-tuple-element.330.refs_5_), channel_id=1, source_target_pairs={{0,16},{8,24},{16,0},{24,8},{1,17},{9,25},{17,1},{25,9},{2,18},{10... | collective-permute-start | bytes 835592 | tf_op jit(solution)/shard_map/ppermute | solution.py:635
  150.6 8.0 %collective-permute-start.41 = (bf16[256,512]{1,0:T(8,128)(2,1)S(1)}, bf16[256,512]{1,0:T(8,128)(2,1)S(1)}, u32[]{:S(2)}, u32[]{:S(2)}) collective-permute-start(bf16[256,512]{1,0:T(8,128)(2,1)S(1)} %get-tuple-element.328.refs_1_), channel_id=1, source_target_pairs={{0,8},{8,0},{16,24},{24,16},{1,9},{9,1},{17,25},{25,17},{2,10},{10... | collective-permute-start | bytes 786440 | tf_op jit(solution)/shard_map/ppermute | solution.py:635
  152.0 11.4 %collective-permute-start.40 = (bf16[3,128,512]{2,1,0:T(8,128)(2,1)S(1)}, bf16[3,128,512]{2,1,0:T(8,128)(2,1)S(1)}, u32[]{:S(2)}, u32[]{:S(2)}) collective-permute-start(bf16[3,128,512]{2,1,0:T(8,128)(2,1)S(1)} %get-tuple-element.324.refs_7_), channel_id=1, source_target_pairs={{0,4},{1,5},{4,6},{5,7},{6,2},{7,3},{2,0},{3,1},{8,12},{9,13},{12,... | collective-permute-start | bytes 1179656 | tf_op jit(solution)/shard_map/ppermute | solution.py:951
  158.9 6.0 %collective-permute-start.48 = (bf16[272,512]{1,0:T(8,128)(2,1)S(1)}, bf16[272,512]{1,0:T(8,128)(2,1)S(1)}, u32[]{:S(2)}, u32[]{:S(2)}) collective-permute-start(bf16[272,512]{1,0:T(8,128)(2,1)S(1)} %collective-permute-done.42.refs_6_), channel_id=1, source_target_pairs={{0,1},{1,0},{2,3},{3,2},{4,5},{5,4},{6,7},{7,6},{8,9},{9,8},{10,11... | collective-permute-start | bytes 835592 | tf_op jit(solution)/shard_map/ppermute | solution.py:635
  158.9 6.0 %collective-permute-start.47 = (bf16[272,512]{1,0:T(8,128)(2,1)S(1)}, bf16[272,512]{1,0:T(8,128)(2,1)S(1)}, u32[]{:S(2)}, u32[]{:S(2)}) collective-permute-start(bf16[272,512]{1,0:T(8,128)(2,1)S(1)} %get-tuple-element.330.refs_5_), channel_id=1, source_target_pairs={{0,1},{1,0},{2,3},{3,2},{4,5},{5,4},{6,7},{7,6},{8,9},{9,8},{10,11... | collective-permute-start | bytes 835592 | tf_op jit(solution)/shard_map/ppermute | solution.py:635
  (31 other events, 162.2 us)
where the time goes:
time: 171 us; the launch traced here: 168 us
  waiting for transfers between devices  56.6 us (33%)
  Pallas kernels  54.5 us (32%)
  starting transfers between devices  49.6 us (29%)
  local copies, waits for them, and re-layouts  4.48 us (3%)
    pallas_call x24, Pallas kernels, call(): pl.pallas_call(body_of, grid=grid, in_specs=[SMEM] * scalars + (specs or...  54.5 us
    ppermute x46, waiting for transfers between devices, exchange(): return lax.ppermute(array, axis, [(i, i ^ mask) for i in range(count)])  49.5 us
    ppermute x46, starting transfers between devices, exchange(): return lax.ppermute(array, axis, [(i, i ^ mask) for i in range(count)])  42 us
    ppermute x3, starting transfers between devices, body(): moving = lax.ppermute(moving, 'seq', ring)  7.61 us
    ppermute x3, waiting for transfers between devices, body(): moving = lax.ppermute(moving, 'seq', ring)  7.12 us
  transfers between devices with their start and end apart: 49, of which 24 were waited for; matrix products, arithmetic and copies ran while one was open for 2% of the time, Pallas kernels for 23%

commit v1 on v0

--- a/solution.py
+++ b/solution.py
@@ -54,14 +54,6 @@
     for j in range(count):
         seg += (pos >= offsets[row, j]).astype(jnp.int32)
     return seg + count * (pos >= crop[row]).astype(jnp.int32)
-
-
-def ring_station(place, count):
-    return jnp.where(place < count // 2, 2 * place, 2 * (count - 1 - place) + 1)
-
-
-def ring_place(station, count):
-    return jnp.where(station % 2 == 0, station // 2, count - 1 - station // 2)
 
 
 def positions(sp, chunk, tok, shape, dim):
@@ -254,20 +246,24 @@
     vec[7:8, :] = jnp.sum(low.astype(F32), axis=0, keepdims=True)
 
 
-def ffn_grad_kernel(sp, hid_m, pre_m, n_m, got, g_m, g_o, d_keep, d_send, u_keep, u_send, gd, gu):
+def ffn_grad_kernel(sp, hid_m, pre_m, n_m, got, g_m, g_o, d_keep, d_send, u_keep, u_send):
     half = hid_m.shape[1]
-    gd[...] = tn(hid_m[...], g_m[...]) + tn(got[:, :half], g_o[...])
-    gu[...] = tn(n_m[...], pre_m[...]) + tn(got[:, 2 * half :], got[:, half : 2 * half])
-    rd = gd.shape[0] // PIECES
-    ru = gu.shape[0] // PIECES
-    width = gd.shape[1]
-    for slot in range(PIECES):
-        d, u = (d_keep, u_keep) if slot < PIECES // 2 else (d_send, u_send)
-        at = slot % (PIECES // 2)
-        d[at] = gd[pl.ds(pl.multiple_of((sp[2] ^ slot) * rd, rd), rd), :].astype(BF16)
-        rows = pl.ds(pl.multiple_of((sp[3] ^ slot) * ru, ru), ru)
-        for i in range(half // width):
-            u[at, i * ru : (i + 1) * ru, :] = gu[rows, i * width : (i + 1) * width].astype(BF16)
+    width = g_m.shape[1]
+    per = PIECES // 2
+    rd, ru = half // PIECES, width // PIECES
+    for send, d, u in ((1, d_send, u_send), (0, d_keep, u_keep)):
+        part = (sp[2] // per) ^ send
+        cols = half_of(part, half // 2)
+        gd = tn(hid_m[:, cols], g_m[...]) + tn(got[:, cols], g_o[...])
+        part = (sp[3] // per) ^ send
+        own = half_of(part, width // 2)
+        others = pl.ds(pl.multiple_of(2 * half + part * (width // 2), 128), width // 2)
+        gu = tn(n_m[:, own], pre_m[...]) + tn(got[:, others], got[:, half : 2 * half])
+        for p in range(per):
+            d[(sp[2] & (per - 1)) ^ p] = gd[p * rd : (p + 1) * rd].astype(BF16)
+            at = (sp[3] & (per - 1)) ^ p
+            for i in range(half // width):
+                u[at, i * ru : (i + 1) * ru, :] = gu[p * ru : (p + 1) * ru, i * width : (i + 1) * width].astype(BF16)
 
 
 def attend_back_kernel(stations, tok, row, whole, last, *refs):
@@ -283,7 +279,9 @@
     sums_in = take(5) if row else None
     if last:
         vectors, vec_in = take(2)
+        before = take(row)
     dn_m, dn_o = take(2)
+    base = row * stations if last else 0
     if last:
         ones, twos = take(2), take(2)
     gq, gk, gv, go, sums = take(5)
@@ -354,7 +352,7 @@
             if b + i == 0:
                 part += nt(dq, weights[0])
             dn_m[b * block + i] = part[:tok].astype(BF16)
-            dn_o[b * block + i] = part[tok:].astype(BF16)
+            dn_o[base + b * block + i] = part[tok:].astype(BF16)
     sum_q = jnp.sum(dq.astype(F32), axis=0, keepdims=True)
     made_here = (gq_row, gk_row, gv_row, go_row, jnp.concatenate([sum_q, sum_v, sum_k, jnp.zeros((5, half), F32)]))
     for i, (ref, value) in enumerate(zip((gq, gk, gv, go, sums), made_here)):
@@ -362,6 +360,8 @@
     if not last:
         return
 
+    for r, part in enumerate(before):
+        dn_o[r * stations : (r + 1) * stations] = part[...]
     vec = refs[0]
     lane = lax.broadcasted_iota(jnp.int32, (2, width), 1)
     both = sums[0:2, :]
@@ -409,7 +409,12 @@
     rows, tok, width = tokens.shape
     flat = rows * tok
     unit, scale = normalize(tokens[...].reshape(flat, width).astype(F32))
-    parts = [refs[2 * r][0].astype(F32) + refs[2 * r + 1][0].astype(F32) + refs[-2][r].astype(F32) for r in range(rows)]
+    parts = []
+    for r in range(rows):
+        part = refs[r][0].astype(F32) + refs[rows][r * refs[0].shape[0]].astype(F32)
+        for arrived in refs[rows + 1 : -1]:
+            part += arrived[r].astype(F32)
+        parts.append(part)
     grad = mid_grad[...] + norm_back(jnp.concatenate(parts, axis=0), unit, scale, gain[0:1, :])
     out[...] = grad.astype(BF16).reshape(rows, tok, width)
 
@@ -581,15 +586,11 @@
     two[2 * n :] = fill(lines)
 
 
-def norm_grad_kernel(step, stations, rows, sp, *refs):
+def norm_grad_kernel(chunk, rows, *refs):
     out = refs[-1]
-    place = lax.rem(ring_place(sp[4], stations) + stations - step, stations)
-    chunk = sp[4] ^ ring_station(place, stations)
+    stations = refs[0].shape[0]
     for r in range(rows):
-        values = [refs[2 * r][chunk], refs[2 * r + 1][chunk]]
-        if step > 1:
-            values.append(refs[2 * rows][r])
-        out[r] = total(*values)
+        out[r] = total(refs[r][chunk], refs[rows][r * stations + chunk], *[a[r] for a in refs[rows + 1 : -1]])
 
 
 VMEM = pl.BlockSpec(memory_space=pltpu.VMEM)
@@ -682,12 +683,6 @@
     seq = lax.axis_index("seq")
     core, station = seq % 2, seq // 2
     line = lambda v: v.reshape(1, -1)
-
-    order = list(range(0, stations, 2)) + list(range(1, stations, 2))[::-1]
-    ring = []
-    for i, s in enumerate(order):
-        after = order[(i + 1) % stations]
-        ring += [(2 * s + c, 2 * after + c) for c in range(2)]
 
     dp_bits = [("dp", 1 << i) for i in range(dp_count.bit_length() - 1)]
     st_bits = [("seq", 2 << i) for i in range(stations.bit_length() - 1)]
@@ -774,9 +769,9 @@
     d_keep, d_send, u_keep, u_send = call(
         ffn_grad_kernel, [sp, hid_m, pre_m, normed_two, got, g_v.reshape(flat, width), g_other],
         [piece, piece, piece, piece],
-        scratch=[pltpu.VMEM((hidden // 2, width), F32), pltpu.VMEM((width, hidden // 2), F32)],
         us=3.0, limit=LIMITS[2], name="feed_forward_grad",
     )
+    d_send, u_send, branch_r = tied(d_send, u_send, branch_r)
     chain = Chain(u_keep)
 
     q = PIECES // GROUP
@@ -798,10 +793,9 @@
         res = iter(chain(functools.partial(merge, kernel), ins, outs, name))
         return [[next(res) for _ in shapes] for _, _, shapes in jobs]
 
-    def norm_job(chunk, before):
-        pairs = [a for both in zip(dn_m, dn_r) for a in both]
-        kernel = functools.partial(norm_grad_kernel, chunk, stations, rows)
-        return (kernel, [sp] + pairs + before, [made((rows, tok, width), BF16)])
+    def norm_job(chunk, arrived):
+        ins = [*dn_m, dn_r, *arrived]
+        return (functools.partial(norm_grad_kernel, chunk, rows), ins, [made((rows, tok, width), BF16)])
 
     for r in range(rows):
         last = r == rows - 1
@@ -814,13 +808,13 @@
                     specs[i] = pl.BlockSpec(block_shape, functools.partial(lambda r, i: (r, 0, 0), r))
         tail = list(sums)
         if last:
-            tail += [vectors, vec_ffn]
+            tail += [vectors, vec_ffn, *dn_o]
         part = made((stations, tok, width), BF16)
         grads = [made((width, half), F32)] * 3 + [made((half, width), F32), made((8, half), F32)]
         outs = [part, part] + grads
         scratch = []
         if last:
-            outs = [part, part] + [made((width // 2, width), BF16)] * 2 + [made((width // 2 + 16, width), BF16)] * 2
+            outs = [part, made((rows * stations, tok, width), BF16)] + [made((width // 2, width), BF16)] * 2 + [made((width // 2 + 16, width), BF16)] * 2
             scratch = [pltpu.VMEM(g.shape, F32) for g in grads] + [pltpu.VMEM((16, width), F32)]
         run = functools.partial(call, functools.partial(attend_back_kernel, stations, tok, r, small, last))
         res = chain(
@@ -837,7 +831,6 @@
                 "add_quarters", (upper_kernel, [d_keep, d_got, u_keep, u_got], [quarters, quarters])
             )
             d_got2, u_got2 = exchange(d_next, *bit_y), exchange(u_next, *bit_x)
-            dn_r += [exchange(a, "seq", 1) for a in chain.hold(*dn_o)]
     one_keep, one_send, two_keep, two_send = res[2:]
 
     rd = hidden // 2 // PIECES
@@ -870,14 +863,13 @@
         return [exchange(a, "seq", 1) for a in arrays]
 
     two_a, two_b = two_of(ff_part), two_of(at_part)
-    dn_r = chain.hold(*dn_r)
     ((a_keep, a_send),) = together(
         "phase_1", (quarter_kernel, [d_keep, d_got, d_got2, u_keep, u_got, u_got2], [two_a, two_a])
     )
-    one_send, two_send, dn_last = chain.hold(one_send, two_send, dn_o[-1])
+    one_send, two_send, dn_o = chain.hold(one_send, two_send, dn_o[-1])
     a_got = exchange(a_send, *bit_z)
     one_got, two_got = exchange(one_send, *bit_x), exchange(two_send, *bit_y)
-    dn_r += chain.hold(*other_core(dn_last))
+    (dn_r,) = chain.hold(*other_core(dn_o))
 
     one_shape, two_shape = made((4 * n, width), BF16), made((4 * n + 16, width), BF16)
     (a_keep, a_send), (one_next, two_next) = together(
@@ -905,58 +897,61 @@
     a_far = exchange(a_pair, *bit_z)
     b_got = exchange(b_send, *bit_w)
 
-    (d_mine, u_mine), (b_own,) = together(
+    arrived = {c: [] for c in range(stations)}
+    top = stations // 2
+    inner = [c for c in reversed(turns) if c not in (0, 1, top)]
+    for c in inner[:-1]:
+        ((moving,),) = together("norm_step", norm_job(c, arrived[c]))
+        arrived[c & (c - 1)].append(exchange(moving, "seq", 2 * (c & -c)))
+    c = inner[-1]
+    (d_mine, u_mine), (b_own,), (moving,) = together(
         "phase_5",
         (divide_kernel, [a_pair, a_far], [quarters, quarters]),
         (sum_kernel, [b_keep, b_got], [at_part]),
+        norm_job(c, arrived[c]),
     )
     b_own = over_rest(b_own)
     d_y, u_x = exchange(d_mine, *bit_y), exchange(u_mine, *bit_x)
     b_near = exchange(b_own, *bit_w)
+    (moving,) = chain.hold(exchange(moving, "seq", 2 * (c & -c)))
+    arrived[c & (c - 1)].append(moving)
 
     (d_near, u_near), (b_pair,), (moving,) = together(
         "phase_6",
         (join_kernel, [d_mine, d_y, u_mine, u_x], [piece, piece]),
         (pair_kernel, [b_own, b_near], [two_b]),
-        norm_job(1, []),
+        norm_job(top, arrived[top]),
     )
     d_far, u_far = exchange(d_near, *bit_x), exchange(u_near, *bit_y)
     b_far = exchange(b_pair, *bit_z)
-    moving = lax.ppermute(moving, "seq", ring)
-    for chunk in range(2, stations - 2):
-        ((moving,),) = together("norm_step", norm_job(chunk, [moving]))
-        moving = lax.ppermute(moving, "seq", ring)
+    moving = exchange(moving, "seq", 2 * top)
     d_far, u_far = chain.hold(d_far, u_far)
 
-    (one_mine, two_mine), (moving,) = together(
-        "phase_7",
-        (attend_divide_kernel, [b_pair, b_far], [one_shape, two_shape]),
-        norm_job(stations - 2, [moving]),
+    (one_mine, two_mine), (nearest,) = together(
+        "phase_7", (attend_divide_kernel, [b_pair, b_far], [one_shape, two_shape]), norm_job(1, [])
     )
     one_y, two_x = exchange(one_mine, *bit_y), exchange(two_mine, *bit_x)
-    moving = lax.ppermute(moving, "seq", ring)
-    d_near, u_near = chain.hold(d_near, u_near)
-    d_near_o, u_near_o = chain.hold(*other_core(d_near, u_near))
-    grad_down, grad_up = unpack(False, d_near, d_near_o, u_near, u_near_o, [])
-
-    (one_near, two_near), (moving,) = together(
+    nearest = exchange(chain.hold(nearest)[0], "seq", 2)
+    (moving,) = chain.hold(moving)
+    ((one_near, two_near),) = together(
         "phase_8",
         (
             attend_join_kernel, [one_mine, one_y, two_mine, two_x],
             [made((8 * n, width), BF16), made((8 * n + 16, width), BF16)],
         ),
-        norm_job(stations - 1, [moving]),
     )
     one_far, two_far = exchange(one_near, *bit_x), exchange(two_near, *bit_y)
-    moving = lax.ppermute(moving, "seq", ring)
-    d_far, u_far = chain.hold(d_far, u_far)
+    d_near, u_near = chain.hold(d_near, u_near)
+    d_near_o, u_near_o = chain.hold(*other_core(d_near, u_near))
+    grad_down, grad_up = unpack(False, d_near, d_near_o, u_near, u_near_o, [])
     d_far_o, u_far_o = chain.hold(*other_core(d_far, u_far))
     grad_down, grad_up = unpack(True, d_far, d_far_o, u_far, u_far_o, [grad_down, grad_up])
+    far_held = chain.hold(one_far, two_far, nearest)
+    nearest = far_held[2]
     one_near_o, two_near_o = other_core(*chain.hold(one_near, two_near))
-    one_far_o, two_far_o = other_core(*chain.hold(one_far, two_far))
-    pairs = [a for both in zip(dn_m, dn_r) for a in both]
+    one_far_o, two_far_o = other_core(*far_held[:2])
     input_grad = call(
-        last_kernel, [tokens_v, vectors, mid_grad] + pairs + [moving], [token_block],
+        last_kernel, [tokens_v, vectors, mid_grad, *dn_m, dn_r, *arrived[0], moving, nearest], [token_block],
         us=0.1, limit=LIMITS[4], name="input_grad", scalars=0, extra=[chain.token],
     )[0]
     one_all = [one_near, one_far, one_near_o, one_far_o]

time: 171 us -> 165 us (0.965)
  waiting for transfers between devices: 56.6 us -> 53.4 us
  Pallas kernels: 54.5 us -> 52.2 us
    ppermute x3 -> x0, starting transfers between devices: 7.61 us -> none  [body(): moving = lax.ppermute(moving, 'seq', ring)]
    ppermute x3 -> x0, waiting for transfers between devices: 7.12 us -> none  [body(): moving = lax.ppermute(moving, 'seq', ring)]
    ppermute x46 -> x47, starting transfers between devices: 42 us -> 49.1 us  [exchange(): return lax.ppermute(array, axis, [(i, i ^ mask) for i in range(count)])]
    ppermute x46 -> x47, waiting for transfers between devices: 49.5 us -> 53.4 us  [exchange(): return lax.ppermute(array, axis, [(i, i ^ mask) for i in range(count)])]
    pallas_call x24, Pallas kernels: 54.5 us -> 52.2 us  [call(): pl.pallas_call(body_of, grid=grid, in_specs=[SMEM] * scalars + (specs or...]
  transfers between devices with their start and end apart: 49 -> 47, of which waited for: 24 -> 22; matrix products, arithmetic and copies ran while one was open for 2% -> 3% of each run, Pallas kernels for 23% -> 26%
where the time goes in v1:
time: 165 us; the launch traced here: 162 us
  waiting for transfers between devices  53.4 us (32%)
  Pallas kernels  52.2 us (32%)
  starting transfers between devices  49.1 us (30%)
  local copies, waits for them, and re-layouts  4.48 us (3%)
    ppermute x47, waiting for transfers between devices, exchange(): return lax.ppermute(array, axis, [(i, i ^ mask) for i in range(count)])  53.4 us
    pallas_call x24, Pallas kernels, call(): pl.pallas_call(body_of, grid=grid, in_specs=[SMEM] * scalars + (specs or...  52.2 us
    ppermute x47, starting transfers between devices, exchange(): return lax.ppermute(array, axis, [(i, i ^ mask) for i in range(count)])  49.1 us
  transfers between devices with their start and end apart: 47, of which 22 were waited for; matrix products, arithmetic and copies ran while one was open for 3% of the time, Pallas kernels for 26%

profile of v1, /device:TPU:0, one launch (start us, length us, event | category | flops | bytes accessed | tf_op | source)
XLA Modules:
  0.0 162.1 jit_solution(8298091577438283372)
XLA Ops:
  1.2 3.7 %collective-permute-start = (bf16[3,128,512]{2,1,0:T(8,128)(2,1)}, bf16[3,128,512]{2,1,0:T(8,128)(2,1)S(1)}, u32[]{:S(2)}, u32[]{:S(2)}) collective-permute-start(bf16[3,128,512]{2,1,0:T(8,128)(2,1)} %refs_1_.9), channel_id=1, source_target_pairs={{0,4},{1,5},{2,6},{3,7},{4,0},{5,1},{6,2},{7,3},{8,12},{9,13},{10,... | collective-permute-start | bytes 1179656 | tf_op jit(solution)/shard_map/ppermute | solution.py:636
  10.7 3.5 %attend_chunk_0.1 = (bf16[3,256,256]{2,1,0:T(8,128)(2,1)S(1)}, bf16[3,256,256]{2,1,0:T(8,128)(2,1)S(1)}, bf16[3,256,256]{2,1,0:T(8,128)(2,1)S(1)}, bf16[3,512,25...) custom-call(s32[5]{0:T(128)S(1)} %stack.53.refs_0_, ...), custom_call_target="tpu_custom_call" | custom-call | flops 55000000 | tf_op jit(solution)/shard_map/attend_chunk_0/pallas_call | solution.py:608
  17.5 5.8 %collective-permute-done.refs_3_ = bf16[3,128,512]{2,1,0:T(8,128)(2,1)S(1)} collective-permute-done((bf16[3,128,512]{2,1,0:T(8,128)(2,1)}, bf16[3,128,512]{2,1,0:T(8,128)(2,1)S(1)}, u32[]{:S(2)}, u32[]{:S(2)}) %collective-permute-start) | collective-permute-done | bytes 393248 | tf_op jit(solution)/shard_map/ppermute | solution.py:636
  25.1 3.3 %attend_chunk_2.1 = (bf16[3,256,256]{2,1,0:T(8,128)(2,1)S(1)}, bf16[3,256,256]{2,1,0:T(8,128)(2,1)S(1)}, bf16[3,256,256]{2,1,0:T(8,128)(2,1)S(1)}, bf16[3,512,25...) custom-call(s32[5]{0:T(128)S(1)} %stack.53.refs_0_, ...), custom_call_target="tpu_custom_call" | custom-call | flops 55000000 | tf_op jit(solution)/shard_map/attend_chunk_2/pallas_call | solution.py:608
  28.4 3.3 %attend_chunk_1.1 = (bf16[3,256,256]{2,1,0:T(8,128)(2,1)S(1)}, bf16[3,256,256]{2,1,0:T(8,128)(2,1)S(1)}, bf16[3,256,256]{2,1,0:T(8,128)(2,1)S(1)}, bf16[3,512,25...) custom-call(s32[5]{0:T(128)S(1)} %stack.53.refs_0_, ...), custom_call_target="tpu_custom_call" | custom-call | flops 55000000 | tf_op jit(solution)/shard_map/attend_chunk_1/pallas_call | solution.py:608
  31.8 3.6 %collective-permute-done.2.refs_3_ = bf16[3,128,512]{2,1,0:T(8,128)(2,1)S(1)} collective-permute-done((bf16[3,128,512]{2,1,0:T(8,128)(2,1)S(1)}, bf16[3,128,512]{2,1,0:T(8,128)(2,1)S(1)}, u32[]{:S(2)}, u32[]{:S(2)}) %collective-permute-start.2) | collective-permute-done | bytes 393248 | tf_op jit(solution)/shard_map/ppermute | solution.py:636
  37.1 3.4 %attend_chunk_3.1 = (bf16[3,256,256]{2,1,0:T(8,128)(2,1)S(1)}, bf16[3,256,256]{2,1,0:T(8,128)(2,1)S(1)}, bf16[3,256,256]{2,1,0:T(8,128)(2,1)S(1)}, bf16[3,512,25...) custom-call(s32[5]{0:T(128)S(1)} %stack.53.refs_0_, ...), custom_call_target="tpu_custom_call" | custom-call | flops 55000000 | tf_op jit(solution)/shard_map/attend_chunk_3/pallas_call | solution.py:608
  42.0 3.4 %feed_forward_a.1 = (f32[384,512]{1,0:T(8,128)S(1)}, bf16[384,512]{1,0:T(8,128)(2,1)S(1)}, bf16[384,2560]{1,0:T(8,128)(2,1)S(1)}, f32[384,512]{1,0:T(8,128)S(1)}...) custom-call(s32[5]{0:T(128)S(1)} %stack.53.refs_0_, bf16[3,128,256]{2,1,0:T(8,128)(2,1)S(1)} %get-tuple-element.203.refs_1_, ...), custom_call_target="tpu_custom_call" | custom-call | flops 4400000000 | tf_op jit(solution)/shard_map/feed_forward_a/pallas_call | solution.py:608
  45.7 3.7 %feed_forward_b.1 = (bf16[3,128,512]{2,1,0:T(8,128)(2,1)}, bf16[384,1024]{1,0:T(8,128)(2,1)S(1)}, bf16[384,1024]{1,0:T(8,128)(2,1)S(1)}, f32[384,512]{1,0:T(8,12...) custom-call(s32[5]{0:T(128)S(1)} %stack.53.refs_0_, f32[384,512]{1,0:T(8,128)S(1)} %get-tuple-element.213.refs_1_, ...), custom_call_target="tpu_custom_call" | custom-call | flops 4400000000 | tf_op jit(solution)/shard_map/feed_forward_b/pallas_call | solution.py:608
  49.7 2.9 %feed_forward_grad.1 = (bf16[8,64,512]{2,1,0:T(8,128)(2,1)S(1)}, bf16[8,64,512]{2,1,0:T(8,128)(2,1)S(1)}, bf16[8,64,512]{2,1,0:T(8,128)(2,1)S(1)}, bf16[8,64,512]{2,1,0:T(8,128)(2,1)S(1)}) custom-call(s32[5]{0:T(128)S(1)} %stack.53.refs_0_, bf16[384,1024]{1,0:T(8,128)(2,1)S(1)} %get-tuple-element.222.refs_1_, ...), custom_call_target="tpu_custom_call" | custom-call | flops 3300000000 | tf_op jit(solution)/shard_map/feed_forward_grad/pallas_call | solution.py:608
  55.8 5.2 %attend_back_0.1 = (bf16[4,128,512]{2,1,0:T(8,128)(2,1)S(1)}, bf16[4,128,512]{2,1,0:T(8,128)(2,1)S(1)}, f32[512,256]{1,0:T(8,128)S(1)}, f32[512,256]{1,0:T(8,128...) custom-call(s32[5]{0:T(128)S(1)} %stack.53.refs_0_, s32[3,4]{1,0:T(4,128)S(1)} %copy-done.3, ...), custom_call_target="tpu_custom_call" | custom-call | flops 55000000 | tf_op jit(solution)/shard_map/attend_back_0/pallas_call | solution.py:608
  60.9 5.4 %attend_back_1.1 = (bf16[4,128,512]{2,1,0:T(8,128)(2,1)S(1)}, bf16[4,128,512]{2,1,0:T(8,128)(2,1)S(1)}, f32[512,256]{1,0:T(8,128)S(1)}, f32[512,256]{1,0:T(8,128...) custom-call(s32[5]{0:T(128)S(1)} %stack.53.refs_0_, s32[3,4]{1,0:T(4,128)S(1)} %copy-done.3, ...), custom_call_target="tpu_custom_call" | custom-call | flops 55000000 | tf_op jit(solution)/shard_map/attend_back_1/pallas_call | solution.py:608
  70.2 5.8 %attend_back_2.1 = (bf16[4,128,512]{2,1,0:T(8,128)(2,1)S(1)}, bf16[12,128,512]{2,1,0:T(8,128)(2,1)S(1)}, bf16[256,512]{1,0:T(8,128)(2,1)S(1)}, bf16[256,512]{1,0...) custom-call(s32[5]{0:T(128)S(1)} %stack.53.refs_0_, s32[3,4]{1,0:T(4,128)S(1)} %copy-done.3, ...), custom_call_target="tpu_custom_call" | custom-call | flops 55000000 | tf_op jit(solution)/shard_map/attend_back_2/pallas_call | solution.py:608
  80.3 5.6 %collective-permute-done.17.refs_3_ = bf16[256,512]{1,0:T(8,128)(2,1)S(1)} collective-permute-done((bf16[256,512]{1,0:T(8,128)(2,1)S(1)}, bf16[256,512]{1,0:T(8,128)(2,1)S(1)}, u32[]{:S(2)}, u32[]{:S(2)}) %collective-permute-start.17) | collective-permute-done | bytes 262176 | tf_op jit(solution)/shard_map/ppermute | solution.py:636
  87.8 2.2 %collective-permute-start.19 = (bf16[128,512]{1,0:T(8,128)(2,1)S(1)}, bf16[128,512]{1,0:T(8,128)(2,1)S(1)}, u32[]{:S(2)}, u32[]{:S(2)}) collective-permute-start(bf16[128,512]{1,0:T(8,128)(2,1)S(1)} %get-tuple-element.283), channel_id=1, source_target_pairs={{0,4},{1,5},{2,6},{3,7},{4,0},{5,1},{6,2},{7,3},{8,12},{9,13},{10,... | collective-permute-start | bytes 393224 | tf_op jit(solution)/shard_map/ppermute | solution.py:636
  91.5 4.1 %collective-permute-done.19.refs_1_ = bf16[128,512]{1,0:T(8,128)(2,1)S(1)} collective-permute-done((bf16[128,512]{1,0:T(8,128)(2,1)S(1)}, bf16[128,512]{1,0:T(8,128)(2,1)S(1)}, u32[]{:S(2)}, u32[]{:S(2)}) %collective-permute-start.19) | collective-permute-done | bytes 131104 | tf_op jit(solution)/shard_map/ppermute | solution.py:636
  96.9 2.6 %collective-permute-start.22 = (bf16[128,512]{1,0:T(8,128)(2,1)S(1)}, bf16[128,512]{1,0:T(8,128)(2,1)S(1)}, u32[]{:S(2)}, u32[]{:S(2)}) collective-permute-start(bf16[128,512]{1,0:T(8,128)(2,1)S(1)} %get-tuple-element.286.refs_0_), channel_id=1, source_target_pairs={{0,4},{1,5},{2,6},{3,7},{4,0},{5,1},{6,2},{7,3},{8,12},{9,13},{10,... | collective-permute-start | bytes 393224 | tf_op jit(solution)/shard_map/ppermute | solution.py:636
  99.6 4.5 %collective-permute-done.22.refs_1_ = bf16[128,512]{1,0:T(8,128)(2,1)S(1)} collective-permute-done((bf16[128,512]{1,0:T(8,128)(2,1)S(1)}, bf16[128,512]{1,0:T(8,128)(2,1)S(1)}, u32[]{:S(2)}, u32[]{:S(2)}) %collective-permute-start.22) | collective-permute-done | bytes 131104 | tf_op jit(solution)/shard_map/ppermute | solution.py:636
  104.1 2.0 %collective-permute-start.24 = (bf16[2,128,512]{2,1,0:T(8,128)(2,1)S(1)}, bf16[2,128,512]{2,1,0:T(8,128)(2,1)S(1)}, u32[]{:S(2)}, u32[]{:S(2)}) collective-permute-start(bf16[2,128,512]{2,1,0:T(8,128)(2,1)S(1)} %get-tuple-element.289.refs_0_), channel_id=1, source_target_pairs={{0,2},{1,3},{2,0},{3,1},{4,6},{5,7},{6,4},{7,5},{8,10},{9,11},{10,... | collective-permute-start | bytes 786440 | tf_op jit(solution)/shard_map/ppermute | solution.py:636
  106.0 2.0 %collective-permute-start.25 = (bf16[80,512]{1,0:T(8,128)(2,1)S(1)}, bf16[80,512]{1,0:T(8,128)(2,1)S(1)}, u32[]{:S(2)}, u32[]{:S(2)}) collective-permute-start(bf16[80,512]{1,0:T(8,128)(2,1)S(1)} %get-tuple-element.291.refs_8_), channel_id=1, source_target_pairs={{0,4},{1,5},{2,6},{3,7},{4,0},{5,1},{6,2},{7,3},{8,12},{9,13},{10,... | collective-permute-start | bytes 245768 | tf_op jit(solution)/shard_map/ppermute | solution.py:636
  108.0 4.2 %collective-permute-done.25.refs_3_ = bf16[80,512]{1,0:T(8,128)(2,1)S(1)} collective-permute-done((bf16[80,512]{1,0:T(8,128)(2,1)S(1)}, bf16[80,512]{1,0:T(8,128)(2,1)S(1)}, u32[]{:S(2)}, u32[]{:S(2)}) %collective-permute-start.25) | collective-permute-done | bytes 81952 | tf_op jit(solution)/shard_map/ppermute | solution.py:636
  112.5 2.5 %collective-permute-start.29 = (bf16[3,128,512]{2,1,0:T(8,128)(2,1)S(1)}, bf16[3,128,512]{2,1,0:T(8,128)(2,1)S(1)}, u32[]{:S(2)}, u32[]{:S(2)}) collective-permute-start(bf16[3,128,512]{2,1,0:T(8,128)(2,1)S(1)} %get-tuple-element.297.refs_11_), channel_id=1, source_target_pairs={{0,2},{1,3},{2,0},{3,1},{4,6},{5,7},{6,4},{7,5},{8,10},{9,11},{10,... | collective-permute-start | bytes 1179656 | tf_op jit(solution)/shard_map/ppermute | solution.py:636
  118.8 4.8 %collective-permute-done.29.refs_10_ = bf16[3,128,512]{2,1,0:T(8,128)(2,1)S(1)} collective-permute-done((bf16[3,128,512]{2,1,0:T(8,128)(2,1)S(1)}, bf16[3,128,512]{2,1,0:T(8,128)(2,1)S(1)}, u32[]{:S(2)}, u32[]{:S(2)}) %collective-permute-start.29) | collective-permute-done | bytes 393248 | tf_op jit(solution)/shard_map/ppermute | solution.py:636
  126.5 2.6 %collective-permute-start.30 = (bf16[3,128,512]{2,1,0:T(8,128)(2,1)S(1)}, bf16[3,128,512]{2,1,0:T(8,128)(2,1)S(1)}, u32[]{:S(2)}, u32[]{:S(2)}) collective-permute-start(bf16[3,128,512]{2,1,0:T(8,128)(2,1)S(1)} %get-tuple-element.302.refs_6_), channel_id=1, source_target_pairs={{0,4},{1,5},{2,6},{3,7},{4,0},{5,1},{6,2},{7,3},{8,12},{9,13},{10,... | collective-permute-start | bytes 1179656 | tf_op jit(solution)/shard_map/ppermute | solution.py:636
  130.0 4.2 %collective-permute-done.32.refs_1_ = bf16[8,64,512]{2,1,0:T(8,128)(2,1)S(1)} collective-permute-done((bf16[8,64,512]{2,1,0:T(8,128)(2,1)S(1)}, bf16[8,64,512]{2,1,0:T(8,128)(2,1)S(1)}, u32[]{:S(2)}, u32[]{:S(2)}) %collective-permute-start.32) | collective-permute-done | bytes 524320 | tf_op jit(solution)/shard_map/ppermute | solution.py:636
  134.9 2.1 %collective-permute-done.31.refs_1_ = bf16[2,80,512]{2,1,0:T(8,128)(2,1)S(1)} collective-permute-done((bf16[2,80,512]{2,1,0:T(8,128)(2,1)S(1)}, bf16[2,80,512]{2,1,0:T(8,128)(2,1)S(1)}, u32[]{:S(2)}, u32[]{:S(2)}) %collective-permute-start.31) | collective-permute-done | bytes 163872 | tf_op jit(solution)/shard_map/ppermute | solution.py:636
  138.7 3.9 %collective-permute-done.30.refs_7_ = bf16[3,128,512]{2,1,0:T(8,128)(2,1)S(1)} collective-permute-done((bf16[3,128,512]{2,1,0:T(8,128)(2,1)S(1)}, bf16[3,128,512]{2,1,0:T(8,128)(2,1)S(1)}, u32[]{:S(2)}, u32[]{:S(2)}) %collective-permute-start.30) | collective-permute-done | bytes 393248 | tf_op jit(solution)/shard_map/ppermute | solution.py:636
  144.4 2.5 %collective-permute-start.38 = (bf16[3,128,512]{2,1,0:T(8,128)(2,1)S(1)}, bf16[3,128,512]{2,1,0:T(8,128)(2,1)S(1)}, u32[]{:S(2)}, u32[]{:S(2)}) collective-permute-start(bf16[3,128,512]{2,1,0:T(8,128)(2,1)S(1)} %get-tuple-element.311.refs_4_), channel_id=1, source_target_pairs={{0,2},{1,3},{2,0},{3,1},{4,6},{5,7},{6,4},{7,5},{8,10},{9,11},{10,... | collective-permute-start | bytes 1179656 | tf_op jit(solution)/shard_map/ppermute | solution.py:636
  148.7 2.7 %unpack_feed_forward.2 = (f32[2048,512]{1,0:T(8,128)}, f32[512,2048]{1,0:T(8,128)}, f32[8,128]{1,0:T(8,128)S(1)}) custom-call(s32[5]{0:T(128)S(1)} %stack.53.refs_0_, bf16[8,64,512]{2,1,0:T(8,128)(2,1)S(1)} %get-tuple-element.314.refs_1_, bf16[8,64,512]{2,1,0:T(8,128)(2,1)S(1)} %collective-permute-done.41.refs_2_, ...), custom_call_target="tpu_custom_call" | custom-call | flops 110000000 | tf_op jit(solution)/shard_map/unpack_feed_forward/pallas_call | solution.py:608
  151.4 2.7 %unpack_feed_forward.3 = (f32[2048,512]{1,0:T(8,128)}, f32[512,2048]{1,0:T(8,128)}, f32[8,128]{1,0:T(8,128)S(1)}) custom-call(s32[5]{0:T(128)S(1)} %stack.53.refs_0_, bf16[8,64,512]{2,1,0:T(8,128)(2,1)S(1)} %collective-permute-done.32.refs_1_, bf16[8,64,512]{2,1,0:T(8,128)(2,1)S(1)} %collective-permute-done.39.refs_2_, ...), custom_call_target="tpu_custom_call", output_to_operand_aliasing={{0}: (5, {}), {1}: (6, {})} | custom-call | flops 110000000 | tf_op jit(solution)/shard_map/unpack_feed_forward/pallas_call | solution.py:608
  154.1 2.2 %collective-permute-done.38.refs_8_ = bf16[3,128,512]{2,1,0:T(8,128)(2,1)S(1)} collective-permute-done((bf16[3,128,512]{2,1,0:T(8,128)(2,1)S(1)}, bf16[3,128,512]{2,1,0:T(8,128)(2,1)S(1)}, u32[]{:S(2)}, u32[]{:S(2)}) %collective-permute-start.38) | collective-permute-done | bytes 393248 | tf_op jit(solution)/shard_map/ppermute | solution.py:636
  159.0 2.7 %unpack_attend.1 = (f32[512,512]{1,0:T(8,128)}, f32[512,512]{1,0:T(8,128)}, f32[512,512]{1,0:T(8,128)}, f32[512,512]{1,0:T(8,128)}, f32[1,512]{1,0:T(1,128)}, /*...) custom-call(s32[5]{0:T(128)S(1)} %stack.53.refs_0_, ...), custom_call_target="tpu_custom_call" | custom-call | flops 110000000 | tf_op jit(solution)/shard_map/unpack_attend/pallas_call | solution.py:608
  (120 shorter events, 47.5 us)
Async XLA Ops:
  0.7 10.0 %collective-permute-start.1 = (bf16[3,128,512]{2,1,0:T(8,128)(2,1)}, bf16[3,128,512]{2,1,0:T(8,128)(2,1)S(1)}, u32[]{:S(2)}, u32[]{:S(2)}) collective-permute-start(bf16[3,128,512]{2,1,0:T(8,128)(2,1)} %refs_1_.9), channel_id=1, source_target_pairs={{0,1},{1,0},{2,3},{3,2},{4,5},{5,4},{6,7},{7,6},{8,9},{9,8},{10,11... | collective-permute-start | bytes 1179656 | tf_op jit(solution)/shard_map/ppermute | solution.py:636
  1.2 22.1 %collective-permute-start = (bf16[3,128,512]{2,1,0:T(8,128)(2,1)}, bf16[3,128,512]{2,1,0:T(8,128)(2,1)S(1)}, u32[]{:S(2)}, u32[]{:S(2)}) collective-permute-start(bf16[3,128,512]{2,1,0:T(8,128)(2,1)} %refs_1_.9), channel_id=1, source_target_pairs={{0,4},{1,5},{2,6},{3,7},{4,0},{5,1},{6,2},{7,3},{8,12},{9,13},{10,... | collective-permute-start | bytes 1179656 | tf_op jit(solution)/shard_map/ppermute | solution.py:636
  4.9 19.0 %collective-permute-start.3 = (bf16[3,128,512]{2,1,0:T(8,128)(2,1)}, bf16[3,128,512]{2,1,0:T(8,128)(2,1)S(1)}, u32[]{:S(2)}, u32[]{:S(2)}) collective-permute-start(bf16[3,128,512]{2,1,0:T(8,128)(2,1)} %refs_1_.9), channel_id=1, source_target_pairs={{0,2},{1,3},{2,0},{3,1},{4,6},{5,7},{6,4},{7,5},{8,10},{9,11},{10,... | collective-permute-start | bytes 1179656 | tf_op jit(solution)/shard_map/ppermute | solution.py:636
  23.9 11.5 %collective-permute-start.2 = (bf16[3,128,512]{2,1,0:T(8,128)(2,1)S(1)}, bf16[3,128,512]{2,1,0:T(8,128)(2,1)S(1)}, u32[]{:S(2)}, u32[]{:S(2)}) collective-permute-start(bf16[3,128,512]{2,1,0:T(8,128)(2,1)S(1)} %collective-permute-done.refs_3_), channel_id=1, source_target_pairs={{0,2},{1,3},{2,0},{3,1},{4,6},{5,7},{6,4},{7,5},{8,10},{9,11},{10,... | collective-permute-start | bytes 1179656 | tf_op jit(solution)/shard_map/ppermute | solution.py:636
  52.6 14.1 %collective-permute-start.11 = (bf16[8,64,512]{2,1,0:T(8,128)(2,1)S(1)}, bf16[8,64,512]{2,1,0:T(8,128)(2,1)S(1)}, u32[]{:S(2)}, u32[]{:S(2)}) collective-permute-start(bf16[8,64,512]{2,1,0:T(8,128)(2,1)S(1)} %get-tuple-element.264), channel_id=1, source_target_pairs={{0,8},{8,0},{16,24},{24,16},{1,9},{9,1},{17,25},{25,17},{2,10},{10... | collective-permute-start | bytes 1572872 | tf_op jit(solution)/shard_map/ppermute | solution.py:636
  54.2 13.7 %collective-permute-start.12 = (bf16[8,64,512]{2,1,0:T(8,128)(2,1)S(1)}, bf16[8,64,512]{2,1,0:T(8,128)(2,1)S(1)}, u32[]{:S(2)}, u32[]{:S(2)}) collective-permute-start(bf16[8,64,512]{2,1,0:T(8,128)(2,1)S(1)} %get-tuple-element.265), channel_id=1, source_target_pairs={{0,16},{8,24},{16,0},{24,8},{1,17},{9,25},{17,1},{25,9},{2,18},{10... | collective-permute-start | bytes 1572872 | tf_op jit(solution)/shard_map/ppermute | solution.py:636
  68.1 8.0 %collective-permute-start.13 = (bf16[4,64,512]{2,1,0:T(8,128)(2,1)S(1)}, bf16[4,64,512]{2,1,0:T(8,128)(2,1)S(1)}, u32[]{:S(2)}, u32[]{:S(2)}) collective-permute-start(bf16[4,64,512]{2,1,0:T(8,128)(2,1)S(1)} %get-tuple-element.271), channel_id=1, source_target_pairs={{0,16},{8,24},{16,0},{24,8},{1,17},{9,25},{17,1},{25,9},{2,18},{10... | collective-permute-start | bytes 786440 | tf_op jit(solution)/shard_map/ppermute | solution.py:636
  69.7 7.0 %collective-permute-start.14 = (bf16[4,64,512]{2,1,0:T(8,128)(2,1)S(1)}, bf16[4,64,512]{2,1,0:T(8,128)(2,1)S(1)}, u32[]{:S(2)}, u32[]{:S(2)}) collective-permute-start(bf16[4,64,512]{2,1,0:T(8,128)(2,1)S(1)} %get-tuple-element.266.refs_35_), channel_id=1, source_target_pairs={{0,8},{8,0},{16,24},{24,16},{1,9},{9,1},{17,25},{25,17},{2,10},{10... | collective-permute-start | bytes 786440 | tf_op jit(solution)/shard_map/ppermute | solution.py:636
  76.9 9.6 %collective-permute-start.18 = (bf16[272,512]{1,0:T(8,128)(2,1)S(1)}, bf16[272,512]{1,0:T(8,128)(2,1)S(1)}, u32[]{:S(2)}, u32[]{:S(2)}) collective-permute-start(bf16[272,512]{1,0:T(8,128)(2,1)S(1)} %get-tuple-element.280.refs_6_), channel_id=1, source_target_pairs={{0,16},{8,24},{16,0},{24,8},{1,17},{9,25},{17,1},{25,9},{2,18},{10... | collective-permute-start | bytes 835592 | tf_op jit(solution)/shard_map/ppermute | solution.py:636
  77.5 8.4 %collective-permute-start.17 = (bf16[256,512]{1,0:T(8,128)(2,1)S(1)}, bf16[256,512]{1,0:T(8,128)(2,1)S(1)}, u32[]{:S(2)}, u32[]{:S(2)}) collective-permute-start(bf16[256,512]{1,0:T(8,128)(2,1)S(1)} %get-tuple-element.278), channel_id=1, source_target_pairs={{0,8},{8,0},{16,24},{24,16},{1,9},{9,1},{17,25},{25,17},{2,10},{10... | collective-permute-start | bytes 786440 | tf_op jit(solution)/shard_map/ppermute | solution.py:636
  78.4 8.1 %collective-permute-start.16 = (bf16[2,128,512]{2,1,0:T(8,128)(2,1)S(1)}, bf16[2,128,512]{2,1,0:T(8,128)(2,1)S(1)}, u32[]{:S(2)}, u32[]{:S(2)}) collective-permute-start(bf16[2,128,512]{2,1,0:T(8,128)(2,1)S(1)} %get-tuple-element.281.refs_6_), channel_id=1, source_target_pairs={{0,2},{1,3},{2,0},{3,1},{4,6},{5,7},{6,4},{7,5},{8,10},{9,11},{10,... | collective-permute-start | bytes 786440 | tf_op jit(solution)/shard_map/ppermute | solution.py:636
  86.7 9.0 %collective-permute-start.21 = (bf16[144,512]{1,0:T(8,128)(2,1)S(1)}, bf16[144,512]{1,0:T(8,128)(2,1)S(1)}, u32[]{:S(2)}, u32[]{:S(2)}) collective-permute-start(bf16[144,512]{1,0:T(8,128)(2,1)S(1)} %get-tuple-element.285.refs_8_), channel_id=1, source_target_pairs={{0,8},{8,0},{16,24},{24,16},{1,9},{9,1},{17,25},{25,17},{2,10},{10... | collective-permute-start | bytes 442376 | tf_op jit(solution)/shard_map/ppermute | solution.py:636
  87.8 7.8 %collective-permute-start.19 = (bf16[128,512]{1,0:T(8,128)(2,1)S(1)}, bf16[128,512]{1,0:T(8,128)(2,1)S(1)}, u32[]{:S(2)}, u32[]{:S(2)}) collective-permute-start(bf16[128,512]{1,0:T(8,128)(2,1)S(1)} %get-tuple-element.283), channel_id=1, source_target_pairs={{0,4},{1,5},{2,6},{3,7},{4,0},{5,1},{6,2},{7,3},{8,12},{9,13},{10,... | collective-permute-start | bytes 393224 | tf_op jit(solution)/shard_map/ppermute | solution.py:636
  90.0 5.6 %collective-permute-start.20 = (bf16[128,512]{1,0:T(8,128)(2,1)S(1)}, bf16[128,512]{1,0:T(8,128)(2,1)S(1)}, u32[]{:S(2)}, u32[]{:S(2)}) collective-permute-start(bf16[128,512]{1,0:T(8,128)(2,1)S(1)} %get-tuple-element.284), channel_id=1, source_target_pairs={{0,16},{8,24},{16,0},{24,8},{1,17},{9,25},{17,1},{25,9},{2,18},{10... | collective-permute-start | bytes 393224 | tf_op jit(solution)/shard_map/ppermute | solution.py:636
  95.8 8.2 %collective-permute-start.23 = (bf16[2,80,512]{2,1,0:T(8,128)(2,1)S(1)}, bf16[2,80,512]{2,1,0:T(8,128)(2,1)S(1)}, u32[]{:S(2)}, u32[]{:S(2)}) collective-permute-start(bf16[2,80,512]{2,1,0:T(8,128)(2,1)S(1)} %get-tuple-element.288.refs_4_), channel_id=1, source_target_pairs={{0,2},{1,3},{2,0},{3,1},{4,6},{5,7},{6,4},{7,5},{8,10},{9,11},{10,... | collective-permute-start | bytes 491528 | tf_op jit(solution)/shard_map/ppermute | solution.py:636
  96.9 7.1 %collective-permute-start.22 = (bf16[128,512]{1,0:T(8,128)(2,1)S(1)}, bf16[128,512]{1,0:T(8,128)(2,1)S(1)}, u32[]{:S(2)}, u32[]{:S(2)}) collective-permute-start(bf16[128,512]{1,0:T(8,128)(2,1)S(1)} %get-tuple-element.286.refs_0_), channel_id=1, source_target_pairs={{0,4},{1,5},{2,6},{3,7},{4,0},{5,1},{6,2},{7,3},{8,12},{9,13},{10,... | collective-permute-start | bytes 393224 | tf_op jit(solution)/shard_map/ppermute | solution.py:636
  104.1 8.3 %collective-permute-start.24 = (bf16[2,128,512]{2,1,0:T(8,128)(2,1)S(1)}, bf16[2,128,512]{2,1,0:T(8,128)(2,1)S(1)}, u32[]{:S(2)}, u32[]{:S(2)}) collective-permute-start(bf16[2,128,512]{2,1,0:T(8,128)(2,1)S(1)} %get-tuple-element.289.refs_0_), channel_id=1, source_target_pairs={{0,2},{1,3},{2,0},{3,1},{4,6},{5,7},{6,4},{7,5},{8,10},{9,11},{10,... | collective-permute-start | bytes 786440 | tf_op jit(solution)/shard_map/ppermute | solution.py:636
  106.0 6.2 %collective-permute-start.25 = (bf16[80,512]{1,0:T(8,128)(2,1)S(1)}, bf16[80,512]{1,0:T(8,128)(2,1)S(1)}, u32[]{:S(2)}, u32[]{:S(2)}) collective-permute-start(bf16[80,512]{1,0:T(8,128)(2,1)S(1)} %get-tuple-element.291.refs_8_), channel_id=1, source_target_pairs={{0,4},{1,5},{2,6},{3,7},{4,0},{5,1},{6,2},{7,3},{8,12},{9,13},{10,... | collective-permute-start | bytes 245768 | tf_op jit(solution)/shard_map/ppermute | solution.py:636
  112.5 11.1 %collective-permute-start.29 = (bf16[3,128,512]{2,1,0:T(8,128)(2,1)S(1)}, bf16[3,128,512]{2,1,0:T(8,128)(2,1)S(1)}, u32[]{:S(2)}, u32[]{:S(2)}) collective-permute-start(bf16[3,128,512]{2,1,0:T(8,128)(2,1)S(1)} %get-tuple-element.297.refs_11_), channel_id=1, source_target_pairs={{0,2},{1,3},{2,0},{3,1},{4,6},{5,7},{6,4},{7,5},{8,10},{9,11},{10,... | collective-permute-start | bytes 1179656 | tf_op jit(solution)/shard_map/ppermute | solution.py:636
  115.0 8.6 %collective-permute-start.26 = (bf16[4,64,512]{2,1,0:T(8,128)(2,1)S(1)}, bf16[4,64,512]{2,1,0:T(8,128)(2,1)S(1)}, u32[]{:S(2)}, u32[]{:S(2)}) collective-permute-start(bf16[4,64,512]{2,1,0:T(8,128)(2,1)S(1)} %get-tuple-element.292.refs_0_), channel_id=1, source_target_pairs={{0,16},{8,24},{16,0},{24,8},{1,17},{9,25},{17,1},{25,9},{2,18},{10... | collective-permute-start | bytes 786440 | tf_op jit(solution)/shard_map/ppermute | solution.py:636
  116.6 7.0 %collective-permute-start.27 = (bf16[4,64,512]{2,1,0:T(8,128)(2,1)S(1)}, bf16[4,64,512]{2,1,0:T(8,128)(2,1)S(1)}, u32[]{:S(2)}, u32[]{:S(2)}) collective-permute-start(bf16[4,64,512]{2,1,0:T(8,128)(2,1)S(1)} %get-tuple-element.293.refs_2_), channel_id=1, source_target_pairs={{0,8},{8,0},{16,24},{24,16},{1,9},{9,1},{17,25},{25,17},{2,10},{10... | collective-permute-start | bytes 786440 | tf_op jit(solution)/shard_map/ppermute | solution.py:636
  117.5 6.1 %collective-permute-start.28 = (bf16[80,512]{1,0:T(8,128)(2,1)S(1)}, bf16[80,512]{1,0:T(8,128)(2,1)S(1)}, u32[]{:S(2)}, u32[]{:S(2)}) collective-permute-start(bf16[80,512]{1,0:T(8,128)(2,1)S(1)} %get-tuple-element.294.refs_4_), channel_id=1, source_target_pairs={{0,4},{1,5},{2,6},{3,7},{4,0},{5,1},{6,2},{7,3},{8,12},{9,13},{10,... | collective-permute-start | bytes 245768 | tf_op jit(solution)/shard_map/ppermute | solution.py:636
  123.9 10.3 %collective-permute-start.32 = (bf16[8,64,512]{2,1,0:T(8,128)(2,1)S(1)}, bf16[8,64,512]{2,1,0:T(8,128)(2,1)S(1)}, u32[]{:S(2)}, u32[]{:S(2)}) collective-permute-start(bf16[8,64,512]{2,1,0:T(8,128)(2,1)S(1)} %get-tuple-element.314.refs_1_), channel_id=1, source_target_pairs={{0,8},{8,0},{16,24},{24,16},{1,9},{9,1},{17,25},{25,17},{2,10},{10... | collective-permute-start | bytes 1572872 | tf_op jit(solution)/shard_map/ppermute | solution.py:636
  125.2 9.7 %collective-permute-start.33 = (bf16[8,64,512]{2,1,0:T(8,128)(2,1)S(1)}, bf16[8,64,512]{2,1,0:T(8,128)(2,1)S(1)}, u32[]{:S(2)}, u32[]{:S(2)}) collective-permute-start(bf16[8,64,512]{2,1,0:T(8,128)(2,1)S(1)} %get-tuple-element.315.refs_3_), channel_id=1, source_target_pairs={{0,16},{8,24},{16,0},{24,8},{1,17},{9,25},{17,1},{25,9},{2,18},{10... | collective-permute-start | bytes 1572872 | tf_op jit(solution)/shard_map/ppermute | solution.py:636
  126.5 16.1 %collective-permute-start.30 = (bf16[3,128,512]{2,1,0:T(8,128)(2,1)S(1)}, bf16[3,128,512]{2,1,0:T(8,128)(2,1)S(1)}, u32[]{:S(2)}, u32[]{:S(2)}) collective-permute-start(bf16[3,128,512]{2,1,0:T(8,128)(2,1)S(1)} %get-tuple-element.302.refs_6_), channel_id=1, source_target_pairs={{0,4},{1,5},{2,6},{3,7},{4,0},{5,1},{6,2},{7,3},{8,12},{9,13},{10,... | collective-permute-start | bytes 1179656 | tf_op jit(solution)/shard_map/ppermute | solution.py:636
  129.1 7.9 %collective-permute-start.31 = (bf16[2,80,512]{2,1,0:T(8,128)(2,1)S(1)}, bf16[2,80,512]{2,1,0:T(8,128)(2,1)S(1)}, u32[]{:S(2)}, u32[]{:S(2)}) collective-permute-start(bf16[2,80,512]{2,1,0:T(8,128)(2,1)S(1)} %get-tuple-element.299.refs_0_), channel_id=1, source_target_pairs={{0,2},{1,3},{2,0},{3,1},{4,6},{5,7},{6,4},{7,5},{8,10},{9,11},{10,... | collective-permute-start | bytes 491528 | tf_op jit(solution)/shard_map/ppermute | solution.py:636
  137.1 6.1 %collective-permute-start.35 = (bf16[144,512]{1,0:T(8,128)(2,1)S(1)}, bf16[144,512]{1,0:T(8,128)(2,1)S(1)}, u32[]{:S(2)}, u32[]{:S(2)}) collective-permute-start(bf16[144,512]{1,0:T(8,128)(2,1)S(1)} %get-tuple-element.307.refs_2_), channel_id=1, source_target_pairs={{0,8},{8,0},{16,24},{24,16},{1,9},{9,1},{17,25},{25,17},{2,10},{10... | collective-permute-start | bytes 442376 | tf_op jit(solution)/shard_map/ppermute | solution.py:636
  143.9 7.5 %collective-permute-start.39 = (bf16[8,64,512]{2,1,0:T(8,128)(2,1)S(1)}, bf16[8,64,512]{2,1,0:T(8,128)(2,1)S(1)}, u32[]{:S(2)}, u32[]{:S(2)}) collective-permute-start(bf16[8,64,512]{2,1,0:T(8,128)(2,1)S(1)} %collective-permute-done.32.refs_1_), channel_id=1, source_target_pairs={{0,1},{1,0},{2,3},{3,2},{4,5},{5,4},{6,7},{7,6},{8,9},{9,8},{10,11... | collective-permute-start | bytes 1572872 | tf_op jit(solution)/shard_map/ppermute | solution.py:636
  144.0 7.4 %collective-permute-start.40 = (bf16[8,64,512]{2,1,0:T(8,128)(2,1)S(1)}, bf16[8,64,512]{2,1,0:T(8,128)(2,1)S(1)}, u32[]{:S(2)}, u32[]{:S(2)}) collective-permute-start(bf16[8,64,512]{2,1,0:T(8,128)(2,1)S(1)} %collective-permute-done.33.refs_3_), channel_id=1, source_target_pairs={{0,1},{1,0},{2,3},{3,2},{4,5},{5,4},{6,7},{7,6},{8,9},{9,8},{10,11... | collective-permute-start | bytes 1572872 | tf_op jit(solution)/shard_map/ppermute | solution.py:636
  144.4 11.8 %collective-permute-start.38 = (bf16[3,128,512]{2,1,0:T(8,128)(2,1)S(1)}, bf16[3,128,512]{2,1,0:T(8,128)(2,1)S(1)}, u32[]{:S(2)}, u32[]{:S(2)}) collective-permute-start(bf16[3,128,512]{2,1,0:T(8,128)(2,1)S(1)} %get-tuple-element.311.refs_4_), channel_id=1, source_target_pairs={{0,2},{1,3},{2,0},{3,1},{4,6},{5,7},{6,4},{7,5},{8,10},{9,11},{10,... | collective-permute-start | bytes 1179656 | tf_op jit(solution)/shard_map/ppermute | solution.py:636
  146.9 9.4 %collective-permute-start.37 = (bf16[272,512]{1,0:T(8,128)(2,1)S(1)}, bf16[272,512]{1,0:T(8,128)(2,1)S(1)}, u32[]{:S(2)}, u32[]{:S(2)}) collective-permute-start(bf16[272,512]{1,0:T(8,128)(2,1)S(1)} %get-tuple-element.332.refs_5_), channel_id=1, source_target_pairs={{0,16},{8,24},{16,0},{24,8},{1,17},{9,25},{17,1},{25,9},{2,18},{10... | collective-permute-start | bytes 835592 | tf_op jit(solution)/shard_map/ppermute | solution.py:636
  147.3 8.9 %collective-permute-start.36 = (bf16[256,512]{1,0:T(8,128)(2,1)S(1)}, bf16[256,512]{1,0:T(8,128)(2,1)S(1)}, u32[]{:S(2)}, u32[]{:S(2)}) collective-permute-start(bf16[256,512]{1,0:T(8,128)(2,1)S(1)} %get-tuple-element.330.refs_1_), channel_id=1, source_target_pairs={{0,8},{8,0},{16,24},{24,16},{1,9},{9,1},{17,25},{25,17},{2,10},{10... | collective-permute-start | bytes 786440 | tf_op jit(solution)/shard_map/ppermute | solution.py:636
  (29 other events, 137.6 us)

commit v2 on v1

--- a/solution.py
+++ b/solution.py
@@ -246,27 +246,26 @@
     vec[7:8, :] = jnp.sum(low.astype(F32), axis=0, keepdims=True)
 
 
-def ffn_grad_kernel(sp, hid_m, pre_m, n_m, got, g_m, g_o, d_keep, d_send, u_keep, u_send):
+def ffn_grad_kernel(send, sp, hid_m, pre_m, n_m, got, g_m, g_o, d, u):
     half = hid_m.shape[1]
     width = g_m.shape[1]
     per = PIECES // 2
     rd, ru = half // PIECES, width // PIECES
-    for send, d, u in ((1, d_send, u_send), (0, d_keep, u_keep)):
-        part = (sp[2] // per) ^ send
-        cols = half_of(part, half // 2)
-        gd = tn(hid_m[:, cols], g_m[...]) + tn(got[:, cols], g_o[...])
-        part = (sp[3] // per) ^ send
-        own = half_of(part, width // 2)
-        others = pl.ds(pl.multiple_of(2 * half + part * (width // 2), 128), width // 2)
-        gu = tn(n_m[:, own], pre_m[...]) + tn(got[:, others], got[:, half : 2 * half])
-        for p in range(per):
-            d[(sp[2] & (per - 1)) ^ p] = gd[p * rd : (p + 1) * rd].astype(BF16)
-            at = (sp[3] & (per - 1)) ^ p
-            for i in range(half // width):
-                u[at, i * ru : (i + 1) * ru, :] = gu[p * ru : (p + 1) * ru, i * width : (i + 1) * width].astype(BF16)
-
-
-def attend_back_kernel(stations, tok, row, whole, last, *refs):
+    part = (sp[2] // per) ^ send
+    cols = half_of(part, half // 2)
+    gd = tn(hid_m[:, cols], g_m[...]) + tn(got[:, cols], g_o[...])
+    part = (sp[3] // per) ^ send
+    own = half_of(part, width // 2)
+    others = pl.ds(pl.multiple_of(2 * half + part * (width // 2), 128), width // 2)
+    gu = tn(n_m[:, own], pre_m[...]) + tn(got[:, others], got[:, half : 2 * half])
+    for p in range(per):
+        d[(sp[2] & (per - 1)) ^ p] = gd[p * rd : (p + 1) * rd].astype(BF16)
+        at = (sp[3] & (per - 1)) ^ p
+        for i in range(half // width):
+            u[at, i * ru : (i + 1) * ru, :] = gu[p * ru : (p + 1) * ru, i * width : (i + 1) * width].astype(BF16)
+
+
+def attend_back_kernel(stations, tok, rows_here, whole, last, *refs):
     refs = list(refs)
 
     def take(count):
@@ -276,16 +275,15 @@
 
     sp, offsets, crop, br_m, br_o, wo, qm, lse, ot, weights = take(10)
     k, v, kt, norm_t = (take(stations) for _ in range(4))
-    sums_in = take(5) if row else None
+    sums_in = take(5) if rows_here[0] else None
     if last:
         vectors, vec_in = take(2)
-        before = take(row)
-    dn_m, dn_o = take(2)
-    base = row * stations if last else 0
+        before = take(rows_here[0])
+    dn_m = take(len(rows_here))
+    dn_o = take(1 if last else len(rows_here))
     if last:
         ones, twos = take(2), take(2)
     gq, gk, gv, go, sums = take(5)
-    at = row if whole else 0
     heads = HEADS // 2
     _, width, half = weights.shape
     size = half // heads
@@ -293,75 +291,80 @@
     block = min(4, stations)
     blocks = stations // block
 
-    branch = jnp.concatenate([br_m[at], br_o[at]], axis=0)
-    do = nt(branch, wo[half_of(sp[0], half), :])
-    dot = do.T
-    do = do.astype(BF16)
-    lane = lax.broadcasted_iota(jnp.int32, (chip, 2 * size), 1)
-    head_at = at * heads
-    out_t = jnp.concatenate([ot[head_at + h] for h in range(heads)], axis=0).astype(BF16)
-    go_row = nn(out_t, branch)
-    query_seg = segments(positions(sp, 0, tok, (1, chip), 1), offsets, crop, row)
-    biases = []
-    for chunk in range(stations):
-        key_seg = segments(positions(sp, chunk, tok, (chip, chip), 0), offsets, crop, row)
-        biases.append(jnp.where(key_seg == query_seg, 0.0, MASKED))
-    dqt = []
-    dks = [[] for _ in range(blocks)]
-    dvs = [[] for _ in range(blocks)]
-    for pair in range(heads // 2):
-        lanes = slice(pair * 2 * size, (pair + 1) * 2 * size)
-        dk = [None] * blocks
-        dv = [None] * blocks
-        for h in (2 * pair, 2 * pair + 1):
-            wide = do[:, lanes]
-            dm = jnp.where((lane >= size) if h % 2 else (lane < size), wide, jnp.zeros_like(wide))
-            delta = jnp.sum(ot[head_at + h] * dot[h * size : (h + 1) * size], axis=0, keepdims=True)
-            dq = None
+    made_here = [0.0] * 5
+    for place, row in enumerate(rows_here):
+        at = row if whole else 0
+        branch = jnp.concatenate([br_m[at], br_o[at]], axis=0)
+        do = nt(branch, wo[half_of(sp[0], half), :])
+        dot = do.T
+        do = do.astype(BF16)
+        lane = lax.broadcasted_iota(jnp.int32, (chip, 2 * size), 1)
+        head_at = at * heads
+        out_t = jnp.concatenate([ot[head_at + h] for h in range(heads)], axis=0).astype(BF16)
+        go_row = nn(out_t, branch)
+        query_seg = segments(positions(sp, 0, tok, (1, chip), 1), offsets, crop, row)
+        biases = []
+        for chunk in range(stations):
+            key_seg = segments(positions(sp, chunk, tok, (chip, chip), 0), offsets, crop, row)
+            biases.append(jnp.where(key_seg == query_seg, 0.0, MASKED))
+        dqt = []
+        dks = [[] for _ in range(blocks)]
+        dvs = [[] for _ in range(blocks)]
+        for pair in range(heads // 2):
+            lanes = slice(pair * 2 * size, (pair + 1) * 2 * size)
+            dk = [None] * blocks
+            dv = [None] * blocks
+            for h in (2 * pair, 2 * pair + 1):
+                wide = do[:, lanes]
+                dm = jnp.where((lane >= size) if h % 2 else (lane < size), wide, jnp.zeros_like(wide))
+                delta = jnp.sum(ot[head_at + h] * dot[h * size : (h + 1) * size], axis=0, keepdims=True)
+                dq = None
+                for b in range(blocks):
+                    chunks = range(b * block, (b + 1) * block)
+                    keys = jnp.concatenate([k[c][at, :, lanes] for c in chunks], axis=0)
+                    values = jnp.concatenate([v[c][at, :, lanes] for c in chunks], axis=0)
+                    keys_t = jnp.concatenate([kt[c][at, h * size : (h + 1) * size, :] for c in chunks], axis=1)
+                    bias = jnp.concatenate([biases[c] for c in chunks], axis=0)
+                    p = jnp.exp(nt(keys, qm[head_at + h]) + bias - lse[head_at + h])
+                    ds = (p * (nt(values, dm) - delta)).astype(BF16)
+                    dv_h, dk_h = nn(p.astype(BF16), dm), nn(ds, qm[head_at + h])
+                    dv[b] = dv_h if dv[b] is None else dv[b] + dv_h
+                    dk[b] = dk_h if dk[b] is None else dk[b] + dk_h
+                    more = nn(keys_t, ds)
+                    dq = more if dq is None else dq + more
+                dqt.append(dq)
             for b in range(blocks):
-                chunks = range(b * block, (b + 1) * block)
-                keys = jnp.concatenate([k[c][at, :, lanes] for c in chunks], axis=0)
-                values = jnp.concatenate([v[c][at, :, lanes] for c in chunks], axis=0)
-                keys_t = jnp.concatenate([kt[c][at, h * size : (h + 1) * size, :] for c in chunks], axis=1)
-                bias = jnp.concatenate([biases[c] for c in chunks], axis=0)
-                p = jnp.exp(nt(keys, qm[head_at + h]) + bias - lse[head_at + h])
-                ds = (p * (nt(values, dm) - delta)).astype(BF16)
-                dv_h, dk_h = nn(p.astype(BF16), dm), nn(ds, qm[head_at + h])
-                dv[b] = dv_h if dv[b] is None else dv[b] + dv_h
-                dk[b] = dk_h if dk[b] is None else dk[b] + dk_h
-                more = nn(keys_t, ds)
-                dq = more if dq is None else dq + more
-            dqt.append(dq)
+                dks[b].append(dk[b].astype(BF16))
+                dvs[b].append(dv[b].astype(BF16))
+        dq = (jnp.concatenate(dqt, axis=0) * size**-0.5).T.astype(BF16)
+        gq_row = nn(norm_t[0][at], dq)
+        gk_row = gv_row = sum_k = sum_v = 0.0
         for b in range(blocks):
-            dks[b].append(dk[b].astype(BF16))
-            dvs[b].append(dv[b].astype(BF16))
-    dq = (jnp.concatenate(dqt, axis=0) * size**-0.5).T.astype(BF16)
-    gq_row = nn(norm_t[0][at], dq)
-    gk_row = gv_row = sum_k = sum_v = 0.0
-    for b in range(blocks):
-        dk = jnp.concatenate(dks[b], axis=1)
-        dv = jnp.concatenate(dvs[b], axis=1)
-        normed = jnp.concatenate([norm_t[c][at] for c in range(b * block, (b + 1) * block)], axis=1)
-        gk_row += nn(normed, dk)
-        gv_row += nn(normed, dv)
-        sum_k += jnp.sum(dk.astype(F32), axis=0, keepdims=True)
-        sum_v += jnp.sum(dv.astype(F32), axis=0, keepdims=True)
-        dn = nt(dk, weights[1]) + nt(dv, weights[2])
-        for i in range(block):
-            part = dn[i * chip : (i + 1) * chip]
-            if b + i == 0:
-                part += nt(dq, weights[0])
-            dn_m[b * block + i] = part[:tok].astype(BF16)
-            dn_o[base + b * block + i] = part[tok:].astype(BF16)
-    sum_q = jnp.sum(dq.astype(F32), axis=0, keepdims=True)
-    made_here = (gq_row, gk_row, gv_row, go_row, jnp.concatenate([sum_q, sum_v, sum_k, jnp.zeros((5, half), F32)]))
+            dk = jnp.concatenate(dks[b], axis=1)
+            dv = jnp.concatenate(dvs[b], axis=1)
+            normed = jnp.concatenate([norm_t[c][at] for c in range(b * block, (b + 1) * block)], axis=1)
+            gk_row += nn(normed, dk)
+            gv_row += nn(normed, dv)
+            sum_k += jnp.sum(dk.astype(F32), axis=0, keepdims=True)
+            sum_v += jnp.sum(dv.astype(F32), axis=0, keepdims=True)
+            dn = nt(dk, weights[1]) + nt(dv, weights[2])
+            for i in range(block):
+                part = dn[i * chip : (i + 1) * chip]
+                if b + i == 0:
+                    part += nt(dq, weights[0])
+                dn_m[place][b * block + i] = part[:tok].astype(BF16)
+                dn_o[0 if last else place][(row * stations if last else 0) + b * block + i] = part[tok:].astype(BF16)
+        sum_q = jnp.sum(dq.astype(F32), axis=0, keepdims=True)
+        rest = jnp.zeros((5, half), F32)
+        values = (gq_row, gk_row, gv_row, go_row, jnp.concatenate([sum_q, sum_v, sum_k, rest]))
+        made_here = [a + b for a, b in zip(made_here, values)]
     for i, (ref, value) in enumerate(zip((gq, gk, gv, go, sums), made_here)):
         ref[...] = value if sums_in is None else value + sums_in[i][...]
     if not last:
         return
 
     for r, part in enumerate(before):
-        dn_o[r * stations : (r + 1) * stations] = part[...]
+        dn_o[0][r * stations : (r + 1) * stations] = part[...]
     vec = refs[0]
     lane = lax.broadcasted_iota(jnp.int32, (2, width), 1)
     both = sums[0:2, :]
@@ -766,13 +769,16 @@
     )
     branch_r = exchange(branch, "seq", 1)
     piece = made((PIECES // 2, hidden // 2 // PIECES, width), BF16)
-    d_keep, d_send, u_keep, u_send = call(
-        ffn_grad_kernel, [sp, hid_m, pre_m, normed_two, got, g_v.reshape(flat, width), g_other],
-        [piece, piece, piece, piece],
-        us=3.0, limit=LIMITS[2], name="feed_forward_grad",
+    ins = [sp, hid_m, pre_m, normed_two, got, g_v.reshape(flat, width), g_other]
+    d_send, u_send = call(
+        functools.partial(ffn_grad_kernel, 1), ins, [piece, piece], us=3.0, limit=LIMITS[2], name="feed_forward_grad_sent"
     )
     d_send, u_send, branch_r = tied(d_send, u_send, branch_r)
-    chain = Chain(u_keep)
+    chain = Chain(d_send)
+    d_keep, u_keep = chain(
+        functools.partial(call, functools.partial(ffn_grad_kernel, 0)), ins, [piece, piece], us=0.05, limit=LIMITS[2],
+        name="feed_forward_grad_kept",
+    )
 
     q = PIECES // GROUP
     d_got, u_got = exchange(d_send, *bit_x), exchange(u_send, *bit_y)
@@ -797,8 +803,9 @@
         ins = [*dn_m, dn_r, *arrived]
         return (functools.partial(norm_grad_kernel, chunk, rows), ins, [made((rows, tok, width), BF16)])
 
-    for r in range(rows):
-        last = r == rows - 1
+    groups = [tuple(range(rows - 1)), (rows - 1,)] if small else [(r,) for r in range(rows)]
+    for group in groups:
+        r, last = group[-1], group[-1] == rows - 1
         arrays = [branch, branch_r, wo, query, lse, out_t, weights] + [a for part in kept for a in part]
         specs = [VMEM] * len(arrays)
         if not small:
@@ -811,20 +818,24 @@
             tail += [vectors, vec_ffn, *dn_o]
         part = made((stations, tok, width), BF16)
         grads = [made((width, half), F32)] * 3 + [made((half, width), F32), made((8, half), F32)]
-        outs = [part, part] + grads
+        outs = [part] * (2 * len(group)) + grads
         scratch = []
         if last:
             outs = [part, made((rows * stations, tok, width), BF16)] + [made((width // 2, width), BF16)] * 2 + [made((width // 2 + 16, width), BF16)] * 2
             scratch = [pltpu.VMEM(g.shape, F32) for g in grads] + [pltpu.VMEM((16, width), F32)]
-        run = functools.partial(call, functools.partial(attend_back_kernel, stations, tok, r, small, last))
+        run = functools.partial(call, functools.partial(attend_back_kernel, stations, tok, group, small, last))
         res = chain(
             run, [sp, offsets, crop] + arrays + tail, outs, scratch=scratch,
             us=BACK_US, limit=LIMITS[3] if small else 48, name=f"attend_back_{r}", scalars=3,
             specs=specs + [VMEM] * len(tail), grid=() if small else (1,),
         )
-        dn_m.append(res[0])
-        dn_o.append(res[1])
-        sums = list(res[2:7])
+        if last:
+            dn_m.append(res[0])
+            dn_o.append(res[1])
+        else:
+            dn_m += res[: len(group)]
+            dn_o += res[len(group) : 2 * len(group)]
+            sums = list(res[2 * len(group) :])
         if r == rows - 2:
             quarters = made((q,) + piece.shape[1:], BF16)
             ((d_next, u_next),) = together(

time: 165 us -> 164 us (level)
  transfers between devices with their start and end apart: 47 -> 47, of which waited for: 22 -> 21; matrix products, arithmetic and copies ran while one was open for 3% -> 3% of each run, Pallas kernels for 26% -> 26%
where the time goes in v2:
time: 164 us; the launch traced here: 161 us
  waiting for transfers between devices  52.5 us (32%)
  Pallas kernels  52.3 us (32%)
  starting transfers between devices  49 us (30%)
  local copies, waits for them, and re-layouts  4.48 us (3%)
    ppermute x47, waiting for transfers between devices, exchange(): return lax.ppermute(array, axis, [(i, i ^ mask) for i in range(count)])  52.5 us
    pallas_call x24, Pallas kernels, call(): pl.pallas_call(body_of, grid=grid, in_specs=[SMEM] * scalars + (specs or...  52.3 us
    ppermute x47, starting transfers between devices, exchange(): return lax.ppermute(array, axis, [(i, i ^ mask) for i in range(count)])  49 us
  transfers between devices with their start and end apart: 47, of which 21 were waited for; matrix products, arithmetic and copies ran while one was open for 3% of the time, Pallas kernels for 26%

profile of v2, /device:TPU:0, one launch (start us, length us, event | category | flops | bytes accessed | tf_op | source)
XLA Modules:
  0.0 161.1 jit_solution(13356278830175508827)
XLA Ops:
  1.2 3.7 %collective-permute-start = (bf16[3,128,512]{2,1,0:T(8,128)(2,1)}, bf16[3,128,512]{2,1,0:T(8,128)(2,1)S(1)}, u32[]{:S(2)}, u32[]{:S(2)}) collective-permute-start(bf16[3,128,512]{2,1,0:T(8,128)(2,1)} %refs_1_.8), channel_id=1, source_target_pairs={{0,4},{1,5},{2,6},{3,7},{4,0},{5,1},{6,2},{7,3},{8,12},{9,13},{10,... | collective-permute-start | bytes 1179656 | tf_op jit(solution)/shard_map/ppermute | solution.py:639
  6.5 1.9 %dynamic-slice_bitcast_fusion = (bf16[1,512,256]{2,1,0:T(8,128)(2,1)}, bf16[1,512,256]{2,1,0:T(8,128)(2,1)}) fusion(bf16[512,512]{1,0:T(8,128)(2,1)} %param.25, s32[]{:T(128)S(6)} %select_n.39, bf16[512,512]{1,0:T(8,128)(2,1)} %param.24), kind=kLoop, calls=%fused_computation.1 | loop fusion | bytes 1048580 | tf_op jit(solution)/shard_map/stack | solution.py:698
  10.7 3.5 %attend_chunk_0.1 = (bf16[3,256,256]{2,1,0:T(8,128)(2,1)S(1)}, bf16[3,256,256]{2,1,0:T(8,128)(2,1)S(1)}, bf16[3,256,256]{2,1,0:T(8,128)(2,1)S(1)}, bf16[3,512,25...) custom-call(s32[5]{0:T(128)S(1)} %stack.53.refs_0_, ...), custom_call_target="tpu_custom_call" | custom-call | flops 55000000 | tf_op jit(solution)/shard_map/attend_chunk_0/pallas_call | solution.py:611
  17.5 5.8 %collective-permute-done.refs_3_ = bf16[3,128,512]{2,1,0:T(8,128)(2,1)S(1)} collective-permute-done((bf16[3,128,512]{2,1,0:T(8,128)(2,1)}, bf16[3,128,512]{2,1,0:T(8,128)(2,1)S(1)}, u32[]{:S(2)}, u32[]{:S(2)}) %collective-permute-start) | collective-permute-done | bytes 393248 | tf_op jit(solution)/shard_map/ppermute | solution.py:639
  25.1 3.3 %attend_chunk_2.1 = (bf16[3,256,256]{2,1,0:T(8,128)(2,1)S(1)}, bf16[3,256,256]{2,1,0:T(8,128)(2,1)S(1)}, bf16[3,256,256]{2,1,0:T(8,128)(2,1)S(1)}, bf16[3,512,25...) custom-call(s32[5]{0:T(128)S(1)} %stack.53.refs_0_, ...), custom_call_target="tpu_custom_call" | custom-call | flops 55000000 | tf_op jit(solution)/shard_map/attend_chunk_2/pallas_call | solution.py:611
  28.4 3.3 %attend_chunk_1.1 = (bf16[3,256,256]{2,1,0:T(8,128)(2,1)S(1)}, bf16[3,256,256]{2,1,0:T(8,128)(2,1)S(1)}, bf16[3,256,256]{2,1,0:T(8,128)(2,1)S(1)}, bf16[3,512,25...) custom-call(s32[5]{0:T(128)S(1)} %stack.53.refs_0_, ...), custom_call_target="tpu_custom_call" | custom-call | flops 55000000 | tf_op jit(solution)/shard_map/attend_chunk_1/pallas_call | solution.py:611
  31.8 3.6 %collective-permute-done.2.refs_3_ = bf16[3,128,512]{2,1,0:T(8,128)(2,1)S(1)} collective-permute-done((bf16[3,128,512]{2,1,0:T(8,128)(2,1)S(1)}, bf16[3,128,512]{2,1,0:T(8,128)(2,1)S(1)}, u32[]{:S(2)}, u32[]{:S(2)}) %collective-permute-start.2) | collective-permute-done | bytes 393248 | tf_op jit(solution)/shard_map/ppermute | solution.py:639
  37.1 3.4 %attend_chunk_3.1 = (bf16[3,256,256]{2,1,0:T(8,128)(2,1)S(1)}, bf16[3,256,256]{2,1,0:T(8,128)(2,1)S(1)}, bf16[3,256,256]{2,1,0:T(8,128)(2,1)S(1)}, bf16[3,512,25...) custom-call(s32[5]{0:T(128)S(1)} %stack.53.refs_0_, ...), custom_call_target="tpu_custom_call" | custom-call | flops 55000000 | tf_op jit(solution)/shard_map/attend_chunk_3/pallas_call | solution.py:611
  42.0 3.4 %feed_forward_a.1 = (f32[384,512]{1,0:T(8,128)S(1)}, bf16[384,512]{1,0:T(8,128)(2,1)S(1)}, bf16[384,2560]{1,0:T(8,128)(2,1)S(1)}, f32[384,512]{1,0:T(8,128)S(1)}...) custom-call(s32[5]{0:T(128)S(1)} %stack.53.refs_0_, bf16[3,128,256]{2,1,0:T(8,128)(2,1)S(1)} %get-tuple-element.198.refs_1_, ...), custom_call_target="tpu_custom_call" | custom-call | flops 4400000000 | tf_op jit(solution)/shard_map/feed_forward_a/pallas_call | solution.py:611
  45.7 3.7 %feed_forward_b.1 = (bf16[3,128,512]{2,1,0:T(8,128)(2,1)}, bf16[384,1024]{1,0:T(8,128)(2,1)S(1)}, bf16[384,1024]{1,0:T(8,128)(2,1)S(1)}, f32[384,512]{1,0:T(8,12...) custom-call(s32[5]{0:T(128)S(1)} %stack.53.refs_0_, f32[384,512]{1,0:T(8,128)S(1)} %get-tuple-element.208.refs_1_, ...), custom_call_target="tpu_custom_call" | custom-call | flops 4400000000 | tf_op jit(solution)/shard_map/feed_forward_b/pallas_call | solution.py:611
  54.8 1.8 %feed_forward_grad_kept.1 = (bf16[8,64,512]{2,1,0:T(8,128)(2,1)S(1)}, bf16[8,64,512]{2,1,0:T(8,128)(2,1)S(1)}) custom-call(s32[5]{0:T(128)S(1)} %stack.53.refs_0_, bf16[384,1024]{1,0:T(8,128)(2,1)S(1)} %get-tuple-element.217.refs_1_, bf16[384,1024]{1,0:T(8,128)(2,1)S(1)} %get-tuple-element.218.refs_2_, ...), custom_call_target="tpu_custom_call" | custom-call | flops 55000000 | tf_op jit(solution)/shard_map/feed_forward_grad_kept/pallas_call | solution.py:611
  56.6 9.8 %attend_back_1.1 = (bf16[4,128,512]{2,1,0:T(8,128)(2,1)S(1)}, bf16[4,128,512]{2,1,0:T(8,128)(2,1)S(1)}, bf16[4,128,512]{2,1,0:T(8,128)(2,1)S(1)}, bf16[4,128,512...) custom-call(s32[5]{0:T(128)S(1)} %stack.53.refs_0_, ...), custom_call_target="tpu_custom_call" | custom-call | flops 55000000 | tf_op jit(solution)/shard_map/attend_back_1/pallas_call | solution.py:611
  69.2 5.9 %attend_back_2.1 = (bf16[4,128,512]{2,1,0:T(8,128)(2,1)S(1)}, bf16[12,128,512]{2,1,0:T(8,128)(2,1)S(1)}, bf16[256,512]{1,0:T(8,128)(2,1)S(1)}, bf16[256,512]{1,0...) custom-call(s32[5]{0:T(128)S(1)} %stack.53.refs_0_, s32[3,4]{1,0:T(4,128)S(1)} %copy-done.3, ...), custom_call_target="tpu_custom_call" | custom-call | flops 55000000 | tf_op jit(solution)/shard_map/attend_back_2/pallas_call | solution.py:611
  79.2 5.6 %collective-permute-done.17.refs_3_ = bf16[256,512]{1,0:T(8,128)(2,1)S(1)} collective-permute-done((bf16[256,512]{1,0:T(8,128)(2,1)S(1)}, bf16[256,512]{1,0:T(8,128)(2,1)S(1)}, u32[]{:S(2)}, u32[]{:S(2)}) %collective-permute-start.17) | collective-permute-done | bytes 262176 | tf_op jit(solution)/shard_map/ppermute | solution.py:639
  86.8 2.2 %collective-permute-start.19 = (bf16[128,512]{1,0:T(8,128)(2,1)S(1)}, bf16[128,512]{1,0:T(8,128)(2,1)S(1)}, u32[]{:S(2)}, u32[]{:S(2)}) collective-permute-start(bf16[128,512]{1,0:T(8,128)(2,1)S(1)} %get-tuple-element.273), channel_id=1, source_target_pairs={{0,4},{1,5},{2,6},{3,7},{4,0},{5,1},{6,2},{7,3},{8,12},{9,13},{10,... | collective-permute-start | bytes 393224 | tf_op jit(solution)/shard_map/ppermute | solution.py:639
  90.5 4.2 %collective-permute-done.19.refs_1_ = bf16[128,512]{1,0:T(8,128)(2,1)S(1)} collective-permute-done((bf16[128,512]{1,0:T(8,128)(2,1)S(1)}, bf16[128,512]{1,0:T(8,128)(2,1)S(1)}, u32[]{:S(2)}, u32[]{:S(2)}) %collective-permute-start.19) | collective-permute-done | bytes 131104 | tf_op jit(solution)/shard_map/ppermute | solution.py:639
  96.0 2.6 %collective-permute-start.22 = (bf16[128,512]{1,0:T(8,128)(2,1)S(1)}, bf16[128,512]{1,0:T(8,128)(2,1)S(1)}, u32[]{:S(2)}, u32[]{:S(2)}) collective-permute-start(bf16[128,512]{1,0:T(8,128)(2,1)S(1)} %get-tuple-element.276.refs_0_), channel_id=1, source_target_pairs={{0,4},{1,5},{2,6},{3,7},{4,0},{5,1},{6,2},{7,3},{8,12},{9,13},{10,... | collective-permute-start | bytes 393224 | tf_op jit(solution)/shard_map/ppermute | solution.py:639
  98.6 4.4 %collective-permute-done.22.refs_1_ = bf16[128,512]{1,0:T(8,128)(2,1)S(1)} collective-permute-done((bf16[128,512]{1,0:T(8,128)(2,1)S(1)}, bf16[128,512]{1,0:T(8,128)(2,1)S(1)}, u32[]{:S(2)}, u32[]{:S(2)}) %collective-permute-start.22) | collective-permute-done | bytes 131104 | tf_op jit(solution)/shard_map/ppermute | solution.py:639
  103.1 2.0 %collective-permute-start.24 = (bf16[2,128,512]{2,1,0:T(8,128)(2,1)S(1)}, bf16[2,128,512]{2,1,0:T(8,128)(2,1)S(1)}, u32[]{:S(2)}, u32[]{:S(2)}) collective-permute-start(bf16[2,128,512]{2,1,0:T(8,128)(2,1)S(1)} %get-tuple-element.279.refs_0_), channel_id=1, source_target_pairs={{0,2},{1,3},{2,0},{3,1},{4,6},{5,7},{6,4},{7,5},{8,10},{9,11},{10,... | collective-permute-start | bytes 786440 | tf_op jit(solution)/shard_map/ppermute | solution.py:639
  105.1 2.0 %collective-permute-start.25 = (bf16[80,512]{1,0:T(8,128)(2,1)S(1)}, bf16[80,512]{1,0:T(8,128)(2,1)S(1)}, u32[]{:S(2)}, u32[]{:S(2)}) collective-permute-start(bf16[80,512]{1,0:T(8,128)(2,1)S(1)} %get-tuple-element.281.refs_8_), channel_id=1, source_target_pairs={{0,4},{1,5},{2,6},{3,7},{4,0},{5,1},{6,2},{7,3},{8,12},{9,13},{10,... | collective-permute-start | bytes 245768 | tf_op jit(solution)/shard_map/ppermute | solution.py:639
  107.1 4.2 %collective-permute-done.25.refs_3_ = bf16[80,512]{1,0:T(8,128)(2,1)S(1)} collective-permute-done((bf16[80,512]{1,0:T(8,128)(2,1)S(1)}, bf16[80,512]{1,0:T(8,128)(2,1)S(1)}, u32[]{:S(2)}, u32[]{:S(2)}) %collective-permute-start.25) | collective-permute-done | bytes 81952 | tf_op jit(solution)/shard_map/ppermute | solution.py:639
  111.6 2.5 %collective-permute-start.29 = (bf16[3,128,512]{2,1,0:T(8,128)(2,1)S(1)}, bf16[3,128,512]{2,1,0:T(8,128)(2,1)S(1)}, u32[]{:S(2)}, u32[]{:S(2)}) collective-permute-start(bf16[3,128,512]{2,1,0:T(8,128)(2,1)S(1)} %get-tuple-element.287.refs_11_), channel_id=1, source_target_pairs={{0,2},{1,3},{2,0},{3,1},{4,6},{5,7},{6,4},{7,5},{8,10},{9,11},{10,... | collective-permute-start | bytes 1179656 | tf_op jit(solution)/shard_map/ppermute | solution.py:639
  117.9 4.8 %collective-permute-done.29.refs_10_ = bf16[3,128,512]{2,1,0:T(8,128)(2,1)S(1)} collective-permute-done((bf16[3,128,512]{2,1,0:T(8,128)(2,1)S(1)}, bf16[3,128,512]{2,1,0:T(8,128)(2,1)S(1)}, u32[]{:S(2)}, u32[]{:S(2)}) %collective-permute-start.29) | collective-permute-done | bytes 393248 | tf_op jit(solution)/shard_map/ppermute | solution.py:639
  125.5 2.6 %collective-permute-start.30 = (bf16[3,128,512]{2,1,0:T(8,128)(2,1)S(1)}, bf16[3,128,512]{2,1,0:T(8,128)(2,1)S(1)}, u32[]{:S(2)}, u32[]{:S(2)}) collective-permute-start(bf16[3,128,512]{2,1,0:T(8,128)(2,1)S(1)} %get-tuple-element.292.refs_6_), channel_id=1, source_target_pairs={{0,4},{1,5},{2,6},{3,7},{4,0},{5,1},{6,2},{7,3},{8,12},{9,13},{10,... | collective-permute-start | bytes 1179656 | tf_op jit(solution)/shard_map/ppermute | solution.py:639
  129.0 4.1 %collective-permute-done.32.refs_1_ = bf16[8,64,512]{2,1,0:T(8,128)(2,1)S(1)} collective-permute-done((bf16[8,64,512]{2,1,0:T(8,128)(2,1)S(1)}, bf16[8,64,512]{2,1,0:T(8,128)(2,1)S(1)}, u32[]{:S(2)}, u32[]{:S(2)}) %collective-permute-start.32) | collective-permute-done | bytes 524320 | tf_op jit(solution)/shard_map/ppermute | solution.py:639
  133.7 2.4 %collective-permute-done.31.refs_1_ = bf16[2,80,512]{2,1,0:T(8,128)(2,1)S(1)} collective-permute-done((bf16[2,80,512]{2,1,0:T(8,128)(2,1)S(1)}, bf16[2,80,512]{2,1,0:T(8,128)(2,1)S(1)}, u32[]{:S(2)}, u32[]{:S(2)}) %collective-permute-start.31) | collective-permute-done | bytes 163872 | tf_op jit(solution)/shard_map/ppermute | solution.py:639
  137.8 3.8 %collective-permute-done.30.refs_7_ = bf16[3,128,512]{2,1,0:T(8,128)(2,1)S(1)} collective-permute-done((bf16[3,128,512]{2,1,0:T(8,128)(2,1)S(1)}, bf16[3,128,512]{2,1,0:T(8,128)(2,1)S(1)}, u32[]{:S(2)}, u32[]{:S(2)}) %collective-permute-start.30) | collective-permute-done | bytes 393248 | tf_op jit(solution)/shard_map/ppermute | solution.py:639
  143.5 2.5 %collective-permute-start.38 = (bf16[3,128,512]{2,1,0:T(8,128)(2,1)S(1)}, bf16[3,128,512]{2,1,0:T(8,128)(2,1)S(1)}, u32[]{:S(2)}, u32[]{:S(2)}) collective-permute-start(bf16[3,128,512]{2,1,0:T(8,128)(2,1)S(1)} %get-tuple-element.301.refs_4_), channel_id=1, source_target_pairs={{0,2},{1,3},{2,0},{3,1},{4,6},{5,7},{6,4},{7,5},{8,10},{9,11},{10,... | collective-permute-start | bytes 1179656 | tf_op jit(solution)/shard_map/ppermute | solution.py:639
  147.5 2.7 %unpack_feed_forward.2 = (f32[2048,512]{1,0:T(8,128)}, f32[512,2048]{1,0:T(8,128)}, f32[8,128]{1,0:T(8,128)S(1)}) custom-call(s32[5]{0:T(128)S(1)} %stack.53.refs_0_, bf16[8,64,512]{2,1,0:T(8,128)(2,1)S(1)} %get-tuple-element.304.refs_1_, bf16[8,64,512]{2,1,0:T(8,128)(2,1)S(1)} %collective-permute-done.41.refs_2_, ...), custom_call_target="tpu_custom_call" | custom-call | flops 110000000 | tf_op jit(solution)/shard_map/unpack_feed_forward/pallas_call | solution.py:611
  150.2 2.7 %unpack_feed_forward.3 = (f32[2048,512]{1,0:T(8,128)}, f32[512,2048]{1,0:T(8,128)}, f32[8,128]{1,0:T(8,128)S(1)}) custom-call(s32[5]{0:T(128)S(1)} %stack.53.refs_0_, bf16[8,64,512]{2,1,0:T(8,128)(2,1)S(1)} %collective-permute-done.32.refs_1_, bf16[8,64,512]{2,1,0:T(8,128)(2,1)S(1)} %collective-permute-done.39.refs_2_, ...), custom_call_target="tpu_custom_call", output_to_operand_aliasing={{0}: (5, {}), {1}: (6, {})} | custom-call | flops 110000000 | tf_op jit(solution)/shard_map/unpack_feed_forward/pallas_call | solution.py:611
  152.9 2.4 %collective-permute-done.38.refs_8_ = bf16[3,128,512]{2,1,0:T(8,128)(2,1)S(1)} collective-permute-done((bf16[3,128,512]{2,1,0:T(8,128)(2,1)S(1)}, bf16[3,128,512]{2,1,0:T(8,128)(2,1)S(1)}, u32[]{:S(2)}, u32[]{:S(2)}) %collective-permute-start.38) | collective-permute-done | bytes 393248 | tf_op jit(solution)/shard_map/ppermute | solution.py:639
  158.0 2.7 %unpack_attend.1 = (f32[512,512]{1,0:T(8,128)}, f32[512,512]{1,0:T(8,128)}, f32[512,512]{1,0:T(8,128)}, f32[512,512]{1,0:T(8,128)}, f32[1,512]{1,0:T(1,128)}, /*...) custom-call(s32[5]{0:T(128)S(1)} %stack.53.refs_0_, ...), custom_call_target="tpu_custom_call" | custom-call | flops 110000000 | tf_op jit(solution)/shard_map/unpack_attend/pallas_call | solution.py:611
  (120 shorter events, 45.9 us)
Async XLA Ops:
  0.7 10.0 %collective-permute-start.1 = (bf16[3,128,512]{2,1,0:T(8,128)(2,1)}, bf16[3,128,512]{2,1,0:T(8,128)(2,1)S(1)}, u32[]{:S(2)}, u32[]{:S(2)}) collective-permute-start(bf16[3,128,512]{2,1,0:T(8,128)(2,1)} %refs_1_.8), channel_id=1, source_target_pairs={{0,1},{1,0},{2,3},{3,2},{4,5},{5,4},{6,7},{7,6},{8,9},{9,8},{10,11... | collective-permute-start | bytes 1179656 | tf_op jit(solution)/shard_map/ppermute | solution.py:639
  1.2 22.1 %collective-permute-start = (bf16[3,128,512]{2,1,0:T(8,128)(2,1)}, bf16[3,128,512]{2,1,0:T(8,128)(2,1)S(1)}, u32[]{:S(2)}, u32[]{:S(2)}) collective-permute-start(bf16[3,128,512]{2,1,0:T(8,128)(2,1)} %refs_1_.8), channel_id=1, source_target_pairs={{0,4},{1,5},{2,6},{3,7},{4,0},{5,1},{6,2},{7,3},{8,12},{9,13},{10,... | collective-permute-start | bytes 1179656 | tf_op jit(solution)/shard_map/ppermute | solution.py:639
  4.9 19.0 %collective-permute-start.3 = (bf16[3,128,512]{2,1,0:T(8,128)(2,1)}, bf16[3,128,512]{2,1,0:T(8,128)(2,1)S(1)}, u32[]{:S(2)}, u32[]{:S(2)}) collective-permute-start(bf16[3,128,512]{2,1,0:T(8,128)(2,1)} %refs_1_.8), channel_id=1, source_target_pairs={{0,2},{1,3},{2,0},{3,1},{4,6},{5,7},{6,4},{7,5},{8,10},{9,11},{10,... | collective-permute-start | bytes 1179656 | tf_op jit(solution)/shard_map/ppermute | solution.py:639
  23.9 11.5 %collective-permute-start.2 = (bf16[3,128,512]{2,1,0:T(8,128)(2,1)S(1)}, bf16[3,128,512]{2,1,0:T(8,128)(2,1)S(1)}, u32[]{:S(2)}, u32[]{:S(2)}) collective-permute-start(bf16[3,128,512]{2,1,0:T(8,128)(2,1)S(1)} %collective-permute-done.refs_3_), channel_id=1, source_target_pairs={{0,2},{1,3},{2,0},{3,1},{4,6},{5,7},{6,4},{7,5},{8,10},{9,11},{10,... | collective-permute-start | bytes 1179656 | tf_op jit(solution)/shard_map/ppermute | solution.py:639
  51.6 14.8 %collective-permute-start.11 = (bf16[8,64,512]{2,1,0:T(8,128)(2,1)S(1)}, bf16[8,64,512]{2,1,0:T(8,128)(2,1)S(1)}, u32[]{:S(2)}, u32[]{:S(2)}) collective-permute-start(bf16[8,64,512]{2,1,0:T(8,128)(2,1)S(1)} %get-tuple-element.242.refs_7_), channel_id=1, source_target_pairs={{0,8},{8,0},{16,24},{24,16},{1,9},{9,1},{17,25},{25,17},{2,10},{10... | collective-permute-start | bytes 1572872 | tf_op jit(solution)/shard_map/ppermute | solution.py:639
  53.2 13.7 %collective-permute-start.12 = (bf16[8,64,512]{2,1,0:T(8,128)(2,1)S(1)}, bf16[8,64,512]{2,1,0:T(8,128)(2,1)S(1)}, u32[]{:S(2)}, u32[]{:S(2)}) collective-permute-start(bf16[8,64,512]{2,1,0:T(8,128)(2,1)S(1)} %get-tuple-element.255), channel_id=1, source_target_pairs={{0,16},{8,24},{16,0},{24,8},{1,17},{9,25},{17,1},{25,9},{2,18},{10... | collective-permute-start | bytes 1572872 | tf_op jit(solution)/shard_map/ppermute | solution.py:639
  67.1 8.0 %collective-permute-start.13 = (bf16[4,64,512]{2,1,0:T(8,128)(2,1)S(1)}, bf16[4,64,512]{2,1,0:T(8,128)(2,1)S(1)}, u32[]{:S(2)}, u32[]{:S(2)}) collective-permute-start(bf16[4,64,512]{2,1,0:T(8,128)(2,1)S(1)} %get-tuple-element.261), channel_id=1, source_target_pairs={{0,16},{8,24},{16,0},{24,8},{1,17},{9,25},{17,1},{25,9},{2,18},{10... | collective-permute-start | bytes 786440 | tf_op jit(solution)/shard_map/ppermute | solution.py:639
  68.6 6.9 %collective-permute-start.14 = (bf16[4,64,512]{2,1,0:T(8,128)(2,1)S(1)}, bf16[4,64,512]{2,1,0:T(8,128)(2,1)S(1)}, u32[]{:S(2)}, u32[]{:S(2)}) collective-permute-start(bf16[4,64,512]{2,1,0:T(8,128)(2,1)S(1)} %get-tuple-element.256.refs_35_), channel_id=1, source_target_pairs={{0,8},{8,0},{16,24},{24,16},{1,9},{9,1},{17,25},{25,17},{2,10},{10... | collective-permute-start | bytes 786440 | tf_op jit(solution)/shard_map/ppermute | solution.py:639
  75.8 9.7 %collective-permute-start.18 = (bf16[272,512]{1,0:T(8,128)(2,1)S(1)}, bf16[272,512]{1,0:T(8,128)(2,1)S(1)}, u32[]{:S(2)}, u32[]{:S(2)}) collective-permute-start(bf16[272,512]{1,0:T(8,128)(2,1)S(1)} %get-tuple-element.270.refs_6_), channel_id=1, source_target_pairs={{0,16},{8,24},{16,0},{24,8},{1,17},{9,25},{17,1},{25,9},{2,18},{10... | collective-permute-start | bytes 835592 | tf_op jit(solution)/shard_map/ppermute | solution.py:639
  76.5 8.4 %collective-permute-start.17 = (bf16[256,512]{1,0:T(8,128)(2,1)S(1)}, bf16[256,512]{1,0:T(8,128)(2,1)S(1)}, u32[]{:S(2)}, u32[]{:S(2)}) collective-permute-start(bf16[256,512]{1,0:T(8,128)(2,1)S(1)} %get-tuple-element.268), channel_id=1, source_target_pairs={{0,8},{8,0},{16,24},{24,16},{1,9},{9,1},{17,25},{25,17},{2,10},{10... | collective-permute-start | bytes 786440 | tf_op jit(solution)/shard_map/ppermute | solution.py:639
  77.4 8.1 %collective-permute-start.16 = (bf16[2,128,512]{2,1,0:T(8,128)(2,1)S(1)}, bf16[2,128,512]{2,1,0:T(8,128)(2,1)S(1)}, u32[]{:S(2)}, u32[]{:S(2)}) collective-permute-start(bf16[2,128,512]{2,1,0:T(8,128)(2,1)S(1)} %get-tuple-element.271.refs_6_), channel_id=1, source_target_pairs={{0,2},{1,3},{2,0},{3,1},{4,6},{5,7},{6,4},{7,5},{8,10},{9,11},{10,... | collective-permute-start | bytes 786440 | tf_op jit(solution)/shard_map/ppermute | solution.py:639
  85.7 9.0 %collective-permute-start.21 = (bf16[144,512]{1,0:T(8,128)(2,1)S(1)}, bf16[144,512]{1,0:T(8,128)(2,1)S(1)}, u32[]{:S(2)}, u32[]{:S(2)}) collective-permute-start(bf16[144,512]{1,0:T(8,128)(2,1)S(1)} %get-tuple-element.275.refs_8_), channel_id=1, source_target_pairs={{0,8},{8,0},{16,24},{24,16},{1,9},{9,1},{17,25},{25,17},{2,10},{10... | collective-permute-start | bytes 442376 | tf_op jit(solution)/shard_map/ppermute | solution.py:639
  86.8 7.8 %collective-permute-start.19 = (bf16[128,512]{1,0:T(8,128)(2,1)S(1)}, bf16[128,512]{1,0:T(8,128)(2,1)S(1)}, u32[]{:S(2)}, u32[]{:S(2)}) collective-permute-start(bf16[128,512]{1,0:T(8,128)(2,1)S(1)} %get-tuple-element.273), channel_id=1, source_target_pairs={{0,4},{1,5},{2,6},{3,7},{4,0},{5,1},{6,2},{7,3},{8,12},{9,13},{10,... | collective-permute-start | bytes 393224 | tf_op jit(solution)/shard_map/ppermute | solution.py:639
  89.0 5.6 %collective-permute-start.20 = (bf16[128,512]{1,0:T(8,128)(2,1)S(1)}, bf16[128,512]{1,0:T(8,128)(2,1)S(1)}, u32[]{:S(2)}, u32[]{:S(2)}) collective-permute-start(bf16[128,512]{1,0:T(8,128)(2,1)S(1)} %get-tuple-element.274), channel_id=1, source_target_pairs={{0,16},{8,24},{16,0},{24,8},{1,17},{9,25},{17,1},{25,9},{2,18},{10... | collective-permute-start | bytes 393224 | tf_op jit(solution)/shard_map/ppermute | solution.py:639
  94.8 8.2 %collective-permute-start.23 = (bf16[2,80,512]{2,1,0:T(8,128)(2,1)S(1)}, bf16[2,80,512]{2,1,0:T(8,128)(2,1)S(1)}, u32[]{:S(2)}, u32[]{:S(2)}) collective-permute-start(bf16[2,80,512]{2,1,0:T(8,128)(2,1)S(1)} %get-tuple-element.278.refs_4_), channel_id=1, source_target_pairs={{0,2},{1,3},{2,0},{3,1},{4,6},{5,7},{6,4},{7,5},{8,10},{9,11},{10,... | collective-permute-start | bytes 491528 | tf_op jit(solution)/shard_map/ppermute | solution.py:639
  96.0 7.0 %collective-permute-start.22 = (bf16[128,512]{1,0:T(8,128)(2,1)S(1)}, bf16[128,512]{1,0:T(8,128)(2,1)S(1)}, u32[]{:S(2)}, u32[]{:S(2)}) collective-permute-start(bf16[128,512]{1,0:T(8,128)(2,1)S(1)} %get-tuple-element.276.refs_0_), channel_id=1, source_target_pairs={{0,4},{1,5},{2,6},{3,7},{4,0},{5,1},{6,2},{7,3},{8,12},{9,13},{10,... | collective-permute-start | bytes 393224 | tf_op jit(solution)/shard_map/ppermute | solution.py:639
  103.1 8.4 %collective-permute-start.24 = (bf16[2,128,512]{2,1,0:T(8,128)(2,1)S(1)}, bf16[2,128,512]{2,1,0:T(8,128)(2,1)S(1)}, u32[]{:S(2)}, u32[]{:S(2)}) collective-permute-start(bf16[2,128,512]{2,1,0:T(8,128)(2,1)S(1)} %get-tuple-element.279.refs_0_), channel_id=1, source_target_pairs={{0,2},{1,3},{2,0},{3,1},{4,6},{5,7},{6,4},{7,5},{8,10},{9,11},{10,... | collective-permute-start | bytes 786440 | tf_op jit(solution)/shard_map/ppermute | solution.py:639
  105.1 6.2 %collective-permute-start.25 = (bf16[80,512]{1,0:T(8,128)(2,1)S(1)}, bf16[80,512]{1,0:T(8,128)(2,1)S(1)}, u32[]{:S(2)}, u32[]{:S(2)}) collective-permute-start(bf16[80,512]{1,0:T(8,128)(2,1)S(1)} %get-tuple-element.281.refs_8_), channel_id=1, source_target_pairs={{0,4},{1,5},{2,6},{3,7},{4,0},{5,1},{6,2},{7,3},{8,12},{9,13},{10,... | collective-permute-start | bytes 245768 | tf_op jit(solution)/shard_map/ppermute | solution.py:639
  111.6 11.1 %collective-permute-start.29 = (bf16[3,128,512]{2,1,0:T(8,128)(2,1)S(1)}, bf16[3,128,512]{2,1,0:T(8,128)(2,1)S(1)}, u32[]{:S(2)}, u32[]{:S(2)}) collective-permute-start(bf16[3,128,512]{2,1,0:T(8,128)(2,1)S(1)} %get-tuple-element.287.refs_11_), channel_id=1, source_target_pairs={{0,2},{1,3},{2,0},{3,1},{4,6},{5,7},{6,4},{7,5},{8,10},{9,11},{10,... | collective-permute-start | bytes 1179656 | tf_op jit(solution)/shard_map/ppermute | solution.py:639
  114.1 8.6 %collective-permute-start.26 = (bf16[4,64,512]{2,1,0:T(8,128)(2,1)S(1)}, bf16[4,64,512]{2,1,0:T(8,128)(2,1)S(1)}, u32[]{:S(2)}, u32[]{:S(2)}) collective-permute-start(bf16[4,64,512]{2,1,0:T(8,128)(2,1)S(1)} %get-tuple-element.282.refs_0_), channel_id=1, source_target_pairs={{0,16},{8,24},{16,0},{24,8},{1,17},{9,25},{17,1},{25,9},{2,18},{10... | collective-permute-start | bytes 786440 | tf_op jit(solution)/shard_map/ppermute | solution.py:639
  115.6 7.1 %collective-permute-start.27 = (bf16[4,64,512]{2,1,0:T(8,128)(2,1)S(1)}, bf16[4,64,512]{2,1,0:T(8,128)(2,1)S(1)}, u32[]{:S(2)}, u32[]{:S(2)}) collective-permute-start(bf16[4,64,512]{2,1,0:T(8,128)(2,1)S(1)} %get-tuple-element.283.refs_2_), channel_id=1, source_target_pairs={{0,8},{8,0},{16,24},{24,16},{1,9},{9,1},{17,25},{25,17},{2,10},{10... | collective-permute-start | bytes 786440 | tf_op jit(solution)/shard_map/ppermute | solution.py:639
  116.6 6.2 %collective-permute-start.28 = (bf16[80,512]{1,0:T(8,128)(2,1)S(1)}, bf16[80,512]{1,0:T(8,128)(2,1)S(1)}, u32[]{:S(2)}, u32[]{:S(2)}) collective-permute-start(bf16[80,512]{1,0:T(8,128)(2,1)S(1)} %get-tuple-element.284.refs_4_), channel_id=1, source_target_pairs={{0,4},{1,5},{2,6},{3,7},{4,0},{5,1},{6,2},{7,3},{8,12},{9,13},{10,... | collective-permute-start | bytes 245768 | tf_op jit(solution)/shard_map/ppermute | solution.py:639
  123.0 10.2 %collective-permute-start.32 = (bf16[8,64,512]{2,1,0:T(8,128)(2,1)S(1)}, bf16[8,64,512]{2,1,0:T(8,128)(2,1)S(1)}, u32[]{:S(2)}, u32[]{:S(2)}) collective-permute-start(bf16[8,64,512]{2,1,0:T(8,128)(2,1)S(1)} %get-tuple-element.304.refs_1_), channel_id=1, source_target_pairs={{0,8},{8,0},{16,24},{24,16},{1,9},{9,1},{17,25},{25,17},{2,10},{10... | collective-permute-start | bytes 1572872 | tf_op jit(solution)/shard_map/ppermute | solution.py:639
  124.0 9.6 %collective-permute-start.33 = (bf16[8,64,512]{2,1,0:T(8,128)(2,1)S(1)}, bf16[8,64,512]{2,1,0:T(8,128)(2,1)S(1)}, u32[]{:S(2)}, u32[]{:S(2)}) collective-permute-start(bf16[8,64,512]{2,1,0:T(8,128)(2,1)S(1)} %get-tuple-element.305.refs_3_), channel_id=1, source_target_pairs={{0,16},{8,24},{16,0},{24,8},{1,17},{9,25},{17,1},{25,9},{2,18},{10... | collective-permute-start | bytes 1572872 | tf_op jit(solution)/shard_map/ppermute | solution.py:639
  125.5 16.1 %collective-permute-start.30 = (bf16[3,128,512]{2,1,0:T(8,128)(2,1)S(1)}, bf16[3,128,512]{2,1,0:T(8,128)(2,1)S(1)}, u32[]{:S(2)}, u32[]{:S(2)}) collective-permute-start(bf16[3,128,512]{2,1,0:T(8,128)(2,1)S(1)} %get-tuple-element.292.refs_6_), channel_id=1, source_target_pairs={{0,4},{1,5},{2,6},{3,7},{4,0},{5,1},{6,2},{7,3},{8,12},{9,13},{10,... | collective-permute-start | bytes 1179656 | tf_op jit(solution)/shard_map/ppermute | solution.py:639
  128.1 7.9 %collective-permute-start.31 = (bf16[2,80,512]{2,1,0:T(8,128)(2,1)S(1)}, bf16[2,80,512]{2,1,0:T(8,128)(2,1)S(1)}, u32[]{:S(2)}, u32[]{:S(2)}) collective-permute-start(bf16[2,80,512]{2,1,0:T(8,128)(2,1)S(1)} %get-tuple-element.289.refs_0_), channel_id=1, source_target_pairs={{0,2},{1,3},{2,0},{3,1},{4,6},{5,7},{6,4},{7,5},{8,10},{9,11},{10,... | collective-permute-start | bytes 491528 | tf_op jit(solution)/shard_map/ppermute | solution.py:639
  136.2 6.1 %collective-permute-start.35 = (bf16[144,512]{1,0:T(8,128)(2,1)S(1)}, bf16[144,512]{1,0:T(8,128)(2,1)S(1)}, u32[]{:S(2)}, u32[]{:S(2)}) collective-permute-start(bf16[144,512]{1,0:T(8,128)(2,1)S(1)} %get-tuple-element.297.refs_2_), channel_id=1, source_target_pairs={{0,8},{8,0},{16,24},{24,16},{1,9},{9,1},{17,25},{25,17},{2,10},{10... | collective-permute-start | bytes 442376 | tf_op jit(solution)/shard_map/ppermute | solution.py:639
  142.9 7.2 %collective-permute-start.39 = (bf16[8,64,512]{2,1,0:T(8,128)(2,1)S(1)}, bf16[8,64,512]{2,1,0:T(8,128)(2,1)S(1)}, u32[]{:S(2)}, u32[]{:S(2)}) collective-permute-start(bf16[8,64,512]{2,1,0:T(8,128)(2,1)S(1)} %collective-permute-done.32.refs_1_), channel_id=1, source_target_pairs={{0,1},{1,0},{2,3},{3,2},{4,5},{5,4},{6,7},{7,6},{8,9},{9,8},{10,11... | collective-permute-start | bytes 1572872 | tf_op jit(solution)/shard_map/ppermute | solution.py:639
  143.0 7.2 %collective-permute-start.40 = (bf16[8,64,512]{2,1,0:T(8,128)(2,1)S(1)}, bf16[8,64,512]{2,1,0:T(8,128)(2,1)S(1)}, u32[]{:S(2)}, u32[]{:S(2)}) collective-permute-start(bf16[8,64,512]{2,1,0:T(8,128)(2,1)S(1)} %collective-permute-done.33.refs_3_), channel_id=1, source_target_pairs={{0,1},{1,0},{2,3},{3,2},{4,5},{5,4},{6,7},{7,6},{8,9},{9,8},{10,11... | collective-permute-start | bytes 1572872 | tf_op jit(solution)/shard_map/ppermute | solution.py:639
  143.5 11.8 %collective-permute-start.38 = (bf16[3,128,512]{2,1,0:T(8,128)(2,1)S(1)}, bf16[3,128,512]{2,1,0:T(8,128)(2,1)S(1)}, u32[]{:S(2)}, u32[]{:S(2)}) collective-permute-start(bf16[3,128,512]{2,1,0:T(8,128)(2,1)S(1)} %get-tuple-element.301.refs_4_), channel_id=1, source_target_pairs={{0,2},{1,3},{2,0},{3,1},{4,6},{5,7},{6,4},{7,5},{8,10},{9,11},{10,... | collective-permute-start | bytes 1179656 | tf_op jit(solution)/shard_map/ppermute | solution.py:639
  145.9 9.4 %collective-permute-start.37 = (bf16[272,512]{1,0:T(8,128)(2,1)S(1)}, bf16[272,512]{1,0:T(8,128)(2,1)S(1)}, u32[]{:S(2)}, u32[]{:S(2)}) collective-permute-start(bf16[272,512]{1,0:T(8,128)(2,1)S(1)} %get-tuple-element.322.refs_5_), channel_id=1, source_target_pairs={{0,16},{8,24},{16,0},{24,8},{1,17},{9,25},{17,1},{25,9},{2,18},{10... | collective-permute-start | bytes 835592 | tf_op jit(solution)/shard_map/ppermute | solution.py:639
  146.4 8.9 %collective-permute-start.36 = (bf16[256,512]{1,0:T(8,128)(2,1)S(1)}, bf16[256,512]{1,0:T(8,128)(2,1)S(1)}, u32[]{:S(2)}, u32[]{:S(2)}) collective-permute-start(bf16[256,512]{1,0:T(8,128)(2,1)S(1)} %get-tuple-element.320.refs_1_), channel_id=1, source_target_pairs={{0,8},{8,0},{16,24},{24,16},{1,9},{9,1},{17,25},{25,17},{2,10},{10... | collective-permute-start | bytes 786440 | tf_op jit(solution)/shard_map/ppermute | solution.py:639
  (29 other events, 136.7 us)

commit v3 on v2

--- a/solution.py
+++ b/solution.py
@@ -952,7 +952,6 @@
         ),
     )
     one_far, two_far = exchange(one_near, *bit_x), exchange(two_near, *bit_y)
-    d_near, u_near = chain.hold(d_near, u_near)
     d_near_o, u_near_o = chain.hold(*other_core(d_near, u_near))
     grad_down, grad_up = unpack(False, d_near, d_near_o, u_near, u_near_o, [])
     d_far_o, u_far_o = chain.hold(*other_core(d_far, u_far))

time: 164 us -> 162 us (0.988)
  waiting for transfers between devices: 52.5 us -> 50.3 us
    ppermute x47, waiting for transfers between devices: 52.5 us -> 50.3 us  [exchange(): return lax.ppermute(array, axis, [(i, i ^ mask) for i in range(count)])]
  transfers between devices with their start and end apart: 47 -> 47, of which waited for: 21 -> 20; matrix products, arithmetic and copies ran while one was open for 3% -> 3% of each run, Pallas kernels for 26% -> 26%
where the time goes in v3:
time: 162 us; the launch traced here: 159 us
  Pallas kernels  52.3 us (32%)
  waiting for transfers between devices  50.3 us (31%)
  starting transfers between devices  49.4 us (30%)
  local copies, waits for them, and re-layouts  4.48 us (3%)
  between operations  1.62 us (1%)
    pallas_call x24, Pallas kernels, call(): pl.pallas_call(body_of, grid=grid, in_specs=[SMEM] * scalars + (specs or...  52.3 us
    ppermute x47, waiting for transfers between devices, exchange(): return lax.ppermute(array, axis, [(i, i ^ mask) for i in range(count)])  50.3 us
    ppermute x47, starting transfers between devices, exchange(): return lax.ppermute(array, axis, [(i, i ^ mask) for i in range(count)])  49.4 us
  transfers between devices with their start and end apart: 47, of which 20 were waited for; matrix products, arithmetic and copies ran while one was open for 3% of the time, Pallas kernels for 26%

profile of v3, /device:TPU:0, one launch (start us, length us, event | category | flops | bytes accessed | tf_op | source)
XLA Modules:
  0.0 159.3 jit_solution(790709853240613923)
XLA Ops:
  1.2 3.7 %collective-permute-start = (bf16[3,128,512]{2,1,0:T(8,128)(2,1)}, bf16[3,128,512]{2,1,0:T(8,128)(2,1)S(1)}, u32[]{:S(2)}, u32[]{:S(2)}) collective-permute-start(bf16[3,128,512]{2,1,0:T(8,128)(2,1)} %refs_1_.8), channel_id=1, source_target_pairs={{0,4},{1,5},{2,6},{3,7},{4,0},{5,1},{6,2},{7,3},{8,12},{9,13},{10,... | collective-permute-start | bytes 1179656 | tf_op jit(solution)/shard_map/ppermute | solution.py:639
  6.5 1.9 %dynamic-slice_bitcast_fusion = (bf16[1,512,256]{2,1,0:T(8,128)(2,1)}, bf16[1,512,256]{2,1,0:T(8,128)(2,1)}) fusion(bf16[512,512]{1,0:T(8,128)(2,1)} %param.25, s32[]{:T(128)S(6)} %select_n.39, bf16[512,512]{1,0:T(8,128)(2,1)} %param.24), kind=kLoop, calls=%fused_computation.1 | loop fusion | bytes 1048580 | tf_op jit(solution)/shard_map/stack | solution.py:698
  10.7 3.5 %attend_chunk_0.1 = (bf16[3,256,256]{2,1,0:T(8,128)(2,1)S(1)}, bf16[3,256,256]{2,1,0:T(8,128)(2,1)S(1)}, bf16[3,256,256]{2,1,0:T(8,128)(2,1)S(1)}, bf16[3,512,25...) custom-call(s32[5]{0:T(128)S(1)} %stack.53.refs_0_, ...), custom_call_target="tpu_custom_call" | custom-call | flops 55000000 | tf_op jit(solution)/shard_map/attend_chunk_0/pallas_call | solution.py:611
  17.5 5.8 %collective-permute-done.refs_3_ = bf16[3,128,512]{2,1,0:T(8,128)(2,1)S(1)} collective-permute-done((bf16[3,128,512]{2,1,0:T(8,128)(2,1)}, bf16[3,128,512]{2,1,0:T(8,128)(2,1)S(1)}, u32[]{:S(2)}, u32[]{:S(2)}) %collective-permute-start) | collective-permute-done | bytes 393248 | tf_op jit(solution)/shard_map/ppermute | solution.py:639
  25.1 3.3 %attend_chunk_2.1 = (bf16[3,256,256]{2,1,0:T(8,128)(2,1)S(1)}, bf16[3,256,256]{2,1,0:T(8,128)(2,1)S(1)}, bf16[3,256,256]{2,1,0:T(8,128)(2,1)S(1)}, bf16[3,512,25...) custom-call(s32[5]{0:T(128)S(1)} %stack.53.refs_0_, ...), custom_call_target="tpu_custom_call" | custom-call | flops 55000000 | tf_op jit(solution)/shard_map/attend_chunk_2/pallas_call | solution.py:611
  28.4 3.3 %attend_chunk_1.1 = (bf16[3,256,256]{2,1,0:T(8,128)(2,1)S(1)}, bf16[3,256,256]{2,1,0:T(8,128)(2,1)S(1)}, bf16[3,256,256]{2,1,0:T(8,128)(2,1)S(1)}, bf16[3,512,25...) custom-call(s32[5]{0:T(128)S(1)} %stack.53.refs_0_, ...), custom_call_target="tpu_custom_call" | custom-call | flops 55000000 | tf_op jit(solution)/shard_map/attend_chunk_1/pallas_call | solution.py:611
  31.8 3.6 %collective-permute-done.2.refs_3_ = bf16[3,128,512]{2,1,0:T(8,128)(2,1)S(1)} collective-permute-done((bf16[3,128,512]{2,1,0:T(8,128)(2,1)S(1)}, bf16[3,128,512]{2,1,0:T(8,128)(2,1)S(1)}, u32[]{:S(2)}, u32[]{:S(2)}) %collective-permute-start.2) | collective-permute-done | bytes 393248 | tf_op jit(solution)/shard_map/ppermute | solution.py:639
  37.1 3.4 %attend_chunk_3.1 = (bf16[3,256,256]{2,1,0:T(8,128)(2,1)S(1)}, bf16[3,256,256]{2,1,0:T(8,128)(2,1)S(1)}, bf16[3,256,256]{2,1,0:T(8,128)(2,1)S(1)}, bf16[3,512,25...) custom-call(s32[5]{0:T(128)S(1)} %stack.53.refs_0_, ...), custom_call_target="tpu_custom_call" | custom-call | flops 55000000 | tf_op jit(solution)/shard_map/attend_chunk_3/pallas_call | solution.py:611
  42.0 3.4 %feed_forward_a.1 = (f32[384,512]{1,0:T(8,128)S(1)}, bf16[384,512]{1,0:T(8,128)(2,1)S(1)}, bf16[384,2560]{1,0:T(8,128)(2,1)S(1)}, f32[384,512]{1,0:T(8,128)S(1)}...) custom-call(s32[5]{0:T(128)S(1)} %stack.53.refs_0_, bf16[3,128,256]{2,1,0:T(8,128)(2,1)S(1)} %get-tuple-element.195.refs_1_, ...), custom_call_target="tpu_custom_call" | custom-call | flops 4400000000 | tf_op jit(solution)/shard_map/feed_forward_a/pallas_call | solution.py:611
  45.7 3.7 %feed_forward_b.1 = (bf16[3,128,512]{2,1,0:T(8,128)(2,1)}, bf16[384,1024]{1,0:T(8,128)(2,1)S(1)}, bf16[384,1024]{1,0:T(8,128)(2,1)S(1)}, f32[384,512]{1,0:T(8,12...) custom-call(s32[5]{0:T(128)S(1)} %stack.53.refs_0_, f32[384,512]{1,0:T(8,128)S(1)} %get-tuple-element.205.refs_1_, ...), custom_call_target="tpu_custom_call" | custom-call | flops 4400000000 | tf_op jit(solution)/shard_map/feed_forward_b/pallas_call | solution.py:611
  49.8 1.8 %feed_forward_grad_sent.1 = (bf16[8,64,512]{2,1,0:T(8,128)(2,1)S(1)}, bf16[8,64,512]{2,1,0:T(8,128)(2,1)S(1)}) custom-call(s32[5]{0:T(128)S(1)} %stack.53.refs_0_, bf16[384,1024]{1,0:T(8,128)(2,1)S(1)} %get-tuple-element.214.refs_1_, bf16[384,1024]{1,0:T(8,128)(2,1)S(1)} %get-tuple-element.215.refs_2_, ...), custom_call_target="tpu_custom_call" | custom-call | flops 3300000000 | tf_op jit(solution)/shard_map/feed_forward_grad_sent/pallas_call | solution.py:611
  54.8 1.8 %feed_forward_grad_kept.1 = (bf16[8,64,512]{2,1,0:T(8,128)(2,1)S(1)}, bf16[8,64,512]{2,1,0:T(8,128)(2,1)S(1)}) custom-call(s32[5]{0:T(128)S(1)} %stack.53.refs_0_, bf16[384,1024]{1,0:T(8,128)(2,1)S(1)} %get-tuple-element.214.refs_1_, bf16[384,1024]{1,0:T(8,128)(2,1)S(1)} %get-tuple-element.215.refs_2_, ...), custom_call_target="tpu_custom_call" | custom-call | flops 55000000 | tf_op jit(solution)/shard_map/feed_forward_grad_kept/pallas_call | solution.py:611
  56.6 9.8 %attend_back_1.1 = (bf16[4,128,512]{2,1,0:T(8,128)(2,1)S(1)}, bf16[4,128,512]{2,1,0:T(8,128)(2,1)S(1)}, bf16[4,128,512]{2,1,0:T(8,128)(2,1)S(1)}, bf16[4,128,512...) custom-call(s32[5]{0:T(128)S(1)} %stack.53.refs_0_, ...), custom_call_target="tpu_custom_call" | custom-call | flops 55000000 | tf_op jit(solution)/shard_map/attend_back_1/pallas_call | solution.py:611
  69.2 5.9 %attend_back_2.1 = (bf16[4,128,512]{2,1,0:T(8,128)(2,1)S(1)}, bf16[12,128,512]{2,1,0:T(8,128)(2,1)S(1)}, bf16[256,512]{1,0:T(8,128)(2,1)S(1)}, bf16[256,512]{1,0...) custom-call(s32[5]{0:T(128)S(1)} %stack.53.refs_0_, s32[3,4]{1,0:T(4,128)S(1)} %copy-done.3, ...), custom_call_target="tpu_custom_call" | custom-call | flops 55000000 | tf_op jit(solution)/shard_map/attend_back_2/pallas_call | solution.py:611
  79.2 5.6 %collective-permute-done.17.refs_3_ = bf16[256,512]{1,0:T(8,128)(2,1)S(1)} collective-permute-done((bf16[256,512]{1,0:T(8,128)(2,1)S(1)}, bf16[256,512]{1,0:T(8,128)(2,1)S(1)}, u32[]{:S(2)}, u32[]{:S(2)}) %collective-permute-start.17) | collective-permute-done | bytes 262176 | tf_op jit(solution)/shard_map/ppermute | solution.py:639
  86.8 2.2 %collective-permute-start.19 = (bf16[128,512]{1,0:T(8,128)(2,1)S(1)}, bf16[128,512]{1,0:T(8,128)(2,1)S(1)}, u32[]{:S(2)}, u32[]{:S(2)}) collective-permute-start(bf16[128,512]{1,0:T(8,128)(2,1)S(1)} %get-tuple-element.270), channel_id=1, source_target_pairs={{0,4},{1,5},{2,6},{3,7},{4,0},{5,1},{6,2},{7,3},{8,12},{9,13},{10,... | collective-permute-start | bytes 393224 | tf_op jit(solution)/shard_map/ppermute | solution.py:639
  90.5 4.2 %collective-permute-done.19.refs_1_ = bf16[128,512]{1,0:T(8,128)(2,1)S(1)} collective-permute-done((bf16[128,512]{1,0:T(8,128)(2,1)S(1)}, bf16[128,512]{1,0:T(8,128)(2,1)S(1)}, u32[]{:S(2)}, u32[]{:S(2)}) %collective-permute-start.19) | collective-permute-done | bytes 131104 | tf_op jit(solution)/shard_map/ppermute | solution.py:639
  96.0 2.6 %collective-permute-start.22 = (bf16[128,512]{1,0:T(8,128)(2,1)S(1)}, bf16[128,512]{1,0:T(8,128)(2,1)S(1)}, u32[]{:S(2)}, u32[]{:S(2)}) collective-permute-start(bf16[128,512]{1,0:T(8,128)(2,1)S(1)} %get-tuple-element.273.refs_0_), channel_id=1, source_target_pairs={{0,4},{1,5},{2,6},{3,7},{4,0},{5,1},{6,2},{7,3},{8,12},{9,13},{10,... | collective-permute-start | bytes 393224 | tf_op jit(solution)/shard_map/ppermute | solution.py:639
  98.6 4.4 %collective-permute-done.22.refs_1_ = bf16[128,512]{1,0:T(8,128)(2,1)S(1)} collective-permute-done((bf16[128,512]{1,0:T(8,128)(2,1)S(1)}, bf16[128,512]{1,0:T(8,128)(2,1)S(1)}, u32[]{:S(2)}, u32[]{:S(2)}) %collective-permute-start.22) | collective-permute-done | bytes 131104 | tf_op jit(solution)/shard_map/ppermute | solution.py:639
  103.1 2.0 %collective-permute-start.24 = (bf16[2,128,512]{2,1,0:T(8,128)(2,1)S(1)}, bf16[2,128,512]{2,1,0:T(8,128)(2,1)S(1)}, u32[]{:S(2)}, u32[]{:S(2)}) collective-permute-start(bf16[2,128,512]{2,1,0:T(8,128)(2,1)S(1)} %get-tuple-element.276.refs_0_), channel_id=1, source_target_pairs={{0,2},{1,3},{2,0},{3,1},{4,6},{5,7},{6,4},{7,5},{8,10},{9,11},{10,... | collective-permute-start | bytes 786440 | tf_op jit(solution)/shard_map/ppermute | solution.py:639
  105.1 2.0 %collective-permute-start.25 = (bf16[80,512]{1,0:T(8,128)(2,1)S(1)}, bf16[80,512]{1,0:T(8,128)(2,1)S(1)}, u32[]{:S(2)}, u32[]{:S(2)}) collective-permute-start(bf16[80,512]{1,0:T(8,128)(2,1)S(1)} %get-tuple-element.278.refs_8_), channel_id=1, source_target_pairs={{0,4},{1,5},{2,6},{3,7},{4,0},{5,1},{6,2},{7,3},{8,12},{9,13},{10,... | collective-permute-start | bytes 245768 | tf_op jit(solution)/shard_map/ppermute | solution.py:639
  107.1 4.2 %collective-permute-done.25.refs_3_ = bf16[80,512]{1,0:T(8,128)(2,1)S(1)} collective-permute-done((bf16[80,512]{1,0:T(8,128)(2,1)S(1)}, bf16[80,512]{1,0:T(8,128)(2,1)S(1)}, u32[]{:S(2)}, u32[]{:S(2)}) %collective-permute-start.25) | collective-permute-done | bytes 81952 | tf_op jit(solution)/shard_map/ppermute | solution.py:639
  111.6 2.5 %collective-permute-start.29 = (bf16[3,128,512]{2,1,0:T(8,128)(2,1)S(1)}, bf16[3,128,512]{2,1,0:T(8,128)(2,1)S(1)}, u32[]{:S(2)}, u32[]{:S(2)}) collective-permute-start(bf16[3,128,512]{2,1,0:T(8,128)(2,1)S(1)} %get-tuple-element.284.refs_11_), channel_id=1, source_target_pairs={{0,2},{1,3},{2,0},{3,1},{4,6},{5,7},{6,4},{7,5},{8,10},{9,11},{10,... | collective-permute-start | bytes 1179656 | tf_op jit(solution)/shard_map/ppermute | solution.py:639
  117.9 4.8 %collective-permute-done.29.refs_10_ = bf16[3,128,512]{2,1,0:T(8,128)(2,1)S(1)} collective-permute-done((bf16[3,128,512]{2,1,0:T(8,128)(2,1)S(1)}, bf16[3,128,512]{2,1,0:T(8,128)(2,1)S(1)}, u32[]{:S(2)}, u32[]{:S(2)}) %collective-permute-start.29) | collective-permute-done | bytes 393248 | tf_op jit(solution)/shard_map/ppermute | solution.py:639
  125.5 2.6 %collective-permute-start.30 = (bf16[3,128,512]{2,1,0:T(8,128)(2,1)S(1)}, bf16[3,128,512]{2,1,0:T(8,128)(2,1)S(1)}, u32[]{:S(2)}, u32[]{:S(2)}) collective-permute-start(bf16[3,128,512]{2,1,0:T(8,128)(2,1)S(1)} %get-tuple-element.289.refs_6_), channel_id=1, source_target_pairs={{0,4},{1,5},{2,6},{3,7},{4,0},{5,1},{6,2},{7,3},{8,12},{9,13},{10,... | collective-permute-start | bytes 1179656 | tf_op jit(solution)/shard_map/ppermute | solution.py:639
  129.0 4.1 %collective-permute-done.32.refs_1_ = bf16[8,64,512]{2,1,0:T(8,128)(2,1)S(1)} collective-permute-done((bf16[8,64,512]{2,1,0:T(8,128)(2,1)S(1)}, bf16[8,64,512]{2,1,0:T(8,128)(2,1)S(1)}, u32[]{:S(2)}, u32[]{:S(2)}) %collective-permute-start.32) | collective-permute-done | bytes 524320 | tf_op jit(solution)/shard_map/ppermute | solution.py:639
  133.7 2.4 %collective-permute-done.31.refs_1_ = bf16[2,80,512]{2,1,0:T(8,128)(2,1)S(1)} collective-permute-done((bf16[2,80,512]{2,1,0:T(8,128)(2,1)S(1)}, bf16[2,80,512]{2,1,0:T(8,128)(2,1)S(1)}, u32[]{:S(2)}, u32[]{:S(2)}) %collective-permute-start.31) | collective-permute-done | bytes 163872 | tf_op jit(solution)/shard_map/ppermute | solution.py:639
  137.8 3.8 %collective-permute-done.30.refs_7_ = bf16[3,128,512]{2,1,0:T(8,128)(2,1)S(1)} collective-permute-done((bf16[3,128,512]{2,1,0:T(8,128)(2,1)S(1)}, bf16[3,128,512]{2,1,0:T(8,128)(2,1)S(1)}, u32[]{:S(2)}, u32[]{:S(2)}) %collective-permute-start.30) | collective-permute-done | bytes 393248 | tf_op jit(solution)/shard_map/ppermute | solution.py:639
  142.1 2.4 %collective-permute-start.38 = (bf16[3,128,512]{2,1,0:T(8,128)(2,1)S(1)}, bf16[3,128,512]{2,1,0:T(8,128)(2,1)S(1)}, u32[]{:S(2)}, u32[]{:S(2)}) collective-permute-start(bf16[3,128,512]{2,1,0:T(8,128)(2,1)S(1)} %get-tuple-element.298.refs_4_), channel_id=1, source_target_pairs={{0,2},{1,3},{2,0},{3,1},{4,6},{5,7},{6,4},{7,5},{8,10},{9,11},{10,... | collective-permute-start | bytes 1179656 | tf_op jit(solution)/shard_map/ppermute | solution.py:639
  147.1 2.7 %unpack_feed_forward.2 = (f32[2048,512]{1,0:T(8,128)}, f32[512,2048]{1,0:T(8,128)}, f32[8,128]{1,0:T(8,128)S(1)}) custom-call(s32[5]{0:T(128)S(1)} %stack.53.refs_0_, bf16[8,64,512]{2,1,0:T(8,128)(2,1)S(1)} %get-tuple-element.287.refs_1_, bf16[8,64,512]{2,1,0:T(8,128)(2,1)S(1)} %collective-permute-done.41.refs_2_, ...), custom_call_target="tpu_custom_call" | custom-call | flops 110000000 | tf_op jit(solution)/shard_map/unpack_feed_forward/pallas_call | solution.py:611
  149.8 2.7 %unpack_feed_forward.3 = (f32[2048,512]{1,0:T(8,128)}, f32[512,2048]{1,0:T(8,128)}, f32[8,128]{1,0:T(8,128)S(1)}) custom-call(s32[5]{0:T(128)S(1)} %stack.53.refs_0_, bf16[8,64,512]{2,1,0:T(8,128)(2,1)S(1)} %collective-permute-done.32.refs_1_, bf16[8,64,512]{2,1,0:T(8,128)(2,1)S(1)} %collective-permute-done.39.refs_2_, ...), custom_call_target="tpu_custom_call", output_to_operand_aliasing={{0}: (5, {}), {1}: (6, {})} | custom-call | flops 110000000 | tf_op jit(solution)/shard_map/unpack_feed_forward/pallas_call | solution.py:611
  156.2 2.7 %unpack_attend.1 = (f32[512,512]{1,0:T(8,128)}, f32[512,512]{1,0:T(8,128)}, f32[512,512]{1,0:T(8,128)}, f32[512,512]{1,0:T(8,128)}, f32[1,512]{1,0:T(1,128)}, /*...) custom-call(s32[5]{0:T(128)S(1)} %stack.53.refs_0_, ...), custom_call_target="tpu_custom_call" | custom-call | flops 110000000 | tf_op jit(solution)/shard_map/unpack_attend/pallas_call | solution.py:611
  (120 shorter events, 44.8 us)
Async XLA Ops:
  0.7 10.0 %collective-permute-start.1 = (bf16[3,128,512]{2,1,0:T(8,128)(2,1)}, bf16[3,128,512]{2,1,0:T(8,128)(2,1)S(1)}, u32[]{:S(2)}, u32[]{:S(2)}) collective-permute-start(bf16[3,128,512]{2,1,0:T(8,128)(2,1)} %refs_1_.8), channel_id=1, source_target_pairs={{0,1},{1,0},{2,3},{3,2},{4,5},{5,4},{6,7},{7,6},{8,9},{9,8},{10,11... | collective-permute-start | bytes 1179656 | tf_op jit(solution)/shard_map/ppermute | solution.py:639
  1.2 22.1 %collective-permute-start = (bf16[3,128,512]{2,1,0:T(8,128)(2,1)}, bf16[3,128,512]{2,1,0:T(8,128)(2,1)S(1)}, u32[]{:S(2)}, u32[]{:S(2)}) collective-permute-start(bf16[3,128,512]{2,1,0:T(8,128)(2,1)} %refs_1_.8), channel_id=1, source_target_pairs={{0,4},{1,5},{2,6},{3,7},{4,0},{5,1},{6,2},{7,3},{8,12},{9,13},{10,... | collective-permute-start | bytes 1179656 | tf_op jit(solution)/shard_map/ppermute | solution.py:639
  4.9 19.0 %collective-permute-start.3 = (bf16[3,128,512]{2,1,0:T(8,128)(2,1)}, bf16[3,128,512]{2,1,0:T(8,128)(2,1)S(1)}, u32[]{:S(2)}, u32[]{:S(2)}) collective-permute-start(bf16[3,128,512]{2,1,0:T(8,128)(2,1)} %refs_1_.8), channel_id=1, source_target_pairs={{0,2},{1,3},{2,0},{3,1},{4,6},{5,7},{6,4},{7,5},{8,10},{9,11},{10,... | collective-permute-start | bytes 1179656 | tf_op jit(solution)/shard_map/ppermute | solution.py:639
  23.9 11.5 %collective-permute-start.2 = (bf16[3,128,512]{2,1,0:T(8,128)(2,1)S(1)}, bf16[3,128,512]{2,1,0:T(8,128)(2,1)S(1)}, u32[]{:S(2)}, u32[]{:S(2)}) collective-permute-start(bf16[3,128,512]{2,1,0:T(8,128)(2,1)S(1)} %collective-permute-done.refs_3_), channel_id=1, source_target_pairs={{0,2},{1,3},{2,0},{3,1},{4,6},{5,7},{6,4},{7,5},{8,10},{9,11},{10,... | collective-permute-start | bytes 1179656 | tf_op jit(solution)/shard_map/ppermute | solution.py:639
  51.6 14.8 %collective-permute-start.11 = (bf16[8,64,512]{2,1,0:T(8,128)(2,1)S(1)}, bf16[8,64,512]{2,1,0:T(8,128)(2,1)S(1)}, u32[]{:S(2)}, u32[]{:S(2)}) collective-permute-start(bf16[8,64,512]{2,1,0:T(8,128)(2,1)S(1)} %get-tuple-element.239.refs_7_), channel_id=1, source_target_pairs={{0,8},{8,0},{16,24},{24,16},{1,9},{9,1},{17,25},{25,17},{2,10},{10... | collective-permute-start | bytes 1572872 | tf_op jit(solution)/shard_map/ppermute | solution.py:639
  53.2 13.7 %collective-permute-start.12 = (bf16[8,64,512]{2,1,0:T(8,128)(2,1)S(1)}, bf16[8,64,512]{2,1,0:T(8,128)(2,1)S(1)}, u32[]{:S(2)}, u32[]{:S(2)}) collective-permute-start(bf16[8,64,512]{2,1,0:T(8,128)(2,1)S(1)} %get-tuple-element.252), channel_id=1, source_target_pairs={{0,16},{8,24},{16,0},{24,8},{1,17},{9,25},{17,1},{25,9},{2,18},{10... | collective-permute-start | bytes 1572872 | tf_op jit(solution)/shard_map/ppermute | solution.py:639
  67.1 8.0 %collective-permute-start.13 = (bf16[4,64,512]{2,1,0:T(8,128)(2,1)S(1)}, bf16[4,64,512]{2,1,0:T(8,128)(2,1)S(1)}, u32[]{:S(2)}, u32[]{:S(2)}) collective-permute-start(bf16[4,64,512]{2,1,0:T(8,128)(2,1)S(1)} %get-tuple-element.258), channel_id=1, source_target_pairs={{0,16},{8,24},{16,0},{24,8},{1,17},{9,25},{17,1},{25,9},{2,18},{10... | collective-permute-start | bytes 786440 | tf_op jit(solution)/shard_map/ppermute | solution.py:639
  68.6 6.9 %collective-permute-start.14 = (bf16[4,64,512]{2,1,0:T(8,128)(2,1)S(1)}, bf16[4,64,512]{2,1,0:T(8,128)(2,1)S(1)}, u32[]{:S(2)}, u32[]{:S(2)}) collective-permute-start(bf16[4,64,512]{2,1,0:T(8,128)(2,1)S(1)} %get-tuple-element.253.refs_35_), channel_id=1, source_target_pairs={{0,8},{8,0},{16,24},{24,16},{1,9},{9,1},{17,25},{25,17},{2,10},{10... | collective-permute-start | bytes 786440 | tf_op jit(solution)/shard_map/ppermute | solution.py:639
  75.8 9.7 %collective-permute-start.18 = (bf16[272,512]{1,0:T(8,128)(2,1)S(1)}, bf16[272,512]{1,0:T(8,128)(2,1)S(1)}, u32[]{:S(2)}, u32[]{:S(2)}) collective-permute-start(bf16[272,512]{1,0:T(8,128)(2,1)S(1)} %get-tuple-element.267.refs_6_), channel_id=1, source_target_pairs={{0,16},{8,24},{16,0},{24,8},{1,17},{9,25},{17,1},{25,9},{2,18},{10... | collective-permute-start | bytes 835592 | tf_op jit(solution)/shard_map/ppermute | solution.py:639
  76.5 8.4 %collective-permute-start.17 = (bf16[256,512]{1,0:T(8,128)(2,1)S(1)}, bf16[256,512]{1,0:T(8,128)(2,1)S(1)}, u32[]{:S(2)}, u32[]{:S(2)}) collective-permute-start(bf16[256,512]{1,0:T(8,128)(2,1)S(1)} %get-tuple-element.265), channel_id=1, source_target_pairs={{0,8},{8,0},{16,24},{24,16},{1,9},{9,1},{17,25},{25,17},{2,10},{10... | collective-permute-start | bytes 786440 | tf_op jit(solution)/shard_map/ppermute | solution.py:639
  77.4 8.1 %collective-permute-start.16 = (bf16[2,128,512]{2,1,0:T(8,128)(2,1)S(1)}, bf16[2,128,512]{2,1,0:T(8,128)(2,1)S(1)}, u32[]{:S(2)}, u32[]{:S(2)}) collective-permute-start(bf16[2,128,512]{2,1,0:T(8,128)(2,1)S(1)} %get-tuple-element.268.refs_6_), channel_id=1, source_target_pairs={{0,2},{1,3},{2,0},{3,1},{4,6},{5,7},{6,4},{7,5},{8,10},{9,11},{10,... | collective-permute-start | bytes 786440 | tf_op jit(solution)/shard_map/ppermute | solution.py:639
  85.7 9.0 %collective-permute-start.21 = (bf16[144,512]{1,0:T(8,128)(2,1)S(1)}, bf16[144,512]{1,0:T(8,128)(2,1)S(1)}, u32[]{:S(2)}, u32[]{:S(2)}) collective-permute-start(bf16[144,512]{1,0:T(8,128)(2,1)S(1)} %get-tuple-element.272.refs_8_), channel_id=1, source_target_pairs={{0,8},{8,0},{16,24},{24,16},{1,9},{9,1},{17,25},{25,17},{2,10},{10... | collective-permute-start | bytes 442376 | tf_op jit(solution)/shard_map/ppermute | solution.py:639
  86.8 7.8 %collective-permute-start.19 = (bf16[128,512]{1,0:T(8,128)(2,1)S(1)}, bf16[128,512]{1,0:T(8,128)(2,1)S(1)}, u32[]{:S(2)}, u32[]{:S(2)}) collective-permute-start(bf16[128,512]{1,0:T(8,128)(2,1)S(1)} %get-tuple-element.270), channel_id=1, source_target_pairs={{0,4},{1,5},{2,6},{3,7},{4,0},{5,1},{6,2},{7,3},{8,12},{9,13},{10,... | collective-permute-start | bytes 393224 | tf_op jit(solution)/shard_map/ppermute | solution.py:639
  94.8 8.2 %collective-permute-start.23 = (bf16[2,80,512]{2,1,0:T(8,128)(2,1)S(1)}, bf16[2,80,512]{2,1,0:T(8,128)(2,1)S(1)}, u32[]{:S(2)}, u32[]{:S(2)}) collective-permute-start(bf16[2,80,512]{2,1,0:T(8,128)(2,1)S(1)} %get-tuple-element.275.refs_4_), channel_id=1, source_target_pairs={{0,2},{1,3},{2,0},{3,1},{4,6},{5,7},{6,4},{7,5},{8,10},{9,11},{10,... | collective-permute-start | bytes 491528 | tf_op jit(solution)/shard_map/ppermute | solution.py:639
  96.0 7.0 %collective-permute-start.22 = (bf16[128,512]{1,0:T(8,128)(2,1)S(1)}, bf16[128,512]{1,0:T(8,128)(2,1)S(1)}, u32[]{:S(2)}, u32[]{:S(2)}) collective-permute-start(bf16[128,512]{1,0:T(8,128)(2,1)S(1)} %get-tuple-element.273.refs_0_), channel_id=1, source_target_pairs={{0,4},{1,5},{2,6},{3,7},{4,0},{5,1},{6,2},{7,3},{8,12},{9,13},{10,... | collective-permute-start | bytes 393224 | tf_op jit(solution)/shard_map/ppermute | solution.py:639
  103.1 8.4 %collective-permute-start.24 = (bf16[2,128,512]{2,1,0:T(8,128)(2,1)S(1)}, bf16[2,128,512]{2,1,0:T(8,128)(2,1)S(1)}, u32[]{:S(2)}, u32[]{:S(2)}) collective-permute-start(bf16[2,128,512]{2,1,0:T(8,128)(2,1)S(1)} %get-tuple-element.276.refs_0_), channel_id=1, source_target_pairs={{0,2},{1,3},{2,0},{3,1},{4,6},{5,7},{6,4},{7,5},{8,10},{9,11},{10,... | collective-permute-start | bytes 786440 | tf_op jit(solution)/shard_map/ppermute | solution.py:639
  105.1 6.2 %collective-permute-start.25 = (bf16[80,512]{1,0:T(8,128)(2,1)S(1)}, bf16[80,512]{1,0:T(8,128)(2,1)S(1)}, u32[]{:S(2)}, u32[]{:S(2)}) collective-permute-start(bf16[80,512]{1,0:T(8,128)(2,1)S(1)} %get-tuple-element.278.refs_8_), channel_id=1, source_target_pairs={{0,4},{1,5},{2,6},{3,7},{4,0},{5,1},{6,2},{7,3},{8,12},{9,13},{10,... | collective-permute-start | bytes 245768 | tf_op jit(solution)/shard_map/ppermute | solution.py:639
  111.6 11.1 %collective-permute-start.29 = (bf16[3,128,512]{2,1,0:T(8,128)(2,1)S(1)}, bf16[3,128,512]{2,1,0:T(8,128)(2,1)S(1)}, u32[]{:S(2)}, u32[]{:S(2)}) collective-permute-start(bf16[3,128,512]{2,1,0:T(8,128)(2,1)S(1)} %get-tuple-element.284.refs_11_), channel_id=1, source_target_pairs={{0,2},{1,3},{2,0},{3,1},{4,6},{5,7},{6,4},{7,5},{8,10},{9,11},{10,... | collective-permute-start | bytes 1179656 | tf_op jit(solution)/shard_map/ppermute | solution.py:639
  114.1 8.6 %collective-permute-start.26 = (bf16[4,64,512]{2,1,0:T(8,128)(2,1)S(1)}, bf16[4,64,512]{2,1,0:T(8,128)(2,1)S(1)}, u32[]{:S(2)}, u32[]{:S(2)}) collective-permute-start(bf16[4,64,512]{2,1,0:T(8,128)(2,1)S(1)} %get-tuple-element.279.refs_0_), channel_id=1, source_target_pairs={{0,16},{8,24},{16,0},{24,8},{1,17},{9,25},{17,1},{25,9},{2,18},{10... | collective-permute-start | bytes 786440 | tf_op jit(solution)/shard_map/ppermute | solution.py:639
  115.6 7.1 %collective-permute-start.27 = (bf16[4,64,512]{2,1,0:T(8,128)(2,1)S(1)}, bf16[4,64,512]{2,1,0:T(8,128)(2,1)S(1)}, u32[]{:S(2)}, u32[]{:S(2)}) collective-permute-start(bf16[4,64,512]{2,1,0:T(8,128)(2,1)S(1)} %get-tuple-element.280.refs_2_), channel_id=1, source_target_pairs={{0,8},{8,0},{16,24},{24,16},{1,9},{9,1},{17,25},{25,17},{2,10},{10... | collective-permute-start | bytes 786440 | tf_op jit(solution)/shard_map/ppermute | solution.py:639
  116.6 6.2 %collective-permute-start.28 = (bf16[80,512]{1,0:T(8,128)(2,1)S(1)}, bf16[80,512]{1,0:T(8,128)(2,1)S(1)}, u32[]{:S(2)}, u32[]{:S(2)}) collective-permute-start(bf16[80,512]{1,0:T(8,128)(2,1)S(1)} %get-tuple-element.281.refs_4_), channel_id=1, source_target_pairs={{0,4},{1,5},{2,6},{3,7},{4,0},{5,1},{6,2},{7,3},{8,12},{9,13},{10,... | collective-permute-start | bytes 245768 | tf_op jit(solution)/shard_map/ppermute | solution.py:639
  123.0 10.2 %collective-permute-start.32 = (bf16[8,64,512]{2,1,0:T(8,128)(2,1)S(1)}, bf16[8,64,512]{2,1,0:T(8,128)(2,1)S(1)}, u32[]{:S(2)}, u32[]{:S(2)}) collective-permute-start(bf16[8,64,512]{2,1,0:T(8,128)(2,1)S(1)} %get-tuple-element.287.refs_1_), channel_id=1, source_target_pairs={{0,8},{8,0},{16,24},{24,16},{1,9},{9,1},{17,25},{25,17},{2,10},{10... | collective-permute-start | bytes 1572872 | tf_op jit(solution)/shard_map/ppermute | solution.py:639
  124.0 9.6 %collective-permute-start.33 = (bf16[8,64,512]{2,1,0:T(8,128)(2,1)S(1)}, bf16[8,64,512]{2,1,0:T(8,128)(2,1)S(1)}, u32[]{:S(2)}, u32[]{:S(2)}) collective-permute-start(bf16[8,64,512]{2,1,0:T(8,128)(2,1)S(1)} %get-tuple-element.288.refs_3_), channel_id=1, source_target_pairs={{0,16},{8,24},{16,0},{24,8},{1,17},{9,25},{17,1},{25,9},{2,18},{10... | collective-permute-start | bytes 1572872 | tf_op jit(solution)/shard_map/ppermute | solution.py:639
  125.5 16.1 %collective-permute-start.30 = (bf16[3,128,512]{2,1,0:T(8,128)(2,1)S(1)}, bf16[3,128,512]{2,1,0:T(8,128)(2,1)S(1)}, u32[]{:S(2)}, u32[]{:S(2)}) collective-permute-start(bf16[3,128,512]{2,1,0:T(8,128)(2,1)S(1)} %get-tuple-element.289.refs_6_), channel_id=1, source_target_pairs={{0,4},{1,5},{2,6},{3,7},{4,0},{5,1},{6,2},{7,3},{8,12},{9,13},{10,... | collective-permute-start | bytes 1179656 | tf_op jit(solution)/shard_map/ppermute | solution.py:639
  128.1 7.9 %collective-permute-start.31 = (bf16[2,80,512]{2,1,0:T(8,128)(2,1)S(1)}, bf16[2,80,512]{2,1,0:T(8,128)(2,1)S(1)}, u32[]{:S(2)}, u32[]{:S(2)}) collective-permute-start(bf16[2,80,512]{2,1,0:T(8,128)(2,1)S(1)} %get-tuple-element.286.refs_0_), channel_id=1, source_target_pairs={{0,2},{1,3},{2,0},{3,1},{4,6},{5,7},{6,4},{7,5},{8,10},{9,11},{10,... | collective-permute-start | bytes 491528 | tf_op jit(solution)/shard_map/ppermute | solution.py:639
  129.0 15.5 %collective-permute-start.41 = (bf16[8,64,512]{2,1,0:T(8,128)(2,1)S(1)}, bf16[8,64,512]{2,1,0:T(8,128)(2,1)S(1)}, u32[]{:S(2)}, u32[]{:S(2)}) collective-permute-start(bf16[8,64,512]{2,1,0:T(8,128)(2,1)S(1)} %get-tuple-element.287.refs_1_), channel_id=1, source_target_pairs={{0,1},{1,0},{2,3},{3,2},{4,5},{5,4},{6,7},{7,6},{8,9},{9,8},{10,11... | collective-permute-start | bytes 1572872 | tf_op jit(solution)/shard_map/ppermute | solution.py:639
  133.2 12.8 %collective-permute-start.42 = (bf16[8,64,512]{2,1,0:T(8,128)(2,1)S(1)}, bf16[8,64,512]{2,1,0:T(8,128)(2,1)S(1)}, u32[]{:S(2)}, u32[]{:S(2)}) collective-permute-start(bf16[8,64,512]{2,1,0:T(8,128)(2,1)S(1)} %get-tuple-element.288.refs_3_), channel_id=1, source_target_pairs={{0,1},{1,0},{2,3},{3,2},{4,5},{5,4},{6,7},{7,6},{8,9},{9,8},{10,11... | collective-permute-start | bytes 1572872 | tf_op jit(solution)/shard_map/ppermute | solution.py:639
  141.6 8.2 %collective-permute-start.39 = (bf16[8,64,512]{2,1,0:T(8,128)(2,1)S(1)}, bf16[8,64,512]{2,1,0:T(8,128)(2,1)S(1)}, u32[]{:S(2)}, u32[]{:S(2)}) collective-permute-start(bf16[8,64,512]{2,1,0:T(8,128)(2,1)S(1)} %collective-permute-done.32.refs_1_), channel_id=1, source_target_pairs={{0,1},{1,0},{2,3},{3,2},{4,5},{5,4},{6,7},{7,6},{8,9},{9,8},{10,11... | collective-permute-start | bytes 1572872 | tf_op jit(solution)/shard_map/ppermute | solution.py:639
  141.6 8.2 %collective-permute-start.40 = (bf16[8,64,512]{2,1,0:T(8,128)(2,1)S(1)}, bf16[8,64,512]{2,1,0:T(8,128)(2,1)S(1)}, u32[]{:S(2)}, u32[]{:S(2)}) collective-permute-start(bf16[8,64,512]{2,1,0:T(8,128)(2,1)S(1)} %collective-permute-done.33.refs_3_), channel_id=1, source_target_pairs={{0,1},{1,0},{2,3},{3,2},{4,5},{5,4},{6,7},{7,6},{8,9},{9,8},{10,11... | collective-permute-start | bytes 1572872 | tf_op jit(solution)/shard_map/ppermute | solution.py:639
  142.1 11.4 %collective-permute-start.38 = (bf16[3,128,512]{2,1,0:T(8,128)(2,1)S(1)}, bf16[3,128,512]{2,1,0:T(8,128)(2,1)S(1)}, u32[]{:S(2)}, u32[]{:S(2)}) collective-permute-start(bf16[3,128,512]{2,1,0:T(8,128)(2,1)S(1)} %get-tuple-element.298.refs_4_), channel_id=1, source_target_pairs={{0,2},{1,3},{2,0},{3,1},{4,6},{5,7},{6,4},{7,5},{8,10},{9,11},{10,... | collective-permute-start | bytes 1179656 | tf_op jit(solution)/shard_map/ppermute | solution.py:639
  144.5 9.0 %collective-permute-start.37 = (bf16[272,512]{1,0:T(8,128)(2,1)S(1)}, bf16[272,512]{1,0:T(8,128)(2,1)S(1)}, u32[]{:S(2)}, u32[]{:S(2)}) collective-permute-start(bf16[272,512]{1,0:T(8,128)(2,1)S(1)} %get-tuple-element.316.refs_5_), channel_id=1, source_target_pairs={{0,16},{8,24},{16,0},{24,8},{1,17},{9,25},{17,1},{25,9},{2,18},{10... | collective-permute-start | bytes 835592 | tf_op jit(solution)/shard_map/ppermute | solution.py:639
  146.0 7.5 %collective-permute-start.36 = (bf16[256,512]{1,0:T(8,128)(2,1)S(1)}, bf16[256,512]{1,0:T(8,128)(2,1)S(1)}, u32[]{:S(2)}, u32[]{:S(2)}) collective-permute-start(bf16[256,512]{1,0:T(8,128)(2,1)S(1)} %get-tuple-element.314.refs_1_), channel_id=1, source_target_pairs={{0,8},{8,0},{16,24},{24,16},{1,9},{9,1},{17,25},{25,17},{2,10},{10... | collective-permute-start | bytes 786440 | tf_op jit(solution)/shard_map/ppermute | solution.py:639
  (29 other events, 140.5 us)

commit v4 on v3

--- a/solution.py
+++ b/solution.py
@@ -295,9 +295,8 @@
     for place, row in enumerate(rows_here):
         at = row if whole else 0
         branch = jnp.concatenate([br_m[at], br_o[at]], axis=0)
-        do = nt(branch, wo[half_of(sp[0], half), :])
-        dot = do.T
-        do = do.astype(BF16)
+        do = nt(branch, wo[half_of(sp[0], half), :]).astype(BF16)
+        dot = do.astype(F32).T
         lane = lax.broadcasted_iota(jnp.int32, (chip, 2 * size), 1)
         head_at = at * heads
         out_t = jnp.concatenate([ot[head_at + h] for h in range(heads)], axis=0).astype(BF16)

time: 162 us -> 162 us (level)
  no operation moved by 1% of the time
where the time goes in v4:
time: 162 us; the launch traced here: 159 us
  Pallas kernels  52.4 us (32%)
  waiting for transfers between devices  50.3 us (31%)
  starting transfers between devices  49.4 us (30%)
  local copies, waits for them, and re-layouts  4.48 us (3%)
    pallas_call x24, Pallas kernels, call(): pl.pallas_call(body_of, grid=grid, in_specs=[SMEM] * scalars + (specs or...  52.4 us
    ppermute x47, waiting for transfers between devices, exchange(): return lax.ppermute(array, axis, [(i, i ^ mask) for i in range(count)])  50.3 us
    ppermute x47, starting transfers between devices, exchange(): return lax.ppermute(array, axis, [(i, i ^ mask) for i in range(count)])  49.4 us
  transfers between devices with their start and end apart: 47, of which 20 were waited for; matrix products, arithmetic and copies ran while one was open for 3% of the time, Pallas kernels for 26%

profile of v4, /device:TPU:0, one launch (start us, length us, event | category | flops | bytes accessed | tf_op | source)
XLA Modules:
  0.0 159.4 jit_solution(750229007793011931)
XLA Ops:
  1.2 3.7 %collective-permute-start = (bf16[3,128,512]{2,1,0:T(8,128)(2,1)}, bf16[3,128,512]{2,1,0:T(8,128)(2,1)S(1)}, u32[]{:S(2)}, u32[]{:S(2)}) collective-permute-start(bf16[3,128,512]{2,1,0:T(8,128)(2,1)} %refs_1_.8), channel_id=1, source_target_pairs={{0,4},{1,5},{2,6},{3,7},{4,0},{5,1},{6,2},{7,3},{8,12},{9,13},{10,... | collective-permute-start | bytes 1179656 | tf_op jit(solution)/shard_map/ppermute | solution.py:638
  6.5 1.9 %dynamic-slice_bitcast_fusion = (bf16[1,512,256]{2,1,0:T(8,128)(2,1)}, bf16[1,512,256]{2,1,0:T(8,128)(2,1)}) fusion(bf16[512,512]{1,0:T(8,128)(2,1)} %param.25, s32[]{:T(128)S(6)} %select_n.39, bf16[512,512]{1,0:T(8,128)(2,1)} %param.24), kind=kLoop, calls=%fused_computation.1 | loop fusion | bytes 1048580 | tf_op jit(solution)/shard_map/stack | solution.py:697
  10.7 3.5 %attend_chunk_0.1 = (bf16[3,256,256]{2,1,0:T(8,128)(2,1)S(1)}, bf16[3,256,256]{2,1,0:T(8,128)(2,1)S(1)}, bf16[3,256,256]{2,1,0:T(8,128)(2,1)S(1)}, bf16[3,512,25...) custom-call(s32[5]{0:T(128)S(1)} %stack.53.refs_0_, ...), custom_call_target="tpu_custom_call" | custom-call | flops 55000000 | tf_op jit(solution)/shard_map/attend_chunk_0/pallas_call | solution.py:610
  17.5 5.8 %collective-permute-done.refs_3_ = bf16[3,128,512]{2,1,0:T(8,128)(2,1)S(1)} collective-permute-done((bf16[3,128,512]{2,1,0:T(8,128)(2,1)}, bf16[3,128,512]{2,1,0:T(8,128)(2,1)S(1)}, u32[]{:S(2)}, u32[]{:S(2)}) %collective-permute-start) | collective-permute-done | bytes 393248 | tf_op jit(solution)/shard_map/ppermute | solution.py:638
  25.1 3.3 %attend_chunk_2.1 = (bf16[3,256,256]{2,1,0:T(8,128)(2,1)S(1)}, bf16[3,256,256]{2,1,0:T(8,128)(2,1)S(1)}, bf16[3,256,256]{2,1,0:T(8,128)(2,1)S(1)}, bf16[3,512,25...) custom-call(s32[5]{0:T(128)S(1)} %stack.53.refs_0_, ...), custom_call_target="tpu_custom_call" | custom-call | flops 55000000 | tf_op jit(solution)/shard_map/attend_chunk_2/pallas_call | solution.py:610
  28.4 3.3 %attend_chunk_1.1 = (bf16[3,256,256]{2,1,0:T(8,128)(2,1)S(1)}, bf16[3,256,256]{2,1,0:T(8,128)(2,1)S(1)}, bf16[3,256,256]{2,1,0:T(8,128)(2,1)S(1)}, bf16[3,512,25...) custom-call(s32[5]{0:T(128)S(1)} %stack.53.refs_0_, ...), custom_call_target="tpu_custom_call" | custom-call | flops 55000000 | tf_op jit(solution)/shard_map/attend_chunk_1/pallas_call | solution.py:610
  31.8 3.6 %collective-permute-done.2.refs_3_ = bf16[3,128,512]{2,1,0:T(8,128)(2,1)S(1)} collective-permute-done((bf16[3,128,512]{2,1,0:T(8,128)(2,1)S(1)}, bf16[3,128,512]{2,1,0:T(8,128)(2,1)S(1)}, u32[]{:S(2)}, u32[]{:S(2)}) %collective-permute-start.2) | collective-permute-done | bytes 393248 | tf_op jit(solution)/shard_map/ppermute | solution.py:638
  37.1 3.4 %attend_chunk_3.1 = (bf16[3,256,256]{2,1,0:T(8,128)(2,1)S(1)}, bf16[3,256,256]{2,1,0:T(8,128)(2,1)S(1)}, bf16[3,256,256]{2,1,0:T(8,128)(2,1)S(1)}, bf16[3,512,25...) custom-call(s32[5]{0:T(128)S(1)} %stack.53.refs_0_, ...), custom_call_target="tpu_custom_call" | custom-call | flops 55000000 | tf_op jit(solution)/shard_map/attend_chunk_3/pallas_call | solution.py:610
  42.0 3.4 %feed_forward_a.1 = (f32[384,512]{1,0:T(8,128)S(1)}, bf16[384,512]{1,0:T(8,128)(2,1)S(1)}, bf16[384,2560]{1,0:T(8,128)(2,1)S(1)}, f32[384,512]{1,0:T(8,128)S(1)}...) custom-call(s32[5]{0:T(128)S(1)} %stack.53.refs_0_, bf16[3,128,256]{2,1,0:T(8,128)(2,1)S(1)} %get-tuple-element.195.refs_1_, ...), custom_call_target="tpu_custom_call" | custom-call | flops 4400000000 | tf_op jit(solution)/shard_map/feed_forward_a/pallas_call | solution.py:610
  45.7 3.7 %feed_forward_b.1 = (bf16[3,128,512]{2,1,0:T(8,128)(2,1)}, bf16[384,1024]{1,0:T(8,128)(2,1)S(1)}, bf16[384,1024]{1,0:T(8,128)(2,1)S(1)}, f32[384,512]{1,0:T(8,12...) custom-call(s32[5]{0:T(128)S(1)} %stack.53.refs_0_, f32[384,512]{1,0:T(8,128)S(1)} %get-tuple-element.205.refs_1_, ...), custom_call_target="tpu_custom_call" | custom-call | flops 4400000000 | tf_op jit(solution)/shard_map/feed_forward_b/pallas_call | solution.py:610
  49.8 1.8 %feed_forward_grad_sent.1 = (bf16[8,64,512]{2,1,0:T(8,128)(2,1)S(1)}, bf16[8,64,512]{2,1,0:T(8,128)(2,1)S(1)}) custom-call(s32[5]{0:T(128)S(1)} %stack.53.refs_0_, bf16[384,1024]{1,0:T(8,128)(2,1)S(1)} %get-tuple-element.214.refs_1_, bf16[384,1024]{1,0:T(8,128)(2,1)S(1)} %get-tuple-element.215.refs_2_, ...), custom_call_target="tpu_custom_call" | custom-call | flops 3300000000 | tf_op jit(solution)/shard_map/feed_forward_grad_sent/pallas_call | solution.py:610
  54.8 1.8 %feed_forward_grad_kept.1 = (bf16[8,64,512]{2,1,0:T(8,128)(2,1)S(1)}, bf16[8,64,512]{2,1,0:T(8,128)(2,1)S(1)}) custom-call(s32[5]{0:T(128)S(1)} %stack.53.refs_0_, bf16[384,1024]{1,0:T(8,128)(2,1)S(1)} %get-tuple-element.214.refs_1_, bf16[384,1024]{1,0:T(8,128)(2,1)S(1)} %get-tuple-element.215.refs_2_, ...), custom_call_target="tpu_custom_call" | custom-call | flops 55000000 | tf_op jit(solution)/shard_map/feed_forward_grad_kept/pallas_call | solution.py:610
  56.6 9.8 %attend_back_1.1 = (bf16[4,128,512]{2,1,0:T(8,128)(2,1)S(1)}, bf16[4,128,512]{2,1,0:T(8,128)(2,1)S(1)}, bf16[4,128,512]{2,1,0:T(8,128)(2,1)S(1)}, bf16[4,128,512...) custom-call(s32[5]{0:T(128)S(1)} %stack.53.refs_0_, ...), custom_call_target="tpu_custom_call" | custom-call | flops 55000000 | tf_op jit(solution)/shard_map/attend_back_1/pallas_call | solution.py:610
  69.2 5.9 %attend_back_2.1 = (bf16[4,128,512]{2,1,0:T(8,128)(2,1)S(1)}, bf16[12,128,512]{2,1,0:T(8,128)(2,1)S(1)}, bf16[256,512]{1,0:T(8,128)(2,1)S(1)}, bf16[256,512]{1,0...) custom-call(s32[5]{0:T(128)S(1)} %stack.53.refs_0_, s32[3,4]{1,0:T(4,128)S(1)} %copy-done.3, ...), custom_call_target="tpu_custom_call" | custom-call | flops 55000000 | tf_op jit(solution)/shard_map/attend_back_2/pallas_call | solution.py:610
  79.2 5.6 %collective-permute-done.17.refs_3_ = bf16[256,512]{1,0:T(8,128)(2,1)S(1)} collective-permute-done((bf16[256,512]{1,0:T(8,128)(2,1)S(1)}, bf16[256,512]{1,0:T(8,128)(2,1)S(1)}, u32[]{:S(2)}, u32[]{:S(2)}) %collective-permute-start.17) | collective-permute-done | bytes 262176 | tf_op jit(solution)/shard_map/ppermute | solution.py:638
  86.8 2.2 %collective-permute-start.19 = (bf16[128,512]{1,0:T(8,128)(2,1)S(1)}, bf16[128,512]{1,0:T(8,128)(2,1)S(1)}, u32[]{:S(2)}, u32[]{:S(2)}) collective-permute-start(bf16[128,512]{1,0:T(8,128)(2,1)S(1)} %get-tuple-element.270), channel_id=1, source_target_pairs={{0,4},{1,5},{2,6},{3,7},{4,0},{5,1},{6,2},{7,3},{8,12},{9,13},{10,... | collective-permute-start | bytes 393224 | tf_op jit(solution)/shard_map/ppermute | solution.py:638
  90.5 4.2 %collective-permute-done.19.refs_1_ = bf16[128,512]{1,0:T(8,128)(2,1)S(1)} collective-permute-done((bf16[128,512]{1,0:T(8,128)(2,1)S(1)}, bf16[128,512]{1,0:T(8,128)(2,1)S(1)}, u32[]{:S(2)}, u32[]{:S(2)}) %collective-permute-start.19) | collective-permute-done | bytes 131104 | tf_op jit(solution)/shard_map/ppermute | solution.py:638
  96.0 2.6 %collective-permute-start.22 = (bf16[128,512]{1,0:T(8,128)(2,1)S(1)}, bf16[128,512]{1,0:T(8,128)(2,1)S(1)}, u32[]{:S(2)}, u32[]{:S(2)}) collective-permute-start(bf16[128,512]{1,0:T(8,128)(2,1)S(1)} %get-tuple-element.273.refs_0_), channel_id=1, source_target_pairs={{0,4},{1,5},{2,6},{3,7},{4,0},{5,1},{6,2},{7,3},{8,12},{9,13},{10,... | collective-permute-start | bytes 393224 | tf_op jit(solution)/shard_map/ppermute | solution.py:638
  98.6 4.4 %collective-permute-done.22.refs_1_ = bf16[128,512]{1,0:T(8,128)(2,1)S(1)} collective-permute-done((bf16[128,512]{1,0:T(8,128)(2,1)S(1)}, bf16[128,512]{1,0:T(8,128)(2,1)S(1)}, u32[]{:S(2)}, u32[]{:S(2)}) %collective-permute-start.22) | collective-permute-done | bytes 131104 | tf_op jit(solution)/shard_map/ppermute | solution.py:638
  103.1 2.0 %collective-permute-start.24 = (bf16[2,128,512]{2,1,0:T(8,128)(2,1)S(1)}, bf16[2,128,512]{2,1,0:T(8,128)(2,1)S(1)}, u32[]{:S(2)}, u32[]{:S(2)}) collective-permute-start(bf16[2,128,512]{2,1,0:T(8,128)(2,1)S(1)} %get-tuple-element.276.refs_0_), channel_id=1, source_target_pairs={{0,2},{1,3},{2,0},{3,1},{4,6},{5,7},{6,4},{7,5},{8,10},{9,11},{10,... | collective-permute-start | bytes 786440 | tf_op jit(solution)/shard_map/ppermute | solution.py:638
  105.1 2.0 %collective-permute-start.25 = (bf16[80,512]{1,0:T(8,128)(2,1)S(1)}, bf16[80,512]{1,0:T(8,128)(2,1)S(1)}, u32[]{:S(2)}, u32[]{:S(2)}) collective-permute-start(bf16[80,512]{1,0:T(8,128)(2,1)S(1)} %get-tuple-element.278.refs_8_), channel_id=1, source_target_pairs={{0,4},{1,5},{2,6},{3,7},{4,0},{5,1},{6,2},{7,3},{8,12},{9,13},{10,... | collective-permute-start | bytes 245768 | tf_op jit(solution)/shard_map/ppermute | solution.py:638
  107.1 4.2 %collective-permute-done.25.refs_3_ = bf16[80,512]{1,0:T(8,128)(2,1)S(1)} collective-permute-done((bf16[80,512]{1,0:T(8,128)(2,1)S(1)}, bf16[80,512]{1,0:T(8,128)(2,1)S(1)}, u32[]{:S(2)}, u32[]{:S(2)}) %collective-permute-start.25) | collective-permute-done | bytes 81952 | tf_op jit(solution)/shard_map/ppermute | solution.py:638
  111.6 2.5 %collective-permute-start.29 = (bf16[3,128,512]{2,1,0:T(8,128)(2,1)S(1)}, bf16[3,128,512]{2,1,0:T(8,128)(2,1)S(1)}, u32[]{:S(2)}, u32[]{:S(2)}) collective-permute-start(bf16[3,128,512]{2,1,0:T(8,128)(2,1)S(1)} %get-tuple-element.284.refs_11_), channel_id=1, source_target_pairs={{0,2},{1,3},{2,0},{3,1},{4,6},{5,7},{6,4},{7,5},{8,10},{9,11},{10,... | collective-permute-start | bytes 1179656 | tf_op jit(solution)/shard_map/ppermute | solution.py:638
  117.9 4.8 %collective-permute-done.29.refs_10_ = bf16[3,128,512]{2,1,0:T(8,128)(2,1)S(1)} collective-permute-done((bf16[3,128,512]{2,1,0:T(8,128)(2,1)S(1)}, bf16[3,128,512]{2,1,0:T(8,128)(2,1)S(1)}, u32[]{:S(2)}, u32[]{:S(2)}) %collective-permute-start.29) | collective-permute-done | bytes 393248 | tf_op jit(solution)/shard_map/ppermute | solution.py:638
  125.5 2.6 %collective-permute-start.30 = (bf16[3,128,512]{2,1,0:T(8,128)(2,1)S(1)}, bf16[3,128,512]{2,1,0:T(8,128)(2,1)S(1)}, u32[]{:S(2)}, u32[]{:S(2)}) collective-permute-start(bf16[3,128,512]{2,1,0:T(8,128)(2,1)S(1)} %get-tuple-element.289.refs_6_), channel_id=1, source_target_pairs={{0,4},{1,5},{2,6},{3,7},{4,0},{5,1},{6,2},{7,3},{8,12},{9,13},{10,... | collective-permute-start | bytes 1179656 | tf_op jit(solution)/shard_map/ppermute | solution.py:638
  129.1 4.1 %collective-permute-done.32.refs_1_ = bf16[8,64,512]{2,1,0:T(8,128)(2,1)S(1)} collective-permute-done((bf16[8,64,512]{2,1,0:T(8,128)(2,1)S(1)}, bf16[8,64,512]{2,1,0:T(8,128)(2,1)S(1)}, u32[]{:S(2)}, u32[]{:S(2)}) %collective-permute-start.32) | collective-permute-done | bytes 524320 | tf_op jit(solution)/shard_map/ppermute | solution.py:638
  133.5 2.6 %collective-permute-done.31.refs_1_ = bf16[2,80,512]{2,1,0:T(8,128)(2,1)S(1)} collective-permute-done((bf16[2,80,512]{2,1,0:T(8,128)(2,1)S(1)}, bf16[2,80,512]{2,1,0:T(8,128)(2,1)S(1)}, u32[]{:S(2)}, u32[]{:S(2)}) %collective-permute-start.31) | collective-permute-done | bytes 163872 | tf_op jit(solution)/shard_map/ppermute | solution.py:638
  137.9 3.8 %collective-permute-done.30.refs_7_ = bf16[3,128,512]{2,1,0:T(8,128)(2,1)S(1)} collective-permute-done((bf16[3,128,512]{2,1,0:T(8,128)(2,1)S(1)}, bf16[3,128,512]{2,1,0:T(8,128)(2,1)S(1)}, u32[]{:S(2)}, u32[]{:S(2)}) %collective-permute-start.30) | collective-permute-done | bytes 393248 | tf_op jit(solution)/shard_map/ppermute | solution.py:638
  142.2 2.1 %collective-permute-start.38 = (bf16[3,128,512]{2,1,0:T(8,128)(2,1)S(1)}, bf16[3,128,512]{2,1,0:T(8,128)(2,1)S(1)}, u32[]{:S(2)}, u32[]{:S(2)}) collective-permute-start(bf16[3,128,512]{2,1,0:T(8,128)(2,1)S(1)} %get-tuple-element.298.refs_4_), channel_id=1, source_target_pairs={{0,2},{1,3},{2,0},{3,1},{4,6},{5,7},{6,4},{7,5},{8,10},{9,11},{10,... | collective-permute-start | bytes 1179656 | tf_op jit(solution)/shard_map/ppermute | solution.py:638
  147.1 2.7 %unpack_feed_forward.2 = (f32[2048,512]{1,0:T(8,128)}, f32[512,2048]{1,0:T(8,128)}, f32[8,128]{1,0:T(8,128)S(1)}) custom-call(s32[5]{0:T(128)S(1)} %stack.53.refs_0_, bf16[8,64,512]{2,1,0:T(8,128)(2,1)S(1)} %get-tuple-element.287.refs_1_, bf16[8,64,512]{2,1,0:T(8,128)(2,1)S(1)} %collective-permute-done.41.refs_2_, ...), custom_call_target="tpu_custom_call" | custom-call | flops 110000000 | tf_op jit(solution)/shard_map/unpack_feed_forward/pallas_call | solution.py:610
  149.8 2.7 %unpack_feed_forward.3 = (f32[2048,512]{1,0:T(8,128)}, f32[512,2048]{1,0:T(8,128)}, f32[8,128]{1,0:T(8,128)S(1)}) custom-call(s32[5]{0:T(128)S(1)} %stack.53.refs_0_, bf16[8,64,512]{2,1,0:T(8,128)(2,1)S(1)} %collective-permute-done.32.refs_1_, bf16[8,64,512]{2,1,0:T(8,128)(2,1)S(1)} %collective-permute-done.39.refs_2_, ...), custom_call_target="tpu_custom_call", output_to_operand_aliasing={{0}: (5, {}), {1}: (6, {})} | custom-call | flops 110000000 | tf_op jit(solution)/shard_map/unpack_feed_forward/pallas_call | solution.py:610
  156.3 2.7 %unpack_attend.1 = (f32[512,512]{1,0:T(8,128)}, f32[512,512]{1,0:T(8,128)}, f32[512,512]{1,0:T(8,128)}, f32[512,512]{1,0:T(8,128)}, f32[1,512]{1,0:T(1,128)}, /*...) custom-call(s32[5]{0:T(128)S(1)} %stack.53.refs_0_, ...), custom_call_target="tpu_custom_call" | custom-call | flops 110000000 | tf_op jit(solution)/shard_map/unpack_attend/pallas_call | solution.py:610
  (120 shorter events, 44.8 us)
Async XLA Ops:
  0.7 10.0 %collective-permute-start.1 = (bf16[3,128,512]{2,1,0:T(8,128)(2,1)}, bf16[3,128,512]{2,1,0:T(8,128)(2,1)S(1)}, u32[]{:S(2)}, u32[]{:S(2)}) collective-permute-start(bf16[3,128,512]{2,1,0:T(8,128)(2,1)} %refs_1_.8), channel_id=1, source_target_pairs={{0,1},{1,0},{2,3},{3,2},{4,5},{5,4},{6,7},{7,6},{8,9},{9,8},{10,11... | collective-permute-start | bytes 1179656 | tf_op jit(solution)/shard_map/ppermute | solution.py:638
  1.2 22.1 %collective-permute-start = (bf16[3,128,512]{2,1,0:T(8,128)(2,1)}, bf16[3,128,512]{2,1,0:T(8,128)(2,1)S(1)}, u32[]{:S(2)}, u32[]{:S(2)}) collective-permute-start(bf16[3,128,512]{2,1,0:T(8,128)(2,1)} %refs_1_.8), channel_id=1, source_target_pairs={{0,4},{1,5},{2,6},{3,7},{4,0},{5,1},{6,2},{7,3},{8,12},{9,13},{10,... | collective-permute-start | bytes 1179656 | tf_op jit(solution)/shard_map/ppermute | solution.py:638
  4.9 19.0 %collective-permute-start.3 = (bf16[3,128,512]{2,1,0:T(8,128)(2,1)}, bf16[3,128,512]{2,1,0:T(8,128)(2,1)S(1)}, u32[]{:S(2)}, u32[]{:S(2)}) collective-permute-start(bf16[3,128,512]{2,1,0:T(8,128)(2,1)} %refs_1_.8), channel_id=1, source_target_pairs={{0,2},{1,3},{2,0},{3,1},{4,6},{5,7},{6,4},{7,5},{8,10},{9,11},{10,... | collective-permute-start | bytes 1179656 | tf_op jit(solution)/shard_map/ppermute | solution.py:638
  23.9 11.5 %collective-permute-start.2 = (bf16[3,128,512]{2,1,0:T(8,128)(2,1)S(1)}, bf16[3,128,512]{2,1,0:T(8,128)(2,1)S(1)}, u32[]{:S(2)}, u32[]{:S(2)}) collective-permute-start(bf16[3,128,512]{2,1,0:T(8,128)(2,1)S(1)} %collective-permute-done.refs_3_), channel_id=1, source_target_pairs={{0,2},{1,3},{2,0},{3,1},{4,6},{5,7},{6,4},{7,5},{8,10},{9,11},{10,... | collective-permute-start | bytes 1179656 | tf_op jit(solution)/shard_map/ppermute | solution.py:638
  51.6 14.8 %collective-permute-start.11 = (bf16[8,64,512]{2,1,0:T(8,128)(2,1)S(1)}, bf16[8,64,512]{2,1,0:T(8,128)(2,1)S(1)}, u32[]{:S(2)}, u32[]{:S(2)}) collective-permute-start(bf16[8,64,512]{2,1,0:T(8,128)(2,1)S(1)} %get-tuple-element.239.refs_7_), channel_id=1, source_target_pairs={{0,8},{8,0},{16,24},{24,16},{1,9},{9,1},{17,25},{25,17},{2,10},{10... | collective-permute-start | bytes 1572872 | tf_op jit(solution)/shard_map/ppermute | solution.py:638
  53.2 13.7 %collective-permute-start.12 = (bf16[8,64,512]{2,1,0:T(8,128)(2,1)S(1)}, bf16[8,64,512]{2,1,0:T(8,128)(2,1)S(1)}, u32[]{:S(2)}, u32[]{:S(2)}) collective-permute-start(bf16[8,64,512]{2,1,0:T(8,128)(2,1)S(1)} %get-tuple-element.252), channel_id=1, source_target_pairs={{0,16},{8,24},{16,0},{24,8},{1,17},{9,25},{17,1},{25,9},{2,18},{10... | collective-permute-start | bytes 1572872 | tf_op jit(solution)/shard_map/ppermute | solution.py:638
  67.1 8.0 %collective-permute-start.13 = (bf16[4,64,512]{2,1,0:T(8,128)(2,1)S(1)}, bf16[4,64,512]{2,1,0:T(8,128)(2,1)S(1)}, u32[]{:S(2)}, u32[]{:S(2)}) collective-permute-start(bf16[4,64,512]{2,1,0:T(8,128)(2,1)S(1)} %get-tuple-element.258), channel_id=1, source_target_pairs={{0,16},{8,24},{16,0},{24,8},{1,17},{9,25},{17,1},{25,9},{2,18},{10... | collective-permute-start | bytes 786440 | tf_op jit(solution)/shard_map/ppermute | solution.py:638
  68.6 6.9 %collective-permute-start.14 = (bf16[4,64,512]{2,1,0:T(8,128)(2,1)S(1)}, bf16[4,64,512]{2,1,0:T(8,128)(2,1)S(1)}, u32[]{:S(2)}, u32[]{:S(2)}) collective-permute-start(bf16[4,64,512]{2,1,0:T(8,128)(2,1)S(1)} %get-tuple-element.253.refs_35_), channel_id=1, source_target_pairs={{0,8},{8,0},{16,24},{24,16},{1,9},{9,1},{17,25},{25,17},{2,10},{10... | collective-permute-start | bytes 786440 | tf_op jit(solution)/shard_map/ppermute | solution.py:638
  75.8 9.7 %collective-permute-start.18 = (bf16[272,512]{1,0:T(8,128)(2,1)S(1)}, bf16[272,512]{1,0:T(8,128)(2,1)S(1)}, u32[]{:S(2)}, u32[]{:S(2)}) collective-permute-start(bf16[272,512]{1,0:T(8,128)(2,1)S(1)} %get-tuple-element.267.refs_6_), channel_id=1, source_target_pairs={{0,16},{8,24},{16,0},{24,8},{1,17},{9,25},{17,1},{25,9},{2,18},{10... | collective-permute-start | bytes 835592 | tf_op jit(solution)/shard_map/ppermute | solution.py:638
  76.5 8.4 %collective-permute-start.17 = (bf16[256,512]{1,0:T(8,128)(2,1)S(1)}, bf16[256,512]{1,0:T(8,128)(2,1)S(1)}, u32[]{:S(2)}, u32[]{:S(2)}) collective-permute-start(bf16[256,512]{1,0:T(8,128)(2,1)S(1)} %get-tuple-element.265), channel_id=1, source_target_pairs={{0,8},{8,0},{16,24},{24,16},{1,9},{9,1},{17,25},{25,17},{2,10},{10... | collective-permute-start | bytes 786440 | tf_op jit(solution)/shard_map/ppermute | solution.py:638
  77.5 8.1 %collective-permute-start.16 = (bf16[2,128,512]{2,1,0:T(8,128)(2,1)S(1)}, bf16[2,128,512]{2,1,0:T(8,128)(2,1)S(1)}, u32[]{:S(2)}, u32[]{:S(2)}) collective-permute-start(bf16[2,128,512]{2,1,0:T(8,128)(2,1)S(1)} %get-tuple-element.268.refs_6_), channel_id=1, source_target_pairs={{0,2},{1,3},{2,0},{3,1},{4,6},{5,7},{6,4},{7,5},{8,10},{9,11},{10,... | collective-permute-start | bytes 786440 | tf_op jit(solution)/shard_map/ppermute | solution.py:638
  85.7 9.0 %collective-permute-start.21 = (bf16[144,512]{1,0:T(8,128)(2,1)S(1)}, bf16[144,512]{1,0:T(8,128)(2,1)S(1)}, u32[]{:S(2)}, u32[]{:S(2)}) collective-permute-start(bf16[144,512]{1,0:T(8,128)(2,1)S(1)} %get-tuple-element.272.refs_8_), channel_id=1, source_target_pairs={{0,8},{8,0},{16,24},{24,16},{1,9},{9,1},{17,25},{25,17},{2,10},{10... | collective-permute-start | bytes 442376 | tf_op jit(solution)/shard_map/ppermute | solution.py:638
  86.8 7.8 %collective-permute-start.19 = (bf16[128,512]{1,0:T(8,128)(2,1)S(1)}, bf16[128,512]{1,0:T(8,128)(2,1)S(1)}, u32[]{:S(2)}, u32[]{:S(2)}) collective-permute-start(bf16[128,512]{1,0:T(8,128)(2,1)S(1)} %get-tuple-element.270), channel_id=1, source_target_pairs={{0,4},{1,5},{2,6},{3,7},{4,0},{5,1},{6,2},{7,3},{8,12},{9,13},{10,... | collective-permute-start | bytes 393224 | tf_op jit(solution)/shard_map/ppermute | solution.py:638
  94.8 8.2 %collective-permute-start.23 = (bf16[2,80,512]{2,1,0:T(8,128)(2,1)S(1)}, bf16[2,80,512]{2,1,0:T(8,128)(2,1)S(1)}, u32[]{:S(2)}, u32[]{:S(2)}) collective-permute-start(bf16[2,80,512]{2,1,0:T(8,128)(2,1)S(1)} %get-tuple-element.275.refs_4_), channel_id=1, source_target_pairs={{0,2},{1,3},{2,0},{3,1},{4,6},{5,7},{6,4},{7,5},{8,10},{9,11},{10,... | collective-permute-start | bytes 491528 | tf_op jit(solution)/shard_map/ppermute | solution.py:638
  96.0 7.0 %collective-permute-start.22 = (bf16[128,512]{1,0:T(8,128)(2,1)S(1)}, bf16[128,512]{1,0:T(8,128)(2,1)S(1)}, u32[]{:S(2)}, u32[]{:S(2)}) collective-permute-start(bf16[128,512]{1,0:T(8,128)(2,1)S(1)} %get-tuple-element.273.refs_0_), channel_id=1, source_target_pairs={{0,4},{1,5},{2,6},{3,7},{4,0},{5,1},{6,2},{7,3},{8,12},{9,13},{10,... | collective-permute-start | bytes 393224 | tf_op jit(solution)/shard_map/ppermute | solution.py:638
  103.1 8.4 %collective-permute-start.24 = (bf16[2,128,512]{2,1,0:T(8,128)(2,1)S(1)}, bf16[2,128,512]{2,1,0:T(8,128)(2,1)S(1)}, u32[]{:S(2)}, u32[]{:S(2)}) collective-permute-start(bf16[2,128,512]{2,1,0:T(8,128)(2,1)S(1)} %get-tuple-element.276.refs_0_), channel_id=1, source_target_pairs={{0,2},{1,3},{2,0},{3,1},{4,6},{5,7},{6,4},{7,5},{8,10},{9,11},{10,... | collective-permute-start | bytes 786440 | tf_op jit(solution)/shard_map/ppermute | solution.py:638
  105.1 6.2 %collective-permute-start.25 = (bf16[80,512]{1,0:T(8,128)(2,1)S(1)}, bf16[80,512]{1,0:T(8,128)(2,1)S(1)}, u32[]{:S(2)}, u32[]{:S(2)}) collective-permute-start(bf16[80,512]{1,0:T(8,128)(2,1)S(1)} %get-tuple-element.278.refs_8_), channel_id=1, source_target_pairs={{0,4},{1,5},{2,6},{3,7},{4,0},{5,1},{6,2},{7,3},{8,12},{9,13},{10,... | collective-permute-start | bytes 245768 | tf_op jit(solution)/shard_map/ppermute | solution.py:638
  111.6 11.1 %collective-permute-start.29 = (bf16[3,128,512]{2,1,0:T(8,128)(2,1)S(1)}, bf16[3,128,512]{2,1,0:T(8,128)(2,1)S(1)}, u32[]{:S(2)}, u32[]{:S(2)}) collective-permute-start(bf16[3,128,512]{2,1,0:T(8,128)(2,1)S(1)} %get-tuple-element.284.refs_11_), channel_id=1, source_target_pairs={{0,2},{1,3},{2,0},{3,1},{4,6},{5,7},{6,4},{7,5},{8,10},{9,11},{10,... | collective-permute-start | bytes 1179656 | tf_op jit(solution)/shard_map/ppermute | solution.py:638
  114.1 8.6 %collective-permute-start.26 = (bf16[4,64,512]{2,1,0:T(8,128)(2,1)S(1)}, bf16[4,64,512]{2,1,0:T(8,128)(2,1)S(1)}, u32[]{:S(2)}, u32[]{:S(2)}) collective-permute-start(bf16[4,64,512]{2,1,0:T(8,128)(2,1)S(1)} %get-tuple-element.279.refs_0_), channel_id=1, source_target_pairs={{0,16},{8,24},{16,0},{24,8},{1,17},{9,25},{17,1},{25,9},{2,18},{10... | collective-permute-start | bytes 786440 | tf_op jit(solution)/shard_map/ppermute | solution.py:638
  115.6 7.1 %collective-permute-start.27 = (bf16[4,64,512]{2,1,0:T(8,128)(2,1)S(1)}, bf16[4,64,512]{2,1,0:T(8,128)(2,1)S(1)}, u32[]{:S(2)}, u32[]{:S(2)}) collective-permute-start(bf16[4,64,512]{2,1,0:T(8,128)(2,1)S(1)} %get-tuple-element.280.refs_2_), channel_id=1, source_target_pairs={{0,8},{8,0},{16,24},{24,16},{1,9},{9,1},{17,25},{25,17},{2,10},{10... | collective-permute-start | bytes 786440 | tf_op jit(solution)/shard_map/ppermute | solution.py:638
  116.6 6.1 %collective-permute-start.28 = (bf16[80,512]{1,0:T(8,128)(2,1)S(1)}, bf16[80,512]{1,0:T(8,128)(2,1)S(1)}, u32[]{:S(2)}, u32[]{:S(2)}) collective-permute-start(bf16[80,512]{1,0:T(8,128)(2,1)S(1)} %get-tuple-element.281.refs_4_), channel_id=1, source_target_pairs={{0,4},{1,5},{2,6},{3,7},{4,0},{5,1},{6,2},{7,3},{8,12},{9,13},{10,... | collective-permute-start | bytes 245768 | tf_op jit(solution)/shard_map/ppermute | solution.py:638
  123.0 10.2 %collective-permute-start.32 = (bf16[8,64,512]{2,1,0:T(8,128)(2,1)S(1)}, bf16[8,64,512]{2,1,0:T(8,128)(2,1)S(1)}, u32[]{:S(2)}, u32[]{:S(2)}) collective-permute-start(bf16[8,64,512]{2,1,0:T(8,128)(2,1)S(1)} %get-tuple-element.287.refs_1_), channel_id=1, source_target_pairs={{0,8},{8,0},{16,24},{24,16},{1,9},{9,1},{17,25},{25,17},{2,10},{10... | collective-permute-start | bytes 1572872 | tf_op jit(solution)/shard_map/ppermute | solution.py:638
  123.9 9.6 %collective-permute-start.33 = (bf16[8,64,512]{2,1,0:T(8,128)(2,1)S(1)}, bf16[8,64,512]{2,1,0:T(8,128)(2,1)S(1)}, u32[]{:S(2)}, u32[]{:S(2)}) collective-permute-start(bf16[8,64,512]{2,1,0:T(8,128)(2,1)S(1)} %get-tuple-element.288.refs_3_), channel_id=1, source_target_pairs={{0,16},{8,24},{16,0},{24,8},{1,17},{9,25},{17,1},{25,9},{2,18},{10... | collective-permute-start | bytes 1572872 | tf_op jit(solution)/shard_map/ppermute | solution.py:638
  125.5 16.1 %collective-permute-start.30 = (bf16[3,128,512]{2,1,0:T(8,128)(2,1)S(1)}, bf16[3,128,512]{2,1,0:T(8,128)(2,1)S(1)}, u32[]{:S(2)}, u32[]{:S(2)}) collective-permute-start(bf16[3,128,512]{2,1,0:T(8,128)(2,1)S(1)} %get-tuple-element.289.refs_6_), channel_id=1, source_target_pairs={{0,4},{1,5},{2,6},{3,7},{4,0},{5,1},{6,2},{7,3},{8,12},{9,13},{10,... | collective-permute-start | bytes 1179656 | tf_op jit(solution)/shard_map/ppermute | solution.py:638
  128.2 7.9 %collective-permute-start.31 = (bf16[2,80,512]{2,1,0:T(8,128)(2,1)S(1)}, bf16[2,80,512]{2,1,0:T(8,128)(2,1)S(1)}, u32[]{:S(2)}, u32[]{:S(2)}) collective-permute-start(bf16[2,80,512]{2,1,0:T(8,128)(2,1)S(1)} %get-tuple-element.286.refs_0_), channel_id=1, source_target_pairs={{0,2},{1,3},{2,0},{3,1},{4,6},{5,7},{6,4},{7,5},{8,10},{9,11},{10,... | collective-permute-start | bytes 491528 | tf_op jit(solution)/shard_map/ppermute | solution.py:638
  129.1 15.3 %collective-permute-start.41 = (bf16[8,64,512]{2,1,0:T(8,128)(2,1)S(1)}, bf16[8,64,512]{2,1,0:T(8,128)(2,1)S(1)}, u32[]{:S(2)}, u32[]{:S(2)}) collective-permute-start(bf16[8,64,512]{2,1,0:T(8,128)(2,1)S(1)} %get-tuple-element.287.refs_1_), channel_id=1, source_target_pairs={{0,1},{1,0},{2,3},{3,2},{4,5},{5,4},{6,7},{7,6},{8,9},{9,8},{10,11... | collective-permute-start | bytes 1572872 | tf_op jit(solution)/shard_map/ppermute | solution.py:638
  133.2 12.9 %collective-permute-start.42 = (bf16[8,64,512]{2,1,0:T(8,128)(2,1)S(1)}, bf16[8,64,512]{2,1,0:T(8,128)(2,1)S(1)}, u32[]{:S(2)}, u32[]{:S(2)}) collective-permute-start(bf16[8,64,512]{2,1,0:T(8,128)(2,1)S(1)} %get-tuple-element.288.refs_3_), channel_id=1, source_target_pairs={{0,1},{1,0},{2,3},{3,2},{4,5},{5,4},{6,7},{7,6},{8,9},{9,8},{10,11... | collective-permute-start | bytes 1572872 | tf_op jit(solution)/shard_map/ppermute | solution.py:638
  141.7 8.2 %collective-permute-start.39 = (bf16[8,64,512]{2,1,0:T(8,128)(2,1)S(1)}, bf16[8,64,512]{2,1,0:T(8,128)(2,1)S(1)}, u32[]{:S(2)}, u32[]{:S(2)}) collective-permute-start(bf16[8,64,512]{2,1,0:T(8,128)(2,1)S(1)} %collective-permute-done.32.refs_1_), channel_id=1, source_target_pairs={{0,1},{1,0},{2,3},{3,2},{4,5},{5,4},{6,7},{7,6},{8,9},{9,8},{10,11... | collective-permute-start | bytes 1572872 | tf_op jit(solution)/shard_map/ppermute | solution.py:638
  141.7 8.2 %collective-permute-start.40 = (bf16[8,64,512]{2,1,0:T(8,128)(2,1)S(1)}, bf16[8,64,512]{2,1,0:T(8,128)(2,1)S(1)}, u32[]{:S(2)}, u32[]{:S(2)}) collective-permute-start(bf16[8,64,512]{2,1,0:T(8,128)(2,1)S(1)} %collective-permute-done.33.refs_3_), channel_id=1, source_target_pairs={{0,1},{1,0},{2,3},{3,2},{4,5},{5,4},{6,7},{7,6},{8,9},{9,8},{10,11... | collective-permute-start | bytes 1572872 | tf_op jit(solution)/shard_map/ppermute | solution.py:638
  142.2 11.4 %collective-permute-start.38 = (bf16[3,128,512]{2,1,0:T(8,128)(2,1)S(1)}, bf16[3,128,512]{2,1,0:T(8,128)(2,1)S(1)}, u32[]{:S(2)}, u32[]{:S(2)}) collective-permute-start(bf16[3,128,512]{2,1,0:T(8,128)(2,1)S(1)} %get-tuple-element.298.refs_4_), channel_id=1, source_target_pairs={{0,2},{1,3},{2,0},{3,1},{4,6},{5,7},{6,4},{7,5},{8,10},{9,11},{10,... | collective-permute-start | bytes 1179656 | tf_op jit(solution)/shard_map/ppermute | solution.py:638
  144.4 9.2 %collective-permute-start.37 = (bf16[272,512]{1,0:T(8,128)(2,1)S(1)}, bf16[272,512]{1,0:T(8,128)(2,1)S(1)}, u32[]{:S(2)}, u32[]{:S(2)}) collective-permute-start(bf16[272,512]{1,0:T(8,128)(2,1)S(1)} %get-tuple-element.316.refs_5_), channel_id=1, source_target_pairs={{0,16},{8,24},{16,0},{24,8},{1,17},{9,25},{17,1},{25,9},{2,18},{10... | collective-permute-start | bytes 835592 | tf_op jit(solution)/shard_map/ppermute | solution.py:638
  146.1 7.5 %collective-permute-start.36 = (bf16[256,512]{1,0:T(8,128)(2,1)S(1)}, bf16[256,512]{1,0:T(8,128)(2,1)S(1)}, u32[]{:S(2)}, u32[]{:S(2)}) collective-permute-start(bf16[256,512]{1,0:T(8,128)(2,1)S(1)} %get-tuple-element.314.refs_1_), channel_id=1, source_target_pairs={{0,8},{8,0},{16,24},{24,16},{1,9},{9,1},{17,25},{25,17},{2,10},{10... | collective-permute-start | bytes 786440 | tf_op jit(solution)/shard_map/ppermute | solution.py:638
  (29 other events, 140.7 us)

commit v5 on v4

--- a/solution.py
+++ b/solution.py
@@ -957,7 +957,7 @@
     grad_down, grad_up = unpack(True, d_far, d_far_o, u_far, u_far_o, [grad_down, grad_up])
     far_held = chain.hold(one_far, two_far, nearest)
     nearest = far_held[2]
-    one_near_o, two_near_o = other_core(*chain.hold(one_near, two_near))
+    one_near_o, two_near_o = other_core(one_near, two_near)
     one_far_o, two_far_o = other_core(*far_held[:2])
     input_grad = call(
         last_kernel, [tokens_v, vectors, mid_grad, *dn_m, dn_r, *arrived[0], moving, nearest], [token_block],

time: 162 us -> 162 us (level)
  no operation moved by 1% of the time
where the time goes in v5:
time: 162 us; the launch traced here: 159 us
  Pallas kernels  52.4 us (32%)
  waiting for transfers between devices  50.3 us (31%)
  starting transfers between devices  49 us (30%)
  local copies, waits for them, and re-layouts  4.48 us (3%)
  between operations  1.62 us (1%)
    pallas_call x24, Pallas kernels, call(): pl.pallas_call(body_of, grid=grid, in_specs=[SMEM] * scalars + (specs or...  52.4 us
    ppermute x47, waiting for transfers between devices, exchange(): return lax.ppermute(array, axis, [(i, i ^ mask) for i in range(count)])  50.3 us
    ppermute x47, starting transfers between devices, exchange(): return lax.ppermute(array, axis, [(i, i ^ mask) for i in range(count)])  49 us
  transfers between devices with their start and end apart: 47, of which 20 were waited for; matrix products, arithmetic and copies ran while one was open for 3% of the time, Pallas kernels for 26%

profile of v5, /device:TPU:0, one launch (start us, length us, event | category | flops | bytes accessed | tf_op | source)
XLA Modules:
  0.0 159.0 jit_solution(11182225902853793967)
XLA Ops:
  1.2 3.7 %collective-permute-start = (bf16[3,128,512]{2,1,0:T(8,128)(2,1)}, bf16[3,128,512]{2,1,0:T(8,128)(2,1)S(1)}, u32[]{:S(2)}, u32[]{:S(2)}) collective-permute-start(bf16[3,128,512]{2,1,0:T(8,128)(2,1)} %refs_1_.8), channel_id=1, source_target_pairs={{0,4},{1,5},{2,6},{3,7},{4,0},{5,1},{6,2},{7,3},{8,12},{9,13},{10,... | collective-permute-start | bytes 1179656 | tf_op jit(solution)/shard_map/ppermute | solution.py:638
  6.5 1.9 %dynamic-slice_bitcast_fusion = (bf16[1,512,256]{2,1,0:T(8,128)(2,1)}, bf16[1,512,256]{2,1,0:T(8,128)(2,1)}) fusion(bf16[512,512]{1,0:T(8,128)(2,1)} %param.25, s32[]{:T(128)S(6)} %select_n.39, bf16[512,512]{1,0:T(8,128)(2,1)} %param.24), kind=kLoop, calls=%fused_computation.1 | loop fusion | bytes 1048580 | tf_op jit(solution)/shard_map/stack | solution.py:697
  10.7 3.5 %attend_chunk_0.1 = (bf16[3,256,256]{2,1,0:T(8,128)(2,1)S(1)}, bf16[3,256,256]{2,1,0:T(8,128)(2,1)S(1)}, bf16[3,256,256]{2,1,0:T(8,128)(2,1)S(1)}, bf16[3,512,25...) custom-call(s32[5]{0:T(128)S(1)} %stack.53.refs_0_, ...), custom_call_target="tpu_custom_call" | custom-call | flops 55000000 | tf_op jit(solution)/shard_map/attend_chunk_0/pallas_call | solution.py:610
  17.5 5.8 %collective-permute-done.refs_3_ = bf16[3,128,512]{2,1,0:T(8,128)(2,1)S(1)} collective-permute-done((bf16[3,128,512]{2,1,0:T(8,128)(2,1)}, bf16[3,128,512]{2,1,0:T(8,128)(2,1)S(1)}, u32[]{:S(2)}, u32[]{:S(2)}) %collective-permute-start) | collective-permute-done | bytes 393248 | tf_op jit(solution)/shard_map/ppermute | solution.py:638
  25.1 3.3 %attend_chunk_2.1 = (bf16[3,256,256]{2,1,0:T(8,128)(2,1)S(1)}, bf16[3,256,256]{2,1,0:T(8,128)(2,1)S(1)}, bf16[3,256,256]{2,1,0:T(8,128)(2,1)S(1)}, bf16[3,512,25...) custom-call(s32[5]{0:T(128)S(1)} %stack.53.refs_0_, ...), custom_call_target="tpu_custom_call" | custom-call | flops 55000000 | tf_op jit(solution)/shard_map/attend_chunk_2/pallas_call | solution.py:610
  28.4 3.3 %attend_chunk_1.1 = (bf16[3,256,256]{2,1,0:T(8,128)(2,1)S(1)}, bf16[3,256,256]{2,1,0:T(8,128)(2,1)S(1)}, bf16[3,256,256]{2,1,0:T(8,128)(2,1)S(1)}, bf16[3,512,25...) custom-call(s32[5]{0:T(128)S(1)} %stack.53.refs_0_, ...), custom_call_target="tpu_custom_call" | custom-call | flops 55000000 | tf_op jit(solution)/shard_map/attend_chunk_1/pallas_call | solution.py:610
  31.8 3.6 %collective-permute-done.2.refs_3_ = bf16[3,128,512]{2,1,0:T(8,128)(2,1)S(1)} collective-permute-done((bf16[3,128,512]{2,1,0:T(8,128)(2,1)S(1)}, bf16[3,128,512]{2,1,0:T(8,128)(2,1)S(1)}, u32[]{:S(2)}, u32[]{:S(2)}) %collective-permute-start.2) | collective-permute-done | bytes 393248 | tf_op jit(solution)/shard_map/ppermute | solution.py:638
  37.1 3.4 %attend_chunk_3.1 = (bf16[3,256,256]{2,1,0:T(8,128)(2,1)S(1)}, bf16[3,256,256]{2,1,0:T(8,128)(2,1)S(1)}, bf16[3,256,256]{2,1,0:T(8,128)(2,1)S(1)}, bf16[3,512,25...) custom-call(s32[5]{0:T(128)S(1)} %stack.53.refs_0_, ...), custom_call_target="tpu_custom_call" | custom-call | flops 55000000 | tf_op jit(solution)/shard_map/attend_chunk_3/pallas_call | solution.py:610
  42.0 3.4 %feed_forward_a.1 = (f32[384,512]{1,0:T(8,128)S(1)}, bf16[384,512]{1,0:T(8,128)(2,1)S(1)}, bf16[384,2560]{1,0:T(8,128)(2,1)S(1)}, f32[384,512]{1,0:T(8,128)S(1)}...) custom-call(s32[5]{0:T(128)S(1)} %stack.53.refs_0_, bf16[3,128,256]{2,1,0:T(8,128)(2,1)S(1)} %get-tuple-element.192.refs_1_, ...), custom_call_target="tpu_custom_call" | custom-call | flops 4400000000 | tf_op jit(solution)/shard_map/feed_forward_a/pallas_call | solution.py:610
  45.7 3.7 %feed_forward_b.1 = (bf16[3,128,512]{2,1,0:T(8,128)(2,1)}, bf16[384,1024]{1,0:T(8,128)(2,1)S(1)}, bf16[384,1024]{1,0:T(8,128)(2,1)S(1)}, f32[384,512]{1,0:T(8,12...) custom-call(s32[5]{0:T(128)S(1)} %stack.53.refs_0_, f32[384,512]{1,0:T(8,128)S(1)} %get-tuple-element.202.refs_1_, ...), custom_call_target="tpu_custom_call" | custom-call | flops 4400000000 | tf_op jit(solution)/shard_map/feed_forward_b/pallas_call | solution.py:610
  49.8 1.8 %feed_forward_grad_sent.1 = (bf16[8,64,512]{2,1,0:T(8,128)(2,1)S(1)}, bf16[8,64,512]{2,1,0:T(8,128)(2,1)S(1)}) custom-call(s32[5]{0:T(128)S(1)} %stack.53.refs_0_, bf16[384,1024]{1,0:T(8,128)(2,1)S(1)} %get-tuple-element.211.refs_1_, bf16[384,1024]{1,0:T(8,128)(2,1)S(1)} %get-tuple-element.212.refs_2_, ...), custom_call_target="tpu_custom_call" | custom-call | flops 3300000000 | tf_op jit(solution)/shard_map/feed_forward_grad_sent/pallas_call | solution.py:610
  54.8 1.8 %feed_forward_grad_kept.1 = (bf16[8,64,512]{2,1,0:T(8,128)(2,1)S(1)}, bf16[8,64,512]{2,1,0:T(8,128)(2,1)S(1)}) custom-call(s32[5]{0:T(128)S(1)} %stack.53.refs_0_, bf16[384,1024]{1,0:T(8,128)(2,1)S(1)} %get-tuple-element.211.refs_1_, bf16[384,1024]{1,0:T(8,128)(2,1)S(1)} %get-tuple-element.212.refs_2_, ...), custom_call_target="tpu_custom_call" | custom-call | flops 55000000 | tf_op jit(solution)/shard_map/feed_forward_grad_kept/pallas_call | solution.py:610
  56.6 9.8 %attend_back_1.1 = (bf16[4,128,512]{2,1,0:T(8,128)(2,1)S(1)}, bf16[4,128,512]{2,1,0:T(8,128)(2,1)S(1)}, bf16[4,128,512]{2,1,0:T(8,128)(2,1)S(1)}, bf16[4,128,512...) custom-call(s32[5]{0:T(128)S(1)} %stack.53.refs_0_, ...), custom_call_target="tpu_custom_call" | custom-call | flops 55000000 | tf_op jit(solution)/shard_map/attend_back_1/pallas_call | solution.py:610
  69.2 5.9 %attend_back_2.1 = (bf16[4,128,512]{2,1,0:T(8,128)(2,1)S(1)}, bf16[12,128,512]{2,1,0:T(8,128)(2,1)S(1)}, bf16[256,512]{1,0:T(8,128)(2,1)S(1)}, bf16[256,512]{1,0...) custom-call(s32[5]{0:T(128)S(1)} %stack.53.refs_0_, s32[3,4]{1,0:T(4,128)S(1)} %copy-done.3, ...), custom_call_target="tpu_custom_call" | custom-call | flops 55000000 | tf_op jit(solution)/shard_map/attend_back_2/pallas_call | solution.py:610
  79.2 5.6 %collective-permute-done.17.refs_3_ = bf16[256,512]{1,0:T(8,128)(2,1)S(1)} collective-permute-done((bf16[256,512]{1,0:T(8,128)(2,1)S(1)}, bf16[256,512]{1,0:T(8,128)(2,1)S(1)}, u32[]{:S(2)}, u32[]{:S(2)}) %collective-permute-start.17) | collective-permute-done | bytes 262176 | tf_op jit(solution)/shard_map/ppermute | solution.py:638
  86.8 2.2 %collective-permute-start.19 = (bf16[128,512]{1,0:T(8,128)(2,1)S(1)}, bf16[128,512]{1,0:T(8,128)(2,1)S(1)}, u32[]{:S(2)}, u32[]{:S(2)}) collective-permute-start(bf16[128,512]{1,0:T(8,128)(2,1)S(1)} %get-tuple-element.267), channel_id=1, source_target_pairs={{0,4},{1,5},{2,6},{3,7},{4,0},{5,1},{6,2},{7,3},{8,12},{9,13},{10,... | collective-permute-start | bytes 393224 | tf_op jit(solution)/shard_map/ppermute | solution.py:638
  90.5 4.2 %collective-permute-done.19.refs_1_ = bf16[128,512]{1,0:T(8,128)(2,1)S(1)} collective-permute-done((bf16[128,512]{1,0:T(8,128)(2,1)S(1)}, bf16[128,512]{1,0:T(8,128)(2,1)S(1)}, u32[]{:S(2)}, u32[]{:S(2)}) %collective-permute-start.19) | collective-permute-done | bytes 131104 | tf_op jit(solution)/shard_map/ppermute | solution.py:638
  96.0 2.6 %collective-permute-start.22 = (bf16[128,512]{1,0:T(8,128)(2,1)S(1)}, bf16[128,512]{1,0:T(8,128)(2,1)S(1)}, u32[]{:S(2)}, u32[]{:S(2)}) collective-permute-start(bf16[128,512]{1,0:T(8,128)(2,1)S(1)} %get-tuple-element.270.refs_0_), channel_id=1, source_target_pairs={{0,4},{1,5},{2,6},{3,7},{4,0},{5,1},{6,2},{7,3},{8,12},{9,13},{10,... | collective-permute-start | bytes 393224 | tf_op jit(solution)/shard_map/ppermute | solution.py:638
  98.6 4.4 %collective-permute-done.22.refs_1_ = bf16[128,512]{1,0:T(8,128)(2,1)S(1)} collective-permute-done((bf16[128,512]{1,0:T(8,128)(2,1)S(1)}, bf16[128,512]{1,0:T(8,128)(2,1)S(1)}, u32[]{:S(2)}, u32[]{:S(2)}) %collective-permute-start.22) | collective-permute-done | bytes 131104 | tf_op jit(solution)/shard_map/ppermute | solution.py:638
  103.1 2.0 %collective-permute-start.24 = (bf16[2,128,512]{2,1,0:T(8,128)(2,1)S(1)}, bf16[2,128,512]{2,1,0:T(8,128)(2,1)S(1)}, u32[]{:S(2)}, u32[]{:S(2)}) collective-permute-start(bf16[2,128,512]{2,1,0:T(8,128)(2,1)S(1)} %get-tuple-element.273.refs_0_), channel_id=1, source_target_pairs={{0,2},{1,3},{2,0},{3,1},{4,6},{5,7},{6,4},{7,5},{8,10},{9,11},{10,... | collective-permute-start | bytes 786440 | tf_op jit(solution)/shard_map/ppermute | solution.py:638
  105.1 2.0 %collective-permute-start.25 = (bf16[80,512]{1,0:T(8,128)(2,1)S(1)}, bf16[80,512]{1,0:T(8,128)(2,1)S(1)}, u32[]{:S(2)}, u32[]{:S(2)}) collective-permute-start(bf16[80,512]{1,0:T(8,128)(2,1)S(1)} %get-tuple-element.275.refs_8_), channel_id=1, source_target_pairs={{0,4},{1,5},{2,6},{3,7},{4,0},{5,1},{6,2},{7,3},{8,12},{9,13},{10,... | collective-permute-start | bytes 245768 | tf_op jit(solution)/shard_map/ppermute | solution.py:638
  107.1 4.2 %collective-permute-done.25.refs_3_ = bf16[80,512]{1,0:T(8,128)(2,1)S(1)} collective-permute-done((bf16[80,512]{1,0:T(8,128)(2,1)S(1)}, bf16[80,512]{1,0:T(8,128)(2,1)S(1)}, u32[]{:S(2)}, u32[]{:S(2)}) %collective-permute-start.25) | collective-permute-done | bytes 81952 | tf_op jit(solution)/shard_map/ppermute | solution.py:638
  111.6 2.5 %collective-permute-start.29 = (bf16[3,128,512]{2,1,0:T(8,128)(2,1)S(1)}, bf16[3,128,512]{2,1,0:T(8,128)(2,1)S(1)}, u32[]{:S(2)}, u32[]{:S(2)}) collective-permute-start(bf16[3,128,512]{2,1,0:T(8,128)(2,1)S(1)} %get-tuple-element.281.refs_11_), channel_id=1, source_target_pairs={{0,2},{1,3},{2,0},{3,1},{4,6},{5,7},{6,4},{7,5},{8,10},{9,11},{10,... | collective-permute-start | bytes 1179656 | tf_op jit(solution)/shard_map/ppermute | solution.py:638
  117.9 4.8 %collective-permute-done.29.refs_10_ = bf16[3,128,512]{2,1,0:T(8,128)(2,1)S(1)} collective-permute-done((bf16[3,128,512]{2,1,0:T(8,128)(2,1)S(1)}, bf16[3,128,512]{2,1,0:T(8,128)(2,1)S(1)}, u32[]{:S(2)}, u32[]{:S(2)}) %collective-permute-start.29) | collective-permute-done | bytes 393248 | tf_op jit(solution)/shard_map/ppermute | solution.py:638
  125.5 2.6 %collective-permute-start.30 = (bf16[3,128,512]{2,1,0:T(8,128)(2,1)S(1)}, bf16[3,128,512]{2,1,0:T(8,128)(2,1)S(1)}, u32[]{:S(2)}, u32[]{:S(2)}) collective-permute-start(bf16[3,128,512]{2,1,0:T(8,128)(2,1)S(1)} %get-tuple-element.286.refs_6_), channel_id=1, source_target_pairs={{0,4},{1,5},{2,6},{3,7},{4,0},{5,1},{6,2},{7,3},{8,12},{9,13},{10,... | collective-permute-start | bytes 1179656 | tf_op jit(solution)/shard_map/ppermute | solution.py:638
  129.1 4.1 %collective-permute-done.32.refs_1_ = bf16[8,64,512]{2,1,0:T(8,128)(2,1)S(1)} collective-permute-done((bf16[8,64,512]{2,1,0:T(8,128)(2,1)S(1)}, bf16[8,64,512]{2,1,0:T(8,128)(2,1)S(1)}, u32[]{:S(2)}, u32[]{:S(2)}) %collective-permute-start.32) | collective-permute-done | bytes 524320 | tf_op jit(solution)/shard_map/ppermute | solution.py:638
  133.5 2.6 %collective-permute-done.31.refs_1_ = bf16[2,80,512]{2,1,0:T(8,128)(2,1)S(1)} collective-permute-done((bf16[2,80,512]{2,1,0:T(8,128)(2,1)S(1)}, bf16[2,80,512]{2,1,0:T(8,128)(2,1)S(1)}, u32[]{:S(2)}, u32[]{:S(2)}) %collective-permute-start.31) | collective-permute-done | bytes 163872 | tf_op jit(solution)/shard_map/ppermute | solution.py:638
  137.9 3.8 %collective-permute-done.30.refs_7_ = bf16[3,128,512]{2,1,0:T(8,128)(2,1)S(1)} collective-permute-done((bf16[3,128,512]{2,1,0:T(8,128)(2,1)S(1)}, bf16[3,128,512]{2,1,0:T(8,128)(2,1)S(1)}, u32[]{:S(2)}, u32[]{:S(2)}) %collective-permute-start.30) | collective-permute-done | bytes 393248 | tf_op jit(solution)/shard_map/ppermute | solution.py:638
  142.2 2.1 %collective-permute-start.38 = (bf16[3,128,512]{2,1,0:T(8,128)(2,1)S(1)}, bf16[3,128,512]{2,1,0:T(8,128)(2,1)S(1)}, u32[]{:S(2)}, u32[]{:S(2)}) collective-permute-start(bf16[3,128,512]{2,1,0:T(8,128)(2,1)S(1)} %get-tuple-element.295.refs_4_), channel_id=1, source_target_pairs={{0,2},{1,3},{2,0},{3,1},{4,6},{5,7},{6,4},{7,5},{8,10},{9,11},{10,... | collective-permute-start | bytes 1179656 | tf_op jit(solution)/shard_map/ppermute | solution.py:638
  147.1 2.7 %unpack_feed_forward.2 = (f32[2048,512]{1,0:T(8,128)}, f32[512,2048]{1,0:T(8,128)}, f32[8,128]{1,0:T(8,128)S(1)}) custom-call(s32[5]{0:T(128)S(1)} %stack.53.refs_0_, bf16[8,64,512]{2,1,0:T(8,128)(2,1)S(1)} %get-tuple-element.284.refs_1_, bf16[8,64,512]{2,1,0:T(8,128)(2,1)S(1)} %collective-permute-done.41.refs_2_, ...), custom_call_target="tpu_custom_call" | custom-call | flops 110000000 | tf_op jit(solution)/shard_map/unpack_feed_forward/pallas_call | solution.py:610
  149.9 2.7 %unpack_feed_forward.3 = (f32[2048,512]{1,0:T(8,128)}, f32[512,2048]{1,0:T(8,128)}, f32[8,128]{1,0:T(8,128)S(1)}) custom-call(s32[5]{0:T(128)S(1)} %stack.53.refs_0_, bf16[8,64,512]{2,1,0:T(8,128)(2,1)S(1)} %collective-permute-done.32.refs_1_, bf16[8,64,512]{2,1,0:T(8,128)(2,1)S(1)} %collective-permute-done.39.refs_2_, ...), custom_call_target="tpu_custom_call", output_to_operand_aliasing={{0}: (5, {}), {1}: (6, {})} | custom-call | flops 110000000 | tf_op jit(solution)/shard_map/unpack_feed_forward/pallas_call | solution.py:610
  155.9 2.7 %unpack_attend.1 = (f32[512,512]{1,0:T(8,128)}, f32[512,512]{1,0:T(8,128)}, f32[512,512]{1,0:T(8,128)}, f32[512,512]{1,0:T(8,128)}, f32[1,512]{1,0:T(1,128)}, /*...) custom-call(s32[5]{0:T(128)S(1)} %stack.53.refs_0_, ...), custom_call_target="tpu_custom_call" | custom-call | flops 110000000 | tf_op jit(solution)/shard_map/unpack_attend/pallas_call | solution.py:610
  (120 shorter events, 44.4 us)
Async XLA Ops:
  0.7 10.0 %collective-permute-start.1 = (bf16[3,128,512]{2,1,0:T(8,128)(2,1)}, bf16[3,128,512]{2,1,0:T(8,128)(2,1)S(1)}, u32[]{:S(2)}, u32[]{:S(2)}) collective-permute-start(bf16[3,128,512]{2,1,0:T(8,128)(2,1)} %refs_1_.8), channel_id=1, source_target_pairs={{0,1},{1,0},{2,3},{3,2},{4,5},{5,4},{6,7},{7,6},{8,9},{9,8},{10,11... | collective-permute-start | bytes 1179656 | tf_op jit(solution)/shard_map/ppermute | solution.py:638
  1.2 22.1 %collective-permute-start = (bf16[3,128,512]{2,1,0:T(8,128)(2,1)}, bf16[3,128,512]{2,1,0:T(8,128)(2,1)S(1)}, u32[]{:S(2)}, u32[]{:S(2)}) collective-permute-start(bf16[3,128,512]{2,1,0:T(8,128)(2,1)} %refs_1_.8), channel_id=1, source_target_pairs={{0,4},{1,5},{2,6},{3,7},{4,0},{5,1},{6,2},{7,3},{8,12},{9,13},{10,... | collective-permute-start | bytes 1179656 | tf_op jit(solution)/shard_map/ppermute | solution.py:638
  4.9 19.0 %collective-permute-start.3 = (bf16[3,128,512]{2,1,0:T(8,128)(2,1)}, bf16[3,128,512]{2,1,0:T(8,128)(2,1)S(1)}, u32[]{:S(2)}, u32[]{:S(2)}) collective-permute-start(bf16[3,128,512]{2,1,0:T(8,128)(2,1)} %refs_1_.8), channel_id=1, source_target_pairs={{0,2},{1,3},{2,0},{3,1},{4,6},{5,7},{6,4},{7,5},{8,10},{9,11},{10,... | collective-permute-start | bytes 1179656 | tf_op jit(solution)/shard_map/ppermute | solution.py:638
  23.9 11.5 %collective-permute-start.2 = (bf16[3,128,512]{2,1,0:T(8,128)(2,1)S(1)}, bf16[3,128,512]{2,1,0:T(8,128)(2,1)S(1)}, u32[]{:S(2)}, u32[]{:S(2)}) collective-permute-start(bf16[3,128,512]{2,1,0:T(8,128)(2,1)S(1)} %collective-permute-done.refs_3_), channel_id=1, source_target_pairs={{0,2},{1,3},{2,0},{3,1},{4,6},{5,7},{6,4},{7,5},{8,10},{9,11},{10,... | collective-permute-start | bytes 1179656 | tf_op jit(solution)/shard_map/ppermute | solution.py:638
  51.6 14.8 %collective-permute-start.11 = (bf16[8,64,512]{2,1,0:T(8,128)(2,1)S(1)}, bf16[8,64,512]{2,1,0:T(8,128)(2,1)S(1)}, u32[]{:S(2)}, u32[]{:S(2)}) collective-permute-start(bf16[8,64,512]{2,1,0:T(8,128)(2,1)S(1)} %get-tuple-element.236.refs_7_), channel_id=1, source_target_pairs={{0,8},{8,0},{16,24},{24,16},{1,9},{9,1},{17,25},{25,17},{2,10},{10... | collective-permute-start | bytes 1572872 | tf_op jit(solution)/shard_map/ppermute | solution.py:638
  53.2 13.7 %collective-permute-start.12 = (bf16[8,64,512]{2,1,0:T(8,128)(2,1)S(1)}, bf16[8,64,512]{2,1,0:T(8,128)(2,1)S(1)}, u32[]{:S(2)}, u32[]{:S(2)}) collective-permute-start(bf16[8,64,512]{2,1,0:T(8,128)(2,1)S(1)} %get-tuple-element.249), channel_id=1, source_target_pairs={{0,16},{8,24},{16,0},{24,8},{1,17},{9,25},{17,1},{25,9},{2,18},{10... | collective-permute-start | bytes 1572872 | tf_op jit(solution)/shard_map/ppermute | solution.py:638
  67.1 8.0 %collective-permute-start.13 = (bf16[4,64,512]{2,1,0:T(8,128)(2,1)S(1)}, bf16[4,64,512]{2,1,0:T(8,128)(2,1)S(1)}, u32[]{:S(2)}, u32[]{:S(2)}) collective-permute-start(bf16[4,64,512]{2,1,0:T(8,128)(2,1)S(1)} %get-tuple-element.255), channel_id=1, source_target_pairs={{0,16},{8,24},{16,0},{24,8},{1,17},{9,25},{17,1},{25,9},{2,18},{10... | collective-permute-start | bytes 786440 | tf_op jit(solution)/shard_map/ppermute | solution.py:638
  68.6 6.9 %collective-permute-start.14 = (bf16[4,64,512]{2,1,0:T(8,128)(2,1)S(1)}, bf16[4,64,512]{2,1,0:T(8,128)(2,1)S(1)}, u32[]{:S(2)}, u32[]{:S(2)}) collective-permute-start(bf16[4,64,512]{2,1,0:T(8,128)(2,1)S(1)} %get-tuple-element.250.refs_35_), channel_id=1, source_target_pairs={{0,8},{8,0},{16,24},{24,16},{1,9},{9,1},{17,25},{25,17},{2,10},{10... | collective-permute-start | bytes 786440 | tf_op jit(solution)/shard_map/ppermute | solution.py:638
  75.8 9.7 %collective-permute-start.18 = (bf16[272,512]{1,0:T(8,128)(2,1)S(1)}, bf16[272,512]{1,0:T(8,128)(2,1)S(1)}, u32[]{:S(2)}, u32[]{:S(2)}) collective-permute-start(bf16[272,512]{1,0:T(8,128)(2,1)S(1)} %get-tuple-element.264.refs_6_), channel_id=1, source_target_pairs={{0,16},{8,24},{16,0},{24,8},{1,17},{9,25},{17,1},{25,9},{2,18},{10... | collective-permute-start | bytes 835592 | tf_op jit(solution)/shard_map/ppermute | solution.py:638
  76.5 8.4 %collective-permute-start.17 = (bf16[256,512]{1,0:T(8,128)(2,1)S(1)}, bf16[256,512]{1,0:T(8,128)(2,1)S(1)}, u32[]{:S(2)}, u32[]{:S(2)}) collective-permute-start(bf16[256,512]{1,0:T(8,128)(2,1)S(1)} %get-tuple-element.262), channel_id=1, source_target_pairs={{0,8},{8,0},{16,24},{24,16},{1,9},{9,1},{17,25},{25,17},{2,10},{10... | collective-permute-start | bytes 786440 | tf_op jit(solution)/shard_map/ppermute | solution.py:638
  77.5 8.1 %collective-permute-start.16 = (bf16[2,128,512]{2,1,0:T(8,128)(2,1)S(1)}, bf16[2,128,512]{2,1,0:T(8,128)(2,1)S(1)}, u32[]{:S(2)}, u32[]{:S(2)}) collective-permute-start(bf16[2,128,512]{2,1,0:T(8,128)(2,1)S(1)} %get-tuple-element.265.refs_6_), channel_id=1, source_target_pairs={{0,2},{1,3},{2,0},{3,1},{4,6},{5,7},{6,4},{7,5},{8,10},{9,11},{10,... | collective-permute-start | bytes 786440 | tf_op jit(solution)/shard_map/ppermute | solution.py:638
  85.7 9.0 %collective-permute-start.21 = (bf16[144,512]{1,0:T(8,128)(2,1)S(1)}, bf16[144,512]{1,0:T(8,128)(2,1)S(1)}, u32[]{:S(2)}, u32[]{:S(2)}) collective-permute-start(bf16[144,512]{1,0:T(8,128)(2,1)S(1)} %get-tuple-element.269.refs_8_), channel_id=1, source_target_pairs={{0,8},{8,0},{16,24},{24,16},{1,9},{9,1},{17,25},{25,17},{2,10},{10... | collective-permute-start | bytes 442376 | tf_op jit(solution)/shard_map/ppermute | solution.py:638
  86.8 7.8 %collective-permute-start.19 = (bf16[128,512]{1,0:T(8,128)(2,1)S(1)}, bf16[128,512]{1,0:T(8,128)(2,1)S(1)}, u32[]{:S(2)}, u32[]{:S(2)}) collective-permute-start(bf16[128,512]{1,0:T(8,128)(2,1)S(1)} %get-tuple-element.267), channel_id=1, source_target_pairs={{0,4},{1,5},{2,6},{3,7},{4,0},{5,1},{6,2},{7,3},{8,12},{9,13},{10,... | collective-permute-start | bytes 393224 | tf_op jit(solution)/shard_map/ppermute | solution.py:638
  94.8 8.2 %collective-permute-start.23 = (bf16[2,80,512]{2,1,0:T(8,128)(2,1)S(1)}, bf16[2,80,512]{2,1,0:T(8,128)(2,1)S(1)}, u32[]{:S(2)}, u32[]{:S(2)}) collective-permute-start(bf16[2,80,512]{2,1,0:T(8,128)(2,1)S(1)} %get-tuple-element.272.refs_4_), channel_id=1, source_target_pairs={{0,2},{1,3},{2,0},{3,1},{4,6},{5,7},{6,4},{7,5},{8,10},{9,11},{10,... | collective-permute-start | bytes 491528 | tf_op jit(solution)/shard_map/ppermute | solution.py:638
  96.0 7.0 %collective-permute-start.22 = (bf16[128,512]{1,0:T(8,128)(2,1)S(1)}, bf16[128,512]{1,0:T(8,128)(2,1)S(1)}, u32[]{:S(2)}, u32[]{:S(2)}) collective-permute-start(bf16[128,512]{1,0:T(8,128)(2,1)S(1)} %get-tuple-element.270.refs_0_), channel_id=1, source_target_pairs={{0,4},{1,5},{2,6},{3,7},{4,0},{5,1},{6,2},{7,3},{8,12},{9,13},{10,... | collective-permute-start | bytes 393224 | tf_op jit(solution)/shard_map/ppermute | solution.py:638
  103.1 8.4 %collective-permute-start.24 = (bf16[2,128,512]{2,1,0:T(8,128)(2,1)S(1)}, bf16[2,128,512]{2,1,0:T(8,128)(2,1)S(1)}, u32[]{:S(2)}, u32[]{:S(2)}) collective-permute-start(bf16[2,128,512]{2,1,0:T(8,128)(2,1)S(1)} %get-tuple-element.273.refs_0_), channel_id=1, source_target_pairs={{0,2},{1,3},{2,0},{3,1},{4,6},{5,7},{6,4},{7,5},{8,10},{9,11},{10,... | collective-permute-start | bytes 786440 | tf_op jit(solution)/shard_map/ppermute | solution.py:638
  105.1 6.2 %collective-permute-start.25 = (bf16[80,512]{1,0:T(8,128)(2,1)S(1)}, bf16[80,512]{1,0:T(8,128)(2,1)S(1)}, u32[]{:S(2)}, u32[]{:S(2)}) collective-permute-start(bf16[80,512]{1,0:T(8,128)(2,1)S(1)} %get-tuple-element.275.refs_8_), channel_id=1, source_target_pairs={{0,4},{1,5},{2,6},{3,7},{4,0},{5,1},{6,2},{7,3},{8,12},{9,13},{10,... | collective-permute-start | bytes 245768 | tf_op jit(solution)/shard_map/ppermute | solution.py:638
  111.6 11.1 %collective-permute-start.29 = (bf16[3,128,512]{2,1,0:T(8,128)(2,1)S(1)}, bf16[3,128,512]{2,1,0:T(8,128)(2,1)S(1)}, u32[]{:S(2)}, u32[]{:S(2)}) collective-permute-start(bf16[3,128,512]{2,1,0:T(8,128)(2,1)S(1)} %get-tuple-element.281.refs_11_), channel_id=1, source_target_pairs={{0,2},{1,3},{2,0},{3,1},{4,6},{5,7},{6,4},{7,5},{8,10},{9,11},{10,... | collective-permute-start | bytes 1179656 | tf_op jit(solution)/shard_map/ppermute | solution.py:638
  114.1 8.6 %collective-permute-start.26 = (bf16[4,64,512]{2,1,0:T(8,128)(2,1)S(1)}, bf16[4,64,512]{2,1,0:T(8,128)(2,1)S(1)}, u32[]{:S(2)}, u32[]{:S(2)}) collective-permute-start(bf16[4,64,512]{2,1,0:T(8,128)(2,1)S(1)} %get-tuple-element.276.refs_0_), channel_id=1, source_target_pairs={{0,16},{8,24},{16,0},{24,8},{1,17},{9,25},{17,1},{25,9},{2,18},{10... | collective-permute-start | bytes 786440 | tf_op jit(solution)/shard_map/ppermute | solution.py:638
  115.6 7.1 %collective-permute-start.27 = (bf16[4,64,512]{2,1,0:T(8,128)(2,1)S(1)}, bf16[4,64,512]{2,1,0:T(8,128)(2,1)S(1)}, u32[]{:S(2)}, u32[]{:S(2)}) collective-permute-start(bf16[4,64,512]{2,1,0:T(8,128)(2,1)S(1)} %get-tuple-element.277.refs_2_), channel_id=1, source_target_pairs={{0,8},{8,0},{16,24},{24,16},{1,9},{9,1},{17,25},{25,17},{2,10},{10... | collective-permute-start | bytes 786440 | tf_op jit(solution)/shard_map/ppermute | solution.py:638
  116.6 6.1 %collective-permute-start.28 = (bf16[80,512]{1,0:T(8,128)(2,1)S(1)}, bf16[80,512]{1,0:T(8,128)(2,1)S(1)}, u32[]{:S(2)}, u32[]{:S(2)}) collective-permute-start(bf16[80,512]{1,0:T(8,128)(2,1)S(1)} %get-tuple-element.278.refs_4_), channel_id=1, source_target_pairs={{0,4},{1,5},{2,6},{3,7},{4,0},{5,1},{6,2},{7,3},{8,12},{9,13},{10,... | collective-permute-start | bytes 245768 | tf_op jit(solution)/shard_map/ppermute | solution.py:638
  123.0 10.2 %collective-permute-start.32 = (bf16[8,64,512]{2,1,0:T(8,128)(2,1)S(1)}, bf16[8,64,512]{2,1,0:T(8,128)(2,1)S(1)}, u32[]{:S(2)}, u32[]{:S(2)}) collective-permute-start(bf16[8,64,512]{2,1,0:T(8,128)(2,1)S(1)} %get-tuple-element.284.refs_1_), channel_id=1, source_target_pairs={{0,8},{8,0},{16,24},{24,16},{1,9},{9,1},{17,25},{25,17},{2,10},{10... | collective-permute-start | bytes 1572872 | tf_op jit(solution)/shard_map/ppermute | solution.py:638
  123.9 9.6 %collective-permute-start.33 = (bf16[8,64,512]{2,1,0:T(8,128)(2,1)S(1)}, bf16[8,64,512]{2,1,0:T(8,128)(2,1)S(1)}, u32[]{:S(2)}, u32[]{:S(2)}) collective-permute-start(bf16[8,64,512]{2,1,0:T(8,128)(2,1)S(1)} %get-tuple-element.285.refs_3_), channel_id=1, source_target_pairs={{0,16},{8,24},{16,0},{24,8},{1,17},{9,25},{17,1},{25,9},{2,18},{10... | collective-permute-start | bytes 1572872 | tf_op jit(solution)/shard_map/ppermute | solution.py:638
  125.5 16.1 %collective-permute-start.30 = (bf16[3,128,512]{2,1,0:T(8,128)(2,1)S(1)}, bf16[3,128,512]{2,1,0:T(8,128)(2,1)S(1)}, u32[]{:S(2)}, u32[]{:S(2)}) collective-permute-start(bf16[3,128,512]{2,1,0:T(8,128)(2,1)S(1)} %get-tuple-element.286.refs_6_), channel_id=1, source_target_pairs={{0,4},{1,5},{2,6},{3,7},{4,0},{5,1},{6,2},{7,3},{8,12},{9,13},{10,... | collective-permute-start | bytes 1179656 | tf_op jit(solution)/shard_map/ppermute | solution.py:638
  128.2 7.9 %collective-permute-start.31 = (bf16[2,80,512]{2,1,0:T(8,128)(2,1)S(1)}, bf16[2,80,512]{2,1,0:T(8,128)(2,1)S(1)}, u32[]{:S(2)}, u32[]{:S(2)}) collective-permute-start(bf16[2,80,512]{2,1,0:T(8,128)(2,1)S(1)} %get-tuple-element.283.refs_0_), channel_id=1, source_target_pairs={{0,2},{1,3},{2,0},{3,1},{4,6},{5,7},{6,4},{7,5},{8,10},{9,11},{10,... | collective-permute-start | bytes 491528 | tf_op jit(solution)/shard_map/ppermute | solution.py:638
  129.1 15.3 %collective-permute-start.41 = (bf16[8,64,512]{2,1,0:T(8,128)(2,1)S(1)}, bf16[8,64,512]{2,1,0:T(8,128)(2,1)S(1)}, u32[]{:S(2)}, u32[]{:S(2)}) collective-permute-start(bf16[8,64,512]{2,1,0:T(8,128)(2,1)S(1)} %get-tuple-element.284.refs_1_), channel_id=1, source_target_pairs={{0,1},{1,0},{2,3},{3,2},{4,5},{5,4},{6,7},{7,6},{8,9},{9,8},{10,11... | collective-permute-start | bytes 1572872 | tf_op jit(solution)/shard_map/ppermute | solution.py:638
  133.2 12.9 %collective-permute-start.42 = (bf16[8,64,512]{2,1,0:T(8,128)(2,1)S(1)}, bf16[8,64,512]{2,1,0:T(8,128)(2,1)S(1)}, u32[]{:S(2)}, u32[]{:S(2)}) collective-permute-start(bf16[8,64,512]{2,1,0:T(8,128)(2,1)S(1)} %get-tuple-element.285.refs_3_), channel_id=1, source_target_pairs={{0,1},{1,0},{2,3},{3,2},{4,5},{5,4},{6,7},{7,6},{8,9},{9,8},{10,11... | collective-permute-start | bytes 1572872 | tf_op jit(solution)/shard_map/ppermute | solution.py:638
  141.7 8.2 %collective-permute-start.39 = (bf16[8,64,512]{2,1,0:T(8,128)(2,1)S(1)}, bf16[8,64,512]{2,1,0:T(8,128)(2,1)S(1)}, u32[]{:S(2)}, u32[]{:S(2)}) collective-permute-start(bf16[8,64,512]{2,1,0:T(8,128)(2,1)S(1)} %collective-permute-done.32.refs_1_), channel_id=1, source_target_pairs={{0,1},{1,0},{2,3},{3,2},{4,5},{5,4},{6,7},{7,6},{8,9},{9,8},{10,11... | collective-permute-start | bytes 1572872 | tf_op jit(solution)/shard_map/ppermute | solution.py:638
  141.7 8.2 %collective-permute-start.40 = (bf16[8,64,512]{2,1,0:T(8,128)(2,1)S(1)}, bf16[8,64,512]{2,1,0:T(8,128)(2,1)S(1)}, u32[]{:S(2)}, u32[]{:S(2)}) collective-permute-start(bf16[8,64,512]{2,1,0:T(8,128)(2,1)S(1)} %collective-permute-done.33.refs_3_), channel_id=1, source_target_pairs={{0,1},{1,0},{2,3},{3,2},{4,5},{5,4},{6,7},{7,6},{8,9},{9,8},{10,11... | collective-permute-start | bytes 1572872 | tf_op jit(solution)/shard_map/ppermute | solution.py:638
  142.2 11.4 %collective-permute-start.38 = (bf16[3,128,512]{2,1,0:T(8,128)(2,1)S(1)}, bf16[3,128,512]{2,1,0:T(8,128)(2,1)S(1)}, u32[]{:S(2)}, u32[]{:S(2)}) collective-permute-start(bf16[3,128,512]{2,1,0:T(8,128)(2,1)S(1)} %get-tuple-element.295.refs_4_), channel_id=1, source_target_pairs={{0,2},{1,3},{2,0},{3,1},{4,6},{5,7},{6,4},{7,5},{8,10},{9,11},{10,... | collective-permute-start | bytes 1179656 | tf_op jit(solution)/shard_map/ppermute | solution.py:638
  144.4 9.2 %collective-permute-start.37 = (bf16[272,512]{1,0:T(8,128)(2,1)S(1)}, bf16[272,512]{1,0:T(8,128)(2,1)S(1)}, u32[]{:S(2)}, u32[]{:S(2)}) collective-permute-start(bf16[272,512]{1,0:T(8,128)(2,1)S(1)} %get-tuple-element.300.refs_5_), channel_id=1, source_target_pairs={{0,16},{8,24},{16,0},{24,8},{1,17},{9,25},{17,1},{25,9},{2,18},{10... | collective-permute-start | bytes 835592 | tf_op jit(solution)/shard_map/ppermute | solution.py:638
  146.1 7.5 %collective-permute-start.36 = (bf16[256,512]{1,0:T(8,128)(2,1)S(1)}, bf16[256,512]{1,0:T(8,128)(2,1)S(1)}, u32[]{:S(2)}, u32[]{:S(2)}) collective-permute-start(bf16[256,512]{1,0:T(8,128)(2,1)S(1)} %get-tuple-element.293.refs_1_), channel_id=1, source_target_pairs={{0,8},{8,0},{16,24},{24,16},{1,9},{9,1},{17,25},{25,17},{2,10},{10... | collective-permute-start | bytes 786440 | tf_op jit(solution)/shard_map/ppermute | solution.py:638
  (29 other events, 143.2 us)

commit v6 on v4

--- a/solution.py
+++ b/solution.py
@@ -876,10 +876,9 @@
     ((a_keep, a_send),) = together(
         "phase_1", (quarter_kernel, [d_keep, d_got, d_got2, u_keep, u_got, u_got2], [two_a, two_a])
     )
-    one_send, two_send, dn_o = chain.hold(one_send, two_send, dn_o[-1])
+    one_send, two_send = chain.hold(one_send, two_send)
     a_got = exchange(a_send, *bit_z)
     one_got, two_got = exchange(one_send, *bit_x), exchange(two_send, *bit_y)
-    (dn_r,) = chain.hold(*other_core(dn_o))
 
     one_shape, two_shape = made((4 * n, width), BF16), made((4 * n + 16, width), BF16)
     (a_keep, a_send), (one_next, two_next) = together(
@@ -895,6 +894,7 @@
         (sum_kernel, [a_keep, a_got], [ff_part]),
         (attend_quarter_kernel, [one_keep, one_got, one_got2, two_keep, two_got, two_got2], [two_b, two_b]),
     )
+    (dn_r,) = chain.hold(*other_core(*chain.hold(dn_o[-1])))
     a_own = over_rest(a_own)
     a_near = exchange(a_own, *bit_w)
     b_got = exchange(b_send, *bit_z)

time: 162 us -> 165 us (1.019)
  waiting for transfers between devices: 50.3 us -> 56.4 us
  starting transfers between devices: 49.4 us -> 45.8 us
    ppermute x47, waiting for transfers between devices: 50.3 us -> 56.4 us  [exchange(): return lax.ppermute(array, axis, [(i, i ^ mask) for i in range(count)])]
    ppermute x47, starting transfers between devices: 49.4 us -> 45.8 us  [exchange(): return lax.ppermute(array, axis, [(i, i ^ mask) for i in range(count)])]
  transfers between devices with their start and end apart: 47 -> 47, of which waited for: 20 -> 19; matrix products, arithmetic and copies ran while one was open for 3% -> 3% of each run, Pallas kernels for 26% -> 26%
where the time goes in v6:
time: 165 us; the launch traced here: 162 us
  waiting for transfers between devices  56.4 us (34%)
  Pallas kernels  52.4 us (32%)
  starting transfers between devices  45.8 us (28%)
  local copies, waits for them, and re-layouts  4.48 us (3%)
    ppermute x47, waiting for transfers between devices, exchange(): return lax.ppermute(array, axis, [(i, i ^ mask) for i in range(count)])  56.4 us
    pallas_call x24, Pallas kernels, call(): pl.pallas_call(body_of, grid=grid, in_specs=[SMEM] * scalars + (specs or...  52.4 us
    ppermute x47, starting transfers between devices, exchange(): return lax.ppermute(array, axis, [(i, i ^ mask) for i in range(count)])  45.8 us
  transfers between devices with their start and end apart: 47, of which 19 were waited for; matrix products, arithmetic and copies ran while one was open for 3% of the time, Pallas kernels for 26%

profile of v6, /device:TPU:0, one launch (start us, length us, event | category | flops | bytes accessed | tf_op | source)
XLA Modules:
  0.0 161.9 jit_solution(2505559173994746657)
XLA Ops:
  1.2 3.7 %collective-permute-start = (bf16[3,128,512]{2,1,0:T(8,128)(2,1)}, bf16[3,128,512]{2,1,0:T(8,128)(2,1)S(1)}, u32[]{:S(2)}, u32[]{:S(2)}) collective-permute-start(bf16[3,128,512]{2,1,0:T(8,128)(2,1)} %refs_1_.8), channel_id=1, source_target_pairs={{0,4},{1,5},{2,6},{3,7},{4,0},{5,1},{6,2},{7,3},{8,12},{9,13},{10,... | collective-permute-start | bytes 1179656 | tf_op jit(solution)/shard_map/ppermute | solution.py:638
  6.5 1.9 %dynamic-slice_bitcast_fusion = (bf16[1,512,256]{2,1,0:T(8,128)(2,1)}, bf16[1,512,256]{2,1,0:T(8,128)(2,1)}) fusion(bf16[512,512]{1,0:T(8,128)(2,1)} %param.25, s32[]{:T(128)S(6)} %select_n.39, bf16[512,512]{1,0:T(8,128)(2,1)} %param.24), kind=kLoop, calls=%fused_computation.1 | loop fusion | bytes 1048580 | tf_op jit(solution)/shard_map/stack | solution.py:697
  10.7 3.5 %attend_chunk_0.1 = (bf16[3,256,256]{2,1,0:T(8,128)(2,1)S(1)}, bf16[3,256,256]{2,1,0:T(8,128)(2,1)S(1)}, bf16[3,256,256]{2,1,0:T(8,128)(2,1)S(1)}, bf16[3,512,25...) custom-call(s32[5]{0:T(128)S(1)} %stack.53.refs_0_, ...), custom_call_target="tpu_custom_call" | custom-call | flops 55000000 | tf_op jit(solution)/shard_map/attend_chunk_0/pallas_call | solution.py:610
  17.5 5.8 %collective-permute-done.refs_3_ = bf16[3,128,512]{2,1,0:T(8,128)(2,1)S(1)} collective-permute-done((bf16[3,128,512]{2,1,0:T(8,128)(2,1)}, bf16[3,128,512]{2,1,0:T(8,128)(2,1)S(1)}, u32[]{:S(2)}, u32[]{:S(2)}) %collective-permute-start) | collective-permute-done | bytes 393248 | tf_op jit(solution)/shard_map/ppermute | solution.py:638
  25.1 3.3 %attend_chunk_2.1 = (bf16[3,256,256]{2,1,0:T(8,128)(2,1)S(1)}, bf16[3,256,256]{2,1,0:T(8,128)(2,1)S(1)}, bf16[3,256,256]{2,1,0:T(8,128)(2,1)S(1)}, bf16[3,512,25...) custom-call(s32[5]{0:T(128)S(1)} %stack.53.refs_0_, ...), custom_call_target="tpu_custom_call" | custom-call | flops 55000000 | tf_op jit(solution)/shard_map/attend_chunk_2/pallas_call | solution.py:610
  28.4 3.3 %attend_chunk_1.1 = (bf16[3,256,256]{2,1,0:T(8,128)(2,1)S(1)}, bf16[3,256,256]{2,1,0:T(8,128)(2,1)S(1)}, bf16[3,256,256]{2,1,0:T(8,128)(2,1)S(1)}, bf16[3,512,25...) custom-call(s32[5]{0:T(128)S(1)} %stack.53.refs_0_, ...), custom_call_target="tpu_custom_call" | custom-call | flops 55000000 | tf_op jit(solution)/shard_map/attend_chunk_1/pallas_call | solution.py:610
  31.8 3.6 %collective-permute-done.2.refs_3_ = bf16[3,128,512]{2,1,0:T(8,128)(2,1)S(1)} collective-permute-done((bf16[3,128,512]{2,1,0:T(8,128)(2,1)S(1)}, bf16[3,128,512]{2,1,0:T(8,128)(2,1)S(1)}, u32[]{:S(2)}, u32[]{:S(2)}) %collective-permute-start.2) | collective-permute-done | bytes 393248 | tf_op jit(solution)/shard_map/ppermute | solution.py:638
  35.4 1.7 %collective-permute-done.7.refs_4_ = bf16[3,128,512]{2,1,0:T(8,128)(2,1)S(1)} collective-permute-done((bf16[3,128,512]{2,1,0:T(8,128)(2,1)S(1)}, bf16[3,128,512]{2,1,0:T(8,128)(2,1)S(1)}, u32[]{:S(2)}, u32[]{:S(2)}) %collective-permute-start.7) | collective-permute-done | bytes 393248 | tf_op jit(solution)/shard_map/ppermute | solution.py:638
  37.1 3.4 %attend_chunk_3.1 = (bf16[3,256,256]{2,1,0:T(8,128)(2,1)S(1)}, bf16[3,256,256]{2,1,0:T(8,128)(2,1)S(1)}, bf16[3,256,256]{2,1,0:T(8,128)(2,1)S(1)}, bf16[3,512,25...) custom-call(s32[5]{0:T(128)S(1)} %stack.53.refs_0_, ...), custom_call_target="tpu_custom_call" | custom-call | flops 55000000 | tf_op jit(solution)/shard_map/attend_chunk_3/pallas_call | solution.py:610
  42.0 3.4 %feed_forward_a.1 = (f32[384,512]{1,0:T(8,128)S(1)}, bf16[384,512]{1,0:T(8,128)(2,1)S(1)}, bf16[384,2560]{1,0:T(8,128)(2,1)S(1)}, f32[384,512]{1,0:T(8,128)S(1)}...) custom-call(s32[5]{0:T(128)S(1)} %stack.53.refs_0_, bf16[3,128,256]{2,1,0:T(8,128)(2,1)S(1)} %get-tuple-element.196.refs_1_, ...), custom_call_target="tpu_custom_call" | custom-call | flops 4400000000 | tf_op jit(solution)/shard_map/feed_forward_a/pallas_call | solution.py:610
  45.7 3.7 %feed_forward_b.1 = (bf16[3,128,512]{2,1,0:T(8,128)(2,1)}, bf16[384,1024]{1,0:T(8,128)(2,1)S(1)}, bf16[384,1024]{1,0:T(8,128)(2,1)S(1)}, f32[384,512]{1,0:T(8,12...) custom-call(s32[5]{0:T(128)S(1)} %stack.53.refs_0_, f32[384,512]{1,0:T(8,128)S(1)} %get-tuple-element.206.refs_1_, ...), custom_call_target="tpu_custom_call" | custom-call | flops 4400000000 | tf_op jit(solution)/shard_map/feed_forward_b/pallas_call | solution.py:610
  49.8 1.8 %feed_forward_grad_sent.1 = (bf16[8,64,512]{2,1,0:T(8,128)(2,1)S(1)}, bf16[8,64,512]{2,1,0:T(8,128)(2,1)S(1)}) custom-call(s32[5]{0:T(128)S(1)} %stack.53.refs_0_, bf16[384,1024]{1,0:T(8,128)(2,1)S(1)} %get-tuple-element.215.refs_1_, bf16[384,1024]{1,0:T(8,128)(2,1)S(1)} %get-tuple-element.216.refs_2_, ...), custom_call_target="tpu_custom_call" | custom-call | flops 3300000000 | tf_op jit(solution)/shard_map/feed_forward_grad_sent/pallas_call | solution.py:610
  54.8 1.8 %feed_forward_grad_kept.1 = (bf16[8,64,512]{2,1,0:T(8,128)(2,1)S(1)}, bf16[8,64,512]{2,1,0:T(8,128)(2,1)S(1)}) custom-call(s32[5]{0:T(128)S(1)} %stack.53.refs_0_, bf16[384,1024]{1,0:T(8,128)(2,1)S(1)} %get-tuple-element.215.refs_1_, bf16[384,1024]{1,0:T(8,128)(2,1)S(1)} %get-tuple-element.216.refs_2_, ...), custom_call_target="tpu_custom_call" | custom-call | flops 55000000 | tf_op jit(solution)/shard_map/feed_forward_grad_kept/pallas_call | solution.py:610
  56.6 9.8 %attend_back_1.1 = (bf16[4,128,512]{2,1,0:T(8,128)(2,1)S(1)}, bf16[4,128,512]{2,1,0:T(8,128)(2,1)S(1)}, bf16[4,128,512]{2,1,0:T(8,128)(2,1)S(1)}, bf16[4,128,512...) custom-call(s32[5]{0:T(128)S(1)} %stack.53.refs_0_, ...), custom_call_target="tpu_custom_call" | custom-call | flops 55000000 | tf_op jit(solution)/shard_map/attend_back_1/pallas_call | solution.py:610
  69.2 5.9 %attend_back_2.1 = (bf16[4,128,512]{2,1,0:T(8,128)(2,1)S(1)}, bf16[12,128,512]{2,1,0:T(8,128)(2,1)S(1)}, bf16[256,512]{1,0:T(8,128)(2,1)S(1)}, bf16[256,512]{1,0...) custom-call(s32[5]{0:T(128)S(1)} %stack.53.refs_0_, s32[3,4]{1,0:T(4,128)S(1)} %copy-done.3, ...), custom_call_target="tpu_custom_call" | custom-call | flops 55000000 | tf_op jit(solution)/shard_map/attend_back_2/pallas_call | solution.py:610
  78.5 4.3 %collective-permute-done.16.refs_3_ = bf16[256,512]{1,0:T(8,128)(2,1)S(1)} collective-permute-done((bf16[256,512]{1,0:T(8,128)(2,1)S(1)}, bf16[256,512]{1,0:T(8,128)(2,1)S(1)}, u32[]{:S(2)}, u32[]{:S(2)}) %collective-permute-start.16) | collective-permute-done | bytes 262176 | tf_op jit(solution)/shard_map/ppermute | solution.py:638
  85.0 2.2 %collective-permute-start.18 = (bf16[128,512]{1,0:T(8,128)(2,1)S(1)}, bf16[128,512]{1,0:T(8,128)(2,1)S(1)}, u32[]{:S(2)}, u32[]{:S(2)}) collective-permute-start(bf16[128,512]{1,0:T(8,128)(2,1)S(1)} %get-tuple-element.268), channel_id=1, source_target_pairs={{0,4},{1,5},{2,6},{3,7},{4,0},{5,1},{6,2},{7,3},{8,12},{9,13},{10,... | collective-permute-start | bytes 393224 | tf_op jit(solution)/shard_map/ppermute | solution.py:638
  88.7 3.6 %collective-permute-done.18.refs_1_ = bf16[128,512]{1,0:T(8,128)(2,1)S(1)} collective-permute-done((bf16[128,512]{1,0:T(8,128)(2,1)S(1)}, bf16[128,512]{1,0:T(8,128)(2,1)S(1)}, u32[]{:S(2)}, u32[]{:S(2)}) %collective-permute-start.18) | collective-permute-done | bytes 131104 | tf_op jit(solution)/shard_map/ppermute | solution.py:638
  92.5 1.7 %collective-permute-start.23 = (bf16[2,80,512]{2,1,0:T(8,128)(2,1)S(1)}, bf16[2,80,512]{2,1,0:T(8,128)(2,1)S(1)}, u32[]{:S(2)}, u32[]{:S(2)}) collective-permute-start(bf16[2,80,512]{2,1,0:T(8,128)(2,1)S(1)} %get-tuple-element.277.refs_4_), channel_id=1, source_target_pairs={{0,2},{1,3},{2,0},{3,1},{4,6},{5,7},{6,4},{7,5},{8,10},{9,11},{10,... | collective-permute-start | bytes 491528 | tf_op jit(solution)/shard_map/ppermute | solution.py:638
  94.2 2.0 %collective-permute-start.22 = (bf16[128,512]{1,0:T(8,128)(2,1)S(1)}, bf16[128,512]{1,0:T(8,128)(2,1)S(1)}, u32[]{:S(2)}, u32[]{:S(2)}) collective-permute-start(bf16[128,512]{1,0:T(8,128)(2,1)S(1)} %get-tuple-element.275.refs_0_), channel_id=1, source_target_pairs={{0,4},{1,5},{2,6},{3,7},{4,0},{5,1},{6,2},{7,3},{8,12},{9,13},{10,... | collective-permute-start | bytes 393224 | tf_op jit(solution)/shard_map/ppermute | solution.py:638
  96.3 7.3 %collective-permute-done.22.refs_1_ = bf16[128,512]{1,0:T(8,128)(2,1)S(1)} collective-permute-done((bf16[128,512]{1,0:T(8,128)(2,1)S(1)}, bf16[128,512]{1,0:T(8,128)(2,1)S(1)}, u32[]{:S(2)}, u32[]{:S(2)}) %collective-permute-start.22) | collective-permute-done | bytes 131104 | tf_op jit(solution)/shard_map/ppermute | solution.py:638
  104.1 1.7 %collective-permute-start.25 = (bf16[80,512]{1,0:T(8,128)(2,1)S(1)}, bf16[80,512]{1,0:T(8,128)(2,1)S(1)}, u32[]{:S(2)}, u32[]{:S(2)}) collective-permute-start(bf16[80,512]{1,0:T(8,128)(2,1)S(1)} %get-tuple-element.280.refs_8_), channel_id=1, source_target_pairs={{0,4},{1,5},{2,6},{3,7},{4,0},{5,1},{6,2},{7,3},{8,12},{9,13},{10,... | collective-permute-start | bytes 245768 | tf_op jit(solution)/shard_map/ppermute | solution.py:638
  105.7 5.6 %collective-permute-done.25.refs_3_ = bf16[80,512]{1,0:T(8,128)(2,1)S(1)} collective-permute-done((bf16[80,512]{1,0:T(8,128)(2,1)S(1)}, bf16[80,512]{1,0:T(8,128)(2,1)S(1)}, u32[]{:S(2)}, u32[]{:S(2)}) %collective-permute-start.25) | collective-permute-done | bytes 81952 | tf_op jit(solution)/shard_map/ppermute | solution.py:638
  112.3 2.2 %collective-permute-start.29 = (bf16[3,128,512]{2,1,0:T(8,128)(2,1)S(1)}, bf16[3,128,512]{2,1,0:T(8,128)(2,1)S(1)}, u32[]{:S(2)}, u32[]{:S(2)}) collective-permute-start(bf16[3,128,512]{2,1,0:T(8,128)(2,1)S(1)} %get-tuple-element.286.refs_11_), channel_id=1, source_target_pairs={{0,2},{1,3},{2,0},{3,1},{4,6},{5,7},{6,4},{7,5},{8,10},{9,11},{10,... | collective-permute-start | bytes 1179656 | tf_op jit(solution)/shard_map/ppermute | solution.py:638
  118.1 5.9 %collective-permute-done.29.refs_10_ = bf16[3,128,512]{2,1,0:T(8,128)(2,1)S(1)} collective-permute-done((bf16[3,128,512]{2,1,0:T(8,128)(2,1)S(1)}, bf16[3,128,512]{2,1,0:T(8,128)(2,1)S(1)}, u32[]{:S(2)}, u32[]{:S(2)}) %collective-permute-start.29) | collective-permute-done | bytes 393248 | tf_op jit(solution)/shard_map/ppermute | solution.py:638
  126.8 2.6 %collective-permute-start.30 = (bf16[3,128,512]{2,1,0:T(8,128)(2,1)S(1)}, bf16[3,128,512]{2,1,0:T(8,128)(2,1)S(1)}, u32[]{:S(2)}, u32[]{:S(2)}) collective-permute-start(bf16[3,128,512]{2,1,0:T(8,128)(2,1)S(1)} %get-tuple-element.291.refs_6_), channel_id=1, source_target_pairs={{0,4},{1,5},{2,6},{3,7},{4,0},{5,1},{6,2},{7,3},{8,12},{9,13},{10,... | collective-permute-start | bytes 1179656 | tf_op jit(solution)/shard_map/ppermute | solution.py:638
  129.9 5.1 %collective-permute-done.32.refs_1_ = bf16[8,64,512]{2,1,0:T(8,128)(2,1)S(1)} collective-permute-done((bf16[8,64,512]{2,1,0:T(8,128)(2,1)S(1)}, bf16[8,64,512]{2,1,0:T(8,128)(2,1)S(1)}, u32[]{:S(2)}, u32[]{:S(2)}) %collective-permute-start.32) | collective-permute-done | bytes 524320 | tf_op jit(solution)/shard_map/ppermute | solution.py:638
  136.4 1.8 %collective-permute-done.31.refs_1_ = bf16[2,80,512]{2,1,0:T(8,128)(2,1)S(1)} collective-permute-done((bf16[2,80,512]{2,1,0:T(8,128)(2,1)S(1)}, bf16[2,80,512]{2,1,0:T(8,128)(2,1)S(1)}, u32[]{:S(2)}, u32[]{:S(2)}) %collective-permute-start.31) | collective-permute-done | bytes 163872 | tf_op jit(solution)/shard_map/ppermute | solution.py:638
  140.0 4.4 %collective-permute-done.30.refs_7_ = bf16[3,128,512]{2,1,0:T(8,128)(2,1)S(1)} collective-permute-done((bf16[3,128,512]{2,1,0:T(8,128)(2,1)S(1)}, bf16[3,128,512]{2,1,0:T(8,128)(2,1)S(1)}, u32[]{:S(2)}, u32[]{:S(2)}) %collective-permute-start.30) | collective-permute-done | bytes 393248 | tf_op jit(solution)/shard_map/ppermute | solution.py:638
  149.2 2.7 %unpack_feed_forward.2 = (f32[2048,512]{1,0:T(8,128)}, f32[512,2048]{1,0:T(8,128)}, f32[8,128]{1,0:T(8,128)S(1)}) custom-call(s32[5]{0:T(128)S(1)} %stack.53.refs_0_, bf16[8,64,512]{2,1,0:T(8,128)(2,1)S(1)} %get-tuple-element.289.refs_1_, bf16[8,64,512]{2,1,0:T(8,128)(2,1)S(1)} %collective-permute-done.41.refs_2_, ...), custom_call_target="tpu_custom_call" | custom-call | flops 110000000 | tf_op jit(solution)/shard_map/unpack_feed_forward/pallas_call | solution.py:610
  151.9 2.7 %unpack_feed_forward.3 = (f32[2048,512]{1,0:T(8,128)}, f32[512,2048]{1,0:T(8,128)}, f32[8,128]{1,0:T(8,128)S(1)}) custom-call(s32[5]{0:T(128)S(1)} %stack.53.refs_0_, bf16[8,64,512]{2,1,0:T(8,128)(2,1)S(1)} %collective-permute-done.32.refs_1_, bf16[8,64,512]{2,1,0:T(8,128)(2,1)S(1)} %collective-permute-done.39.refs_2_, ...), custom_call_target="tpu_custom_call", output_to_operand_aliasing={{0}: (5, {}), {1}: (6, {})} | custom-call | flops 110000000 | tf_op jit(solution)/shard_map/unpack_feed_forward/pallas_call | solution.py:610
  158.7 2.7 %unpack_attend.1 = (f32[512,512]{1,0:T(8,128)}, f32[512,512]{1,0:T(8,128)}, f32[512,512]{1,0:T(8,128)}, f32[512,512]{1,0:T(8,128)}, f32[1,512]{1,0:T(1,128)}, /*...) custom-call(s32[5]{0:T(128)S(1)} %stack.53.refs_0_, ...), custom_call_target="tpu_custom_call" | custom-call | flops 110000000 | tf_op jit(solution)/shard_map/unpack_attend/pallas_call | solution.py:610
  (120 shorter events, 44.9 us)
Async XLA Ops:
  0.7 10.0 %collective-permute-start.1 = (bf16[3,128,512]{2,1,0:T(8,128)(2,1)}, bf16[3,128,512]{2,1,0:T(8,128)(2,1)S(1)}, u32[]{:S(2)}, u32[]{:S(2)}) collective-permute-start(bf16[3,128,512]{2,1,0:T(8,128)(2,1)} %refs_1_.8), channel_id=1, source_target_pairs={{0,1},{1,0},{2,3},{3,2},{4,5},{5,4},{6,7},{7,6},{8,9},{9,8},{10,11... | collective-permute-start | bytes 1179656 | tf_op jit(solution)/shard_map/ppermute | solution.py:638
  1.2 22.1 %collective-permute-start = (bf16[3,128,512]{2,1,0:T(8,128)(2,1)}, bf16[3,128,512]{2,1,0:T(8,128)(2,1)S(1)}, u32[]{:S(2)}, u32[]{:S(2)}) collective-permute-start(bf16[3,128,512]{2,1,0:T(8,128)(2,1)} %refs_1_.8), channel_id=1, source_target_pairs={{0,4},{1,5},{2,6},{3,7},{4,0},{5,1},{6,2},{7,3},{8,12},{9,13},{10,... | collective-permute-start | bytes 1179656 | tf_op jit(solution)/shard_map/ppermute | solution.py:638
  4.9 19.0 %collective-permute-start.3 = (bf16[3,128,512]{2,1,0:T(8,128)(2,1)}, bf16[3,128,512]{2,1,0:T(8,128)(2,1)S(1)}, u32[]{:S(2)}, u32[]{:S(2)}) collective-permute-start(bf16[3,128,512]{2,1,0:T(8,128)(2,1)} %refs_1_.8), channel_id=1, source_target_pairs={{0,2},{1,3},{2,0},{3,1},{4,6},{5,7},{6,4},{7,5},{8,10},{9,11},{10,... | collective-permute-start | bytes 1179656 | tf_op jit(solution)/shard_map/ppermute | solution.py:638
  23.9 11.5 %collective-permute-start.2 = (bf16[3,128,512]{2,1,0:T(8,128)(2,1)S(1)}, bf16[3,128,512]{2,1,0:T(8,128)(2,1)S(1)}, u32[]{:S(2)}, u32[]{:S(2)}) collective-permute-start(bf16[3,128,512]{2,1,0:T(8,128)(2,1)S(1)} %collective-permute-done.refs_3_), channel_id=1, source_target_pairs={{0,2},{1,3},{2,0},{3,1},{4,6},{5,7},{6,4},{7,5},{8,10},{9,11},{10,... | collective-permute-start | bytes 1179656 | tf_op jit(solution)/shard_map/ppermute | solution.py:638
  51.6 14.8 %collective-permute-start.11 = (bf16[8,64,512]{2,1,0:T(8,128)(2,1)S(1)}, bf16[8,64,512]{2,1,0:T(8,128)(2,1)S(1)}, u32[]{:S(2)}, u32[]{:S(2)}) collective-permute-start(bf16[8,64,512]{2,1,0:T(8,128)(2,1)S(1)} %get-tuple-element.240.refs_7_), channel_id=1, source_target_pairs={{0,8},{8,0},{16,24},{24,16},{1,9},{9,1},{17,25},{25,17},{2,10},{10... | collective-permute-start | bytes 1572872 | tf_op jit(solution)/shard_map/ppermute | solution.py:638
  53.2 13.7 %collective-permute-start.12 = (bf16[8,64,512]{2,1,0:T(8,128)(2,1)S(1)}, bf16[8,64,512]{2,1,0:T(8,128)(2,1)S(1)}, u32[]{:S(2)}, u32[]{:S(2)}) collective-permute-start(bf16[8,64,512]{2,1,0:T(8,128)(2,1)S(1)} %get-tuple-element.253), channel_id=1, source_target_pairs={{0,16},{8,24},{16,0},{24,8},{1,17},{9,25},{17,1},{25,9},{2,18},{10... | collective-permute-start | bytes 1572872 | tf_op jit(solution)/shard_map/ppermute | solution.py:638
  67.1 8.0 %collective-permute-start.13 = (bf16[4,64,512]{2,1,0:T(8,128)(2,1)S(1)}, bf16[4,64,512]{2,1,0:T(8,128)(2,1)S(1)}, u32[]{:S(2)}, u32[]{:S(2)}) collective-permute-start(bf16[4,64,512]{2,1,0:T(8,128)(2,1)S(1)} %get-tuple-element.257), channel_id=1, source_target_pairs={{0,16},{8,24},{16,0},{24,8},{1,17},{9,25},{17,1},{25,9},{2,18},{10... | collective-permute-start | bytes 786440 | tf_op jit(solution)/shard_map/ppermute | solution.py:638
  68.6 6.9 %collective-permute-start.14 = (bf16[4,64,512]{2,1,0:T(8,128)(2,1)S(1)}, bf16[4,64,512]{2,1,0:T(8,128)(2,1)S(1)}, u32[]{:S(2)}, u32[]{:S(2)}) collective-permute-start(bf16[4,64,512]{2,1,0:T(8,128)(2,1)S(1)} %get-tuple-element.254.refs_35_), channel_id=1, source_target_pairs={{0,8},{8,0},{16,24},{24,16},{1,9},{9,1},{17,25},{25,17},{2,10},{10... | collective-permute-start | bytes 786440 | tf_op jit(solution)/shard_map/ppermute | solution.py:638
  75.8 8.0 %collective-permute-start.17 = (bf16[272,512]{1,0:T(8,128)(2,1)S(1)}, bf16[272,512]{1,0:T(8,128)(2,1)S(1)}, u32[]{:S(2)}, u32[]{:S(2)}) collective-permute-start(bf16[272,512]{1,0:T(8,128)(2,1)S(1)} %get-tuple-element.265.refs_6_), channel_id=1, source_target_pairs={{0,16},{8,24},{16,0},{24,8},{1,17},{9,25},{17,1},{25,9},{2,18},{10... | collective-permute-start | bytes 835592 | tf_op jit(solution)/shard_map/ppermute | solution.py:638
  76.4 6.4 %collective-permute-start.16 = (bf16[256,512]{1,0:T(8,128)(2,1)S(1)}, bf16[256,512]{1,0:T(8,128)(2,1)S(1)}, u32[]{:S(2)}, u32[]{:S(2)}) collective-permute-start(bf16[256,512]{1,0:T(8,128)(2,1)S(1)} %get-tuple-element.263), channel_id=1, source_target_pairs={{0,8},{8,0},{16,24},{24,16},{1,9},{9,1},{17,25},{25,17},{2,10},{10... | collective-permute-start | bytes 786440 | tf_op jit(solution)/shard_map/ppermute | solution.py:638
  77.4 6.4 %collective-permute-start.15 = (bf16[2,128,512]{2,1,0:T(8,128)(2,1)S(1)}, bf16[2,128,512]{2,1,0:T(8,128)(2,1)S(1)}, u32[]{:S(2)}, u32[]{:S(2)}) collective-permute-start(bf16[2,128,512]{2,1,0:T(8,128)(2,1)S(1)} %get-tuple-element.266.refs_6_), channel_id=1, source_target_pairs={{0,2},{1,3},{2,0},{3,1},{4,6},{5,7},{6,4},{7,5},{8,10},{9,11},{10,... | collective-permute-start | bytes 786440 | tf_op jit(solution)/shard_map/ppermute | solution.py:638
  83.9 8.4 %collective-permute-start.20 = (bf16[144,512]{1,0:T(8,128)(2,1)S(1)}, bf16[144,512]{1,0:T(8,128)(2,1)S(1)}, u32[]{:S(2)}, u32[]{:S(2)}) collective-permute-start(bf16[144,512]{1,0:T(8,128)(2,1)S(1)} %get-tuple-element.270.refs_8_), channel_id=1, source_target_pairs={{0,8},{8,0},{16,24},{24,16},{1,9},{9,1},{17,25},{25,17},{2,10},{10... | collective-permute-start | bytes 442376 | tf_op jit(solution)/shard_map/ppermute | solution.py:638
  85.0 7.3 %collective-permute-start.18 = (bf16[128,512]{1,0:T(8,128)(2,1)S(1)}, bf16[128,512]{1,0:T(8,128)(2,1)S(1)}, u32[]{:S(2)}, u32[]{:S(2)}) collective-permute-start(bf16[128,512]{1,0:T(8,128)(2,1)S(1)} %get-tuple-element.268), channel_id=1, source_target_pairs={{0,4},{1,5},{2,6},{3,7},{4,0},{5,1},{6,2},{7,3},{8,12},{9,13},{10,... | collective-permute-start | bytes 393224 | tf_op jit(solution)/shard_map/ppermute | solution.py:638
  92.5 11.0 %collective-permute-start.23 = (bf16[2,80,512]{2,1,0:T(8,128)(2,1)S(1)}, bf16[2,80,512]{2,1,0:T(8,128)(2,1)S(1)}, u32[]{:S(2)}, u32[]{:S(2)}) collective-permute-start(bf16[2,80,512]{2,1,0:T(8,128)(2,1)S(1)} %get-tuple-element.277.refs_4_), channel_id=1, source_target_pairs={{0,2},{1,3},{2,0},{3,1},{4,6},{5,7},{6,4},{7,5},{8,10},{9,11},{10,... | collective-permute-start | bytes 491528 | tf_op jit(solution)/shard_map/ppermute | solution.py:638
  94.2 9.3 %collective-permute-start.22 = (bf16[128,512]{1,0:T(8,128)(2,1)S(1)}, bf16[128,512]{1,0:T(8,128)(2,1)S(1)}, u32[]{:S(2)}, u32[]{:S(2)}) collective-permute-start(bf16[128,512]{1,0:T(8,128)(2,1)S(1)} %get-tuple-element.275.refs_0_), channel_id=1, source_target_pairs={{0,4},{1,5},{2,6},{3,7},{4,0},{5,1},{6,2},{7,3},{8,12},{9,13},{10,... | collective-permute-start | bytes 393224 | tf_op jit(solution)/shard_map/ppermute | solution.py:638
  103.6 8.5 %collective-permute-start.24 = (bf16[2,128,512]{2,1,0:T(8,128)(2,1)S(1)}, bf16[2,128,512]{2,1,0:T(8,128)(2,1)S(1)}, u32[]{:S(2)}, u32[]{:S(2)}) collective-permute-start(bf16[2,128,512]{2,1,0:T(8,128)(2,1)S(1)} %get-tuple-element.278.refs_0_), channel_id=1, source_target_pairs={{0,2},{1,3},{2,0},{3,1},{4,6},{5,7},{6,4},{7,5},{8,10},{9,11},{10,... | collective-permute-start | bytes 786440 | tf_op jit(solution)/shard_map/ppermute | solution.py:638
  104.1 7.3 %collective-permute-start.25 = (bf16[80,512]{1,0:T(8,128)(2,1)S(1)}, bf16[80,512]{1,0:T(8,128)(2,1)S(1)}, u32[]{:S(2)}, u32[]{:S(2)}) collective-permute-start(bf16[80,512]{1,0:T(8,128)(2,1)S(1)} %get-tuple-element.280.refs_8_), channel_id=1, source_target_pairs={{0,4},{1,5},{2,6},{3,7},{4,0},{5,1},{6,2},{7,3},{8,12},{9,13},{10,... | collective-permute-start | bytes 245768 | tf_op jit(solution)/shard_map/ppermute | solution.py:638
  112.3 11.7 %collective-permute-start.29 = (bf16[3,128,512]{2,1,0:T(8,128)(2,1)S(1)}, bf16[3,128,512]{2,1,0:T(8,128)(2,1)S(1)}, u32[]{:S(2)}, u32[]{:S(2)}) collective-permute-start(bf16[3,128,512]{2,1,0:T(8,128)(2,1)S(1)} %get-tuple-element.286.refs_11_), channel_id=1, source_target_pairs={{0,2},{1,3},{2,0},{3,1},{4,6},{5,7},{6,4},{7,5},{8,10},{9,11},{10,... | collective-permute-start | bytes 1179656 | tf_op jit(solution)/shard_map/ppermute | solution.py:638
  114.5 9.5 %collective-permute-start.26 = (bf16[4,64,512]{2,1,0:T(8,128)(2,1)S(1)}, bf16[4,64,512]{2,1,0:T(8,128)(2,1)S(1)}, u32[]{:S(2)}, u32[]{:S(2)}) collective-permute-start(bf16[4,64,512]{2,1,0:T(8,128)(2,1)S(1)} %get-tuple-element.281.refs_0_), channel_id=1, source_target_pairs={{0,16},{8,24},{16,0},{24,8},{1,17},{9,25},{17,1},{25,9},{2,18},{10... | collective-permute-start | bytes 786440 | tf_op jit(solution)/shard_map/ppermute | solution.py:638
  115.9 8.1 %collective-permute-start.27 = (bf16[4,64,512]{2,1,0:T(8,128)(2,1)S(1)}, bf16[4,64,512]{2,1,0:T(8,128)(2,1)S(1)}, u32[]{:S(2)}, u32[]{:S(2)}) collective-permute-start(bf16[4,64,512]{2,1,0:T(8,128)(2,1)S(1)} %get-tuple-element.282.refs_2_), channel_id=1, source_target_pairs={{0,8},{8,0},{16,24},{24,16},{1,9},{9,1},{17,25},{25,17},{2,10},{10... | collective-permute-start | bytes 786440 | tf_op jit(solution)/shard_map/ppermute | solution.py:638
  117.0 7.0 %collective-permute-start.28 = (bf16[80,512]{1,0:T(8,128)(2,1)S(1)}, bf16[80,512]{1,0:T(8,128)(2,1)S(1)}, u32[]{:S(2)}, u32[]{:S(2)}) collective-permute-start(bf16[80,512]{1,0:T(8,128)(2,1)S(1)} %get-tuple-element.283.refs_4_), channel_id=1, source_target_pairs={{0,4},{1,5},{2,6},{3,7},{4,0},{5,1},{6,2},{7,3},{8,12},{9,13},{10,... | collective-permute-start | bytes 245768 | tf_op jit(solution)/shard_map/ppermute | solution.py:638
  124.2 10.8 %collective-permute-start.32 = (bf16[8,64,512]{2,1,0:T(8,128)(2,1)S(1)}, bf16[8,64,512]{2,1,0:T(8,128)(2,1)S(1)}, u32[]{:S(2)}, u32[]{:S(2)}) collective-permute-start(bf16[8,64,512]{2,1,0:T(8,128)(2,1)S(1)} %get-tuple-element.289.refs_1_), channel_id=1, source_target_pairs={{0,8},{8,0},{16,24},{24,16},{1,9},{9,1},{17,25},{25,17},{2,10},{10... | collective-permute-start | bytes 1572872 | tf_op jit(solution)/shard_map/ppermute | solution.py:638
  125.3 11.2 %collective-permute-start.33 = (bf16[8,64,512]{2,1,0:T(8,128)(2,1)S(1)}, bf16[8,64,512]{2,1,0:T(8,128)(2,1)S(1)}, u32[]{:S(2)}, u32[]{:S(2)}) collective-permute-start(bf16[8,64,512]{2,1,0:T(8,128)(2,1)S(1)} %get-tuple-element.290.refs_3_), channel_id=1, source_target_pairs={{0,16},{8,24},{16,0},{24,8},{1,17},{9,25},{17,1},{25,9},{2,18},{10... | collective-permute-start | bytes 1572872 | tf_op jit(solution)/shard_map/ppermute | solution.py:638
  126.8 17.6 %collective-permute-start.30 = (bf16[3,128,512]{2,1,0:T(8,128)(2,1)S(1)}, bf16[3,128,512]{2,1,0:T(8,128)(2,1)S(1)}, u32[]{:S(2)}, u32[]{:S(2)}) collective-permute-start(bf16[3,128,512]{2,1,0:T(8,128)(2,1)S(1)} %get-tuple-element.291.refs_6_), channel_id=1, source_target_pairs={{0,4},{1,5},{2,6},{3,7},{4,0},{5,1},{6,2},{7,3},{8,12},{9,13},{10,... | collective-permute-start | bytes 1179656 | tf_op jit(solution)/shard_map/ppermute | solution.py:638
  129.4 8.8 %collective-permute-start.31 = (bf16[2,80,512]{2,1,0:T(8,128)(2,1)S(1)}, bf16[2,80,512]{2,1,0:T(8,128)(2,1)S(1)}, u32[]{:S(2)}, u32[]{:S(2)}) collective-permute-start(bf16[2,80,512]{2,1,0:T(8,128)(2,1)S(1)} %get-tuple-element.288.refs_0_), channel_id=1, source_target_pairs={{0,2},{1,3},{2,0},{3,1},{4,6},{5,7},{6,4},{7,5},{8,10},{9,11},{10,... | collective-permute-start | bytes 491528 | tf_op jit(solution)/shard_map/ppermute | solution.py:638
  129.9 16.6 %collective-permute-start.41 = (bf16[8,64,512]{2,1,0:T(8,128)(2,1)S(1)}, bf16[8,64,512]{2,1,0:T(8,128)(2,1)S(1)}, u32[]{:S(2)}, u32[]{:S(2)}) collective-permute-start(bf16[8,64,512]{2,1,0:T(8,128)(2,1)S(1)} %get-tuple-element.289.refs_1_), channel_id=1, source_target_pairs={{0,1},{1,0},{2,3},{3,2},{4,5},{5,4},{6,7},{7,6},{8,9},{9,8},{10,11... | collective-permute-start | bytes 1572872 | tf_op jit(solution)/shard_map/ppermute | solution.py:638
  135.1 13.1 %collective-permute-start.42 = (bf16[8,64,512]{2,1,0:T(8,128)(2,1)S(1)}, bf16[8,64,512]{2,1,0:T(8,128)(2,1)S(1)}, u32[]{:S(2)}, u32[]{:S(2)}) collective-permute-start(bf16[8,64,512]{2,1,0:T(8,128)(2,1)S(1)} %get-tuple-element.290.refs_3_), channel_id=1, source_target_pairs={{0,1},{1,0},{2,3},{3,2},{4,5},{5,4},{6,7},{7,6},{8,9},{9,8},{10,11... | collective-permute-start | bytes 1572872 | tf_op jit(solution)/shard_map/ppermute | solution.py:638
  144.4 7.5 %collective-permute-start.39 = (bf16[8,64,512]{2,1,0:T(8,128)(2,1)S(1)}, bf16[8,64,512]{2,1,0:T(8,128)(2,1)S(1)}, u32[]{:S(2)}, u32[]{:S(2)}) collective-permute-start(bf16[8,64,512]{2,1,0:T(8,128)(2,1)S(1)} %collective-permute-done.32.refs_1_), channel_id=1, source_target_pairs={{0,1},{1,0},{2,3},{3,2},{4,5},{5,4},{6,7},{7,6},{8,9},{9,8},{10,11... | collective-permute-start | bytes 1572872 | tf_op jit(solution)/shard_map/ppermute | solution.py:638
  144.4 7.5 %collective-permute-start.40 = (bf16[8,64,512]{2,1,0:T(8,128)(2,1)S(1)}, bf16[8,64,512]{2,1,0:T(8,128)(2,1)S(1)}, u32[]{:S(2)}, u32[]{:S(2)}) collective-permute-start(bf16[8,64,512]{2,1,0:T(8,128)(2,1)S(1)} %collective-permute-done.33.refs_3_), channel_id=1, source_target_pairs={{0,1},{1,0},{2,3},{3,2},{4,5},{5,4},{6,7},{7,6},{8,9},{9,8},{10,11... | collective-permute-start | bytes 1572872 | tf_op jit(solution)/shard_map/ppermute | solution.py:638
  144.9 11.1 %collective-permute-start.38 = (bf16[3,128,512]{2,1,0:T(8,128)(2,1)S(1)}, bf16[3,128,512]{2,1,0:T(8,128)(2,1)S(1)}, u32[]{:S(2)}, u32[]{:S(2)}) collective-permute-start(bf16[3,128,512]{2,1,0:T(8,128)(2,1)S(1)} %get-tuple-element.300.refs_4_), channel_id=1, source_target_pairs={{0,2},{1,3},{2,0},{3,1},{4,6},{5,7},{6,4},{7,5},{8,10},{9,11},{10,... | collective-permute-start | bytes 1179656 | tf_op jit(solution)/shard_map/ppermute | solution.py:638
  146.6 9.4 %collective-permute-start.37 = (bf16[272,512]{1,0:T(8,128)(2,1)S(1)}, bf16[272,512]{1,0:T(8,128)(2,1)S(1)}, u32[]{:S(2)}, u32[]{:S(2)}) collective-permute-start(bf16[272,512]{1,0:T(8,128)(2,1)S(1)} %get-tuple-element.318.refs_5_), channel_id=1, source_target_pairs={{0,16},{8,24},{16,0},{24,8},{1,17},{9,25},{17,1},{25,9},{2,18},{10... | collective-permute-start | bytes 835592 | tf_op jit(solution)/shard_map/ppermute | solution.py:638
  148.2 7.8 %collective-permute-start.36 = (bf16[256,512]{1,0:T(8,128)(2,1)S(1)}, bf16[256,512]{1,0:T(8,128)(2,1)S(1)}, u32[]{:S(2)}, u32[]{:S(2)}) collective-permute-start(bf16[256,512]{1,0:T(8,128)(2,1)S(1)} %get-tuple-element.316.refs_1_), channel_id=1, source_target_pairs={{0,8},{8,0},{16,24},{24,16},{1,9},{9,1},{17,25},{25,17},{2,10},{10... | collective-permute-start | bytes 786440 | tf_op jit(solution)/shard_map/ppermute | solution.py:638
  (29 other events, 141.7 us)
